TPU v7x, 128 devices: a whole 4x4x4 slice. The times are simulated.
128 devices in a mesh: row: 8 (over z_hi, x), col: 16 (over z_lo, y, core).
Axes of the slice: x: 4, y: 4, z: 4 (z_hi: 2, z_lo: 2; z = z_hi * 2 + z_lo), core: 2. Of those that a mesh axis runs over, the one named last changes fastest.
Arguments:
- environment: float32 [2, 2048, 4096], P(None, 'row', 'col'), may hold values from -6 to 6
- initial_site: float32 [2, 2, 4096, 4096], P(None, None, 'col', 'row'), may hold values from -0.09375 to 0.09375
- compressed_site: float32 [2, 2, 2048, 2048], P(None, None, 'col', 'row'), may hold values from -0.09375 to 0.09375
Outputs:
- new_environment: float32 [2, 2048, 4096], P(None, 'row', 'col')
All inputs are finite; a program needn't handle non-finite values.
Results may differ from a plain program's by a relative error of at most 0.0001.
Values sent between devices are 32-bit elements; how exact they have to be, the bound alone decides.
No kernel may reach another device: no remote copies, remote signals or barrier semaphores. Data moves between devices by JAX's collectives and lax.ppermute only.
A program may use at most 128 MiB of HBM per device.

v0:
```python
import jax
import jax.numpy as jnp
from jax import lax
from jax.sharding import PartitionSpec as P


def contract(form, left, right):
    return jnp.einsum(
        form, left, right, precision=lax.Precision.HIGHEST, preferred_element_type=jnp.float32
    )


def local(environment, initial_site, compressed_site):
    column = lax.all_gather(environment, "row", axis=1, tiled=True)
    piece = lax.all_gather(compressed_site, "col", axis=2, tiled=True)
    part_re = piece[:, 0]
    part_im = piece[:, 1]
    add_mixed_re = contract("nkb,ka->nba", part_re, column[0]) + contract(
        "nkb,ka->nba", part_im, column[1]
    )
    add_mixed_im = contract("nkb,ka->nba", part_re, column[1]) - contract(
        "nkb,ka->nba", part_im, column[0]
    )
    mixed = jnp.stack([add_mixed_re, add_mixed_im], axis=1)
    mixed_re = mixed[:, 0]
    mixed_im = mixed[:, 1]
    piece = lax.all_gather(initial_site, "row", axis=3, tiled=True)
    orig_re = piece[:, 0]
    orig_im = piece[:, 1]
    term_re = contract("nba,nac->bc", mixed_re, orig_re) - contract(
        "nba,nac->bc", mixed_im, orig_im
    )
    term_im = contract("nba,nac->bc", mixed_re, orig_im) + contract(
        "nba,nac->bc", mixed_im, orig_re
    )
    partial_env = jnp.stack([term_re, term_im])
    result = lax.psum_scatter(partial_env, "col", scatter_dimension=2, tiled=True)
    return result


def solution(mesh):
    return jax.shard_map(
        local,
        mesh=mesh,
        in_specs=(P(None, "row", "col"), P(None, None, "col", "row"), P(None, None, "col", "row")),
        out_specs=P(None, "row", "col"),
        check_vma=False,
    )
```

profile of v0, /device:TPU:62, one launch (start us, length us, event | category | flops | bytes accessed | tf_op | source)
XLA Modules:
  0.0 445.6 jit_solution(5268278988442741318)
XLA Ops:
  6.5 0.0 all-gather.6.cloned.1.call-start
  6.5 0.7 all-gather.6.cloned.1.call-update
  7.3 0.0 all-gather.4.cloned.1.call-start
  7.3 2.0 copy.4
  9.3 0.0 all-gather.4.cloned.1.call-update
  9.4 0.0 all-gather.8.cloned.1.call-start
  9.4 3.1 copy.5
  12.5 0.0 all-gather.8.cloned.1.call-update
  12.5 0.0 reduce-scatter.2.cloned.1.call-start
  12.6 67.6 %all-gather.6.cloned.1.call-done = f32[2,2048,256]{2,1,0:T(8,128)} async-done(((f32[2,256,256]{2,1,0:T(8,128)}), f32[2,2048,256]{2,1,0:T(8,128)}) %all-gather.6.cloned.1.call-update) | async-done | bytes 4194320 | tf_op jit(solution)/shard_map/all_gather | solution.py:14
  80.2 60.6 %all-gather.4.cloned.1.call-done = f32[2,2,2048,256]{2,3,0,1:T(8,128)} async-done(((f32[2,2,128,256]{2,3,0,1:T(8,128)}), f32[2,2,2048,256]{2,3,0,1:T(8,128)}) %all-gather.4.cloned.1.call-update) | async-done | bytes 8388624 | tf_op jit(solution)/shard_map/all_gather | solution.py:15
  140.8 0.0 copy-start.1
  140.8 6.2 %fusion.12 = f32[2,256,256]{2,1,0:T(8,128)S(1)} fusion(f32[2,2,2048,256]{2,3,0,1:T(8,128)} %all-gather.4.cloned.1.call-done, f32[2,2048,256]{2,1,0:T(8,128)} %all-gather.6.cloned.1.call-done), kind=kOutput, calls=%fused_computation.17 | convolution fusion | flops 3221225472 | bytes 6815744 | tf_op jit(solution)/shard_map/nkb,ka->nba/dot_general | solution.py:8
  147.0 0.0 copy-start.2
  147.0 6.2 %fusion.13 = f32[2,256,256]{2,1,0:T(8,128)S(1)} fusion(f32[2,2,2048,256]{2,3,0,1:T(8,128)} %all-gather.4.cloned.1.call-done, f32[2,2048,256]{2,1,0:T(8,128)} %all-gather.6.cloned.1.call-done), kind=kOutput, calls=%fused_computation.18 | convolution fusion | flops 3221225472 | bytes 6815744 | tf_op jit(solution)/shard_map/nkb,ka->nba/dot_general | solution.py:8
  153.2 0.0 copy-done.1
  153.2 0.0 copy-done.2
  153.3 3.4 fusion.17
  156.7 3.4 fusion.16
  160.2 168.4 %all-gather.8.cloned.1.call-done = f32[2,2,256,4096]{3,2,0,1:T(8,128)} async-done(((f32[2,2,256,512]{3,2,0,1:T(8,128)}), f32[2,2,256,4096]{3,2,0,1:T(8,128)}) %all-gather.8.cloned.1.call-update) | async-done | bytes 16777232 | tf_op jit(solution)/shard_map/all_gather | solution.py:27
  328.5 0.0 copy-start
  328.5 9.8 %fusion.5 = f32[256,4096]{1,0:T(8,128)S(1)} fusion(f32[2,256,256]{2,1,0:T(8,128)S(1)} %fusion.16, f32[2,2,256,4096]{3,2,0,1:T(8,128)} %all-gather.8.cloned.1.call-done), kind=kOutput, calls=%fused_computation.8 | convolution fusion | flops 6442450944 | bytes 13107200 | tf_op jit(solution)/shard_map/nba,nac->bc/dot_general | solution.py:8
  338.3 9.6 %fusion.4 = f32[256,4096]{1,0:T(8,128)S(1)} fusion(f32[2,256,256]{2,1,0:T(8,128)S(1)} %fusion.17, f32[2,2,256,4096]{3,2,0,1:T(8,128)} %all-gather.8.cloned.1.call-done), kind=kOutput, calls=%fused_computation.7 | convolution fusion | flops 6442450944 | bytes 13107200 | tf_op jit(solution)/shard_map/nba,nac->bc/dot_general | solution.py:8
  348.0 0.0 copy-done
  348.0 7.8 %fusion.9 = f32[1,256,4096]{2,1,0:T(8,128)S(1)} fusion(f32[256,4096]{1,0:T(8,128)S(1)} %fusion.5, f32[2,256,256]{2,1,0:T(8,128)S(1)} %fusion.17, f32[2,2,256,4096]{3,2,0,1:T(8,128)S(1)} %copy-done), kind=kOutput, calls=%fused_computation.12 | convolution fusion | flops 6443499520 | bytes 17301504 | tf_op jit(solution)/shard_map/nba,nac->bc/dot_general | solution.py:8
  355.8 8.1 %fusion.11 = f32[1,256,4096]{2,1,0:T(8,128)S(1)} fusion(f32[256,4096]{1,0:T(8,128)S(1)} %fusion.4, f32[2,256,256]{2,1,0:T(8,128)S(1)} %fusion.16, f32[2,2,256,4096]{3,2,0,1:T(8,128)S(1)} %copy-done), kind=kOutput, calls=%fused_computation.14 | convolution fusion | flops 6443499520 | bytes 17301504 | tf_op jit(solution)/shard_map/nba,nac->bc/dot_general | solution.py:8
  363.9 4.2 pad_maximum_fusion
  368.1 0.0 reduce-scatter.2.cloned.1.call-update
  368.2 70.9 %reduce-scatter.2.cloned.1.call-done = f32[2,256,256]{2,1,0:T(8,128)} async-done(((f32[2,256,4096]{2,1,0:T(8,128)}), f32[2,256,256]{2,1,0:T(8,128)}) %reduce-scatter.2.cloned.1.call-update) | async-done | bytes 524304 | tf_op jit(solution)/shard_map/reduce_scatter | solution.py:37
Async XLA Ops:
  6.5 73.7 %all-gather.6.cloned.1.call-start = ((), (), s32[]{:S(2)}) async-start(), calls=%async_computation.2 | async-start | bytes 4718592 | tf_op jit(solution)/shard_map/all_gather | solution.py:14
  7.3 133.6 %all-gather.4.cloned.1.call-start = ((), (), s32[]{:S(2)}) async-start(), calls=%async_computation.1 | async-start | bytes 8912896 | tf_op jit(solution)/shard_map/all_gather | solution.py:15
  9.4 319.2 %all-gather.8.cloned.1.call-start = ((), (), s32[]{:S(2)}) async-start(), calls=%async_computation.3 | async-start | bytes 18874368 | tf_op jit(solution)/shard_map/all_gather | solution.py:27
  12.5 426.6 %reduce-scatter.2.cloned.1.call-start = ((), (), s32[]{:S(2)}) async-start(), calls=%async_computation.4 | async-start | bytes 8912896 | tf_op jit(solution)/shard_map/reduce_scatter | solution.py:37
  140.8 12.4 %copy-start.1 = (f32[2,2,2048,256]{2,3,0,1:T(8,128)S(1)}, f32[2,2,2048,256]{2,3,0,1:T(8,128)}, u32[]{:S(2)}) copy-start(f32[2,2,2048,256]{2,3,0,1:T(8,128)} %all-gather.4.cloned.1.call-done) | copy-start | bytes 25165828
  147.0 6.2 %copy-start.2 = (f32[2,2048,256]{2,1,0:T(8,128)S(1)}, f32[2,2048,256]{2,1,0:T(8,128)}, u32[]{:S(2)}) copy-start(f32[2,2048,256]{2,1,0:T(8,128)} %all-gather.6.cloned.1.call-done) | copy-start | bytes 12582916
  328.5 19.4 %copy-start = (f32[2,2,256,4096]{3,2,0,1:T(8,128)S(1)}, f32[2,2,256,4096]{3,2,0,1:T(8,128)}, u32[]{:S(2)}) copy-start(f32[2,2,256,4096]{3,2,0,1:T(8,128)} %all-gather.8.cloned.1.call-done) | copy-start | bytes 50331652
Sparse Core Ops, SparseCore 0:
  9.7 70.4 all-gather.5
  81.8 58.9 all-gather.3
  143.2 185.2 all-gather.7
  368.3 70.7 reduce-scatter.1
where the time goes:
time: 451 us; the launch traced here: 446 us
  waiting for transfers between devices  368 us (82%)
  matrix products  54.6 us (12%)
  between operations  13.2 us (3%)
  local copies, waits for them, and re-layouts  5.13 us (1%)
    all_gather x1, waiting for transfers between devices, local(): piece = lax.all_gather(initial_site, 'row', axis=3, tiled=True)  168 us
    reduce_scatter x1, waiting for transfers between devices, local(): lax.psum_scatter(partial_env, 'col', scatter_dimension=2, tiled=True)  70.9 us
    all_gather x1, waiting for transfers between devices, local(): column = lax.all_gather(environment, 'row', axis=1, tiled=True)  67.6 us
    all_gather x1, waiting for transfers between devices, local(): piece = lax.all_gather(compressed_site, 'col', axis=2, tiled=True)  60.6 us
    dot_general x8, matrix products, contract(): jnp.einsum(form, left, right, precision=lax.Precision.HIGHEST, preferred_...  54.6 us
  transfers between devices with their start and end apart: 4, of which 4 were waited for; matrix products, arithmetic and copies ran while one was open for 5% of the time, Pallas kernels for 0%

commit v1 on v0

v1 whole, which is shorter than its diff:
```python
import jax
import jax.numpy as jnp
from jax import lax
from jax.experimental import pallas as pl
from jax.experimental.pallas import tpu as pltpu
from jax.sharding import Mesh, PartitionSpec as P

PARTS = {"zh": 2, "x": 4, "zl": 2, "y": 4, "core": 2}
F32 = jnp.float32
BF16 = jnp.bfloat16


def move(value, axis, step):
    n = PARTS[axis]
    return lax.ppermute(value, axis, [(i, (i + step) % n) for i in range(n)])


def split(value):
    high = value.astype(BF16)
    return high, (value - high.astype(F32)).astype(BF16)


def dot3(left, right, dims):
    (lh, ll), (rh, rl) = left, right

    def one(a, b):
        return lax.dot_general(a, b, (dims, ((), ())), preferred_element_type=F32)

    return one(lh, rh) + (one(lh, rl) + one(ll, rh))


def mixed_kernel(place, b_ref, *refs):
    l_refs, out_ref = refs[:-1], refs[-1]
    depth = l_refs[0].shape[1]
    for level in range(2):
        total = [None, None]
        for pair in range(len(l_refs) // 2):
            rows = [pl.multiple_of(place[2 * pair + i] * depth, depth) for i in range(2)]

            def block(part):
                return split(
                    jnp.concatenate([b_ref[level, part, pl.ds(r, depth), :] for r in rows], axis=0)
                )

            def env(part):
                return split(
                    jnp.concatenate([l_refs[2 * pair + i][part] for i in range(2)], axis=0)
                )

            b_re, b_im, l_re, l_im = block(0), block(1), env(0), env(1)
            dims = ((0,), (0,))
            new = [
                dot3(b_re, l_re, dims) + dot3(b_im, l_im, dims),
                dot3(b_re, l_im, dims) - dot3(b_im, l_re, dims),
            ]
            total = new if total[0] is None else [t + u for t, u in zip(total, new)]
        for part in range(2):
            out_ref[level, part] = total[part]


def update_kernel(place, m_ref, *refs):
    a_refs, out_ref = refs[:-1], refs[-1]
    wide = a_refs[0].shape[-1]
    dims = ((1,), (0,))
    left = [[split(m_ref[level, part]) for part in range(2)] for level in range(2)]
    for j in range(4):
        total = None
        for level in range(2):
            if j < 3:
                a_re, a_im = a_refs[j][level, 0], a_refs[j][level, 1]
            else:
                a_re, a_im = a_refs[3 + level][0], a_refs[3 + level][1]
            (rh, rl), (ih, il) = split(a_re), split(a_im)

            def beside(p, q):
                return jnp.concatenate([p, q], axis=1)

            new = dot3(left[level][0], (beside(rh, ih), beside(rl, il)), dims) + dot3(
                left[level][1], (beside(-ih, rh), beside(-il, rl)), dims
            )
            total = new if total is None else total + new
        out_ref[place[j], 0] = total[:, :wide]
        out_ref[place[j], 1] = total[:, wide:]


def call(kernel, out_shape, flops, place, *operands):
    vmem = pl.BlockSpec(memory_space=pltpu.VMEM)
    size = sum(4 * v.size for v in operands) + 4 * out_shape.size
    return pl.pallas_call(
        kernel,
        out_shape=out_shape,
        in_specs=[pl.BlockSpec(memory_space=pltpu.SMEM)] + [vmem] * len(operands),
        out_specs=vmem,
        compiler_params=pltpu.CompilerParams(vmem_limit_bytes=48 * 1024 * 1024),
        cost_estimate=pl.CostEstimate(flops=flops, bytes_accessed=size, transcendentals=0),
    )(place, *operands)


def mixed_partial(place, site, blocks):
    levels, _, _, b = site.shape
    a = blocks[0].shape[-1]
    out = jax.ShapeDtypeStruct((levels, 2, b, a), F32)
    flops = 2 * 3 * 4 * levels * site.shape[2] * b * a
    return call(mixed_kernel, out, flops, place, site, *blocks)


def update_partial(place, mixed, pieces):
    levels, _, b, a = mixed.shape
    c = pieces[0].shape[-1]
    out = jax.ShapeDtypeStruct((4, 2, b, c), F32)
    flops = 2 * 3 * 4 * levels * b * a * 4 * c
    return call(update_kernel, out, flops, place, mixed, *pieces)


def half(value, index, axis):
    size = value.shape[axis] // 2
    return lax.dynamic_slice_in_dim(value, index * size, size, axis)


def reduce_y(parts):
    up = move(parts[2, 0], "y", 1)
    down = move(parts[2, 1], "y", -1)
    up = move(jnp.stack([parts[1, 0] + up, parts[1, 1]]), "y", 1)
    down = move(jnp.stack([parts[3, 0], parts[3, 1] + down]), "y", -1)
    return parts[0] + up + down


def local(environment, initial_site, compressed_site):
    zh, x, zl, y, core = (lax.axis_index(name) for name in PARTS)

    rows_mine = half(environment, core, 1)
    rows_other = move(half(environment, 1 - core, 1), "core", 1)
    env = jnp.concatenate([rows_mine, rows_other], axis=2)
    cols_mine = half(initial_site, core, 3)
    cols_other = move(half(initial_site, 1 - core, 3), "core", 1)
    site = jnp.concatenate([cols_mine, cols_other], axis=2)

    comp = lax.all_gather(compressed_site, ("zl", "y"), axis=2, tiled=True)

    env_1 = move(env, "x", -1)
    env_3 = move(env, "x", 1)
    far_0 = move(env, "zh", 1)
    env_2 = jnp.stack([move(env_1[0], "x", -1), move(env_3[1], "x", 1)])
    far_1 = move(env_1, "zh", 1)
    far_3 = move(env_3, "zh", 1)
    far_2 = move(env_2, "zh", 1)
    blocks = [env, env_1, env_2, env_3, far_0, far_1, far_2, far_3]
    place = jnp.stack(
        [(zh if i < 4 else 1 - zh) * 4 + (x + i) % 4 for i in range(8)]
    ).astype(jnp.int32)

    share = mixed_partial(place, comp, blocks)
    other = move(share, "core", 1)
    wide = share.shape[-1] // 2
    mixed_mine = share[..., :wide] + other[..., wide:]
    mixed = jnp.concatenate([mixed_mine, share[..., wide:] + other[..., :wide]], axis=-1)
    far_mine = move(mixed_mine, "zh", 1)
    mixed_far = jnp.concatenate([far_mine, move(far_mine, "core", 1)], axis=-1)

    slices = []
    width = site.shape[-1] // 2
    for s in range(2):
        a_0 = site[..., s * width : (s + 1) * width]
        a_1 = move(a_0, "x", -1)
        a_3 = move(a_0, "x", 1)
        a_2 = [move(a_1[0], "x", -1), move(a_3[1], "x", 1)]
        slices.append([a_0, a_1, a_3, *a_2])
    order = jnp.stack([(x + j - y) % 4 for j in (0, 1, 3, 2)]).astype(jnp.int32)

    results = []
    for s in range(2):
        mine = reduce_y(update_partial(order, mixed, slices[s]))
        far = reduce_y(update_partial(order, mixed_far, slices[s]))
        same = zl == zh
        got = move(jnp.where(same, far, mine), "zl", 1)
        full = jnp.where(same, mine, far) + got
        results.append(lax.ppermute(full, ("zh", "zl"), [(0, 0), (1, 2), (2, 1), (3, 3)]))
    return jnp.concatenate(results, axis=2)


def solution(mesh):
    names = tuple(PARTS)
    parts = Mesh(mesh.devices.reshape(tuple(PARTS.values())), names)
    row, col = names[:2], names[2:]
    return jax.shard_map(
        local,
        mesh=parts,
        in_specs=(P(None, row, col), P(None, None, col, row), P(None, None, col, row)),
        out_specs=P(None, row, col),
        check_vma=False,
    )
```

time: 451 us -> 273 us (0.61)
  waiting for transfers between devices: 368 us -> 150 us
  starting transfers between devices: 0.12 us -> 56.8 us
  matrix products: 54.6 us -> 0 us
  Pallas kernels: 0 us -> 33.2 us
    all_gather x3 -> x1, waiting for transfers between devices: 297 us -> 0.01 us  [local(): comp = lax.all_gather(compressed_site, ('zl', 'y'), axis=2, tiled=True)]
    ppermute x0 -> x41, waiting for transfers between devices: none -> 150 us  [the longest x39 143 us: move(): return lax.ppermute(value, axis, [(i, (i + step) % n) for i in range(n)])]
    reduce_scatter x1 -> x0, waiting for transfers between devices: 70.9 us -> none  [local(): lax.psum_scatter(partial_env, 'col', scatter_dimension=2, tiled=True)]
    ppermute x0 -> x41, starting transfers between devices: none -> 56.8 us  [the longest x39 52.4 us: move(): return lax.ppermute(value, axis, [(i, (i + step) % n) for i in range(n)])]
    dot_general x8 -> x0, matrix products: 54.6 us -> none  [contract(): jnp.einsum(form, left, right, precision=lax.Precision.HIGHEST, preferred_...]
    pallas_call x0 -> x5, Pallas kernels: none -> 33.2 us  [call(): pl.pallas_call(kernel, out_shape=out_shape, in_specs=[pl.BlockSpec(memory...]
  transfers between devices with their start and end apart: 4 -> 42, of which waited for: 4 -> 20; matrix products, arithmetic and copies ran while one was open for 5% -> 5% of each run, Pallas kernels for 0% -> 12%
where the time goes in v1:
time: 273 us; the launch traced here: 271 us
  waiting for transfers between devices  150 us (55%)
  starting transfers between devices  56.8 us (21%)
  Pallas kernels  33.2 us (12%)
  between operations  13.8 us (5%)
  local copies, waits for them, and re-layouts  9.33 us (3%)
  other arithmetic  7.43 us (3%)
    ppermute x39, waiting for transfers between devices, move(): return lax.ppermute(value, axis, [(i, (i + step) % n) for i in range(n)])  143 us
    ppermute x39, starting transfers between devices, move(): return lax.ppermute(value, axis, [(i, (i + step) % n) for i in range(n)])  52.4 us
    pallas_call x5, Pallas kernels, call(): pl.pallas_call(kernel, out_shape=out_shape, in_specs=[pl.BlockSpec(memory...  33.2 us
    ppermute x2, waiting for transfers between devices, local(): lax.ppermute(full, ('zh', 'zl'), [(0, 0), (1, 2), (2, 1), (3, 3)])  6.82 us
  transfers between devices with their start and end apart: 42, of which 20 were waited for; matrix products, arithmetic and copies ran while one was open for 5% of the time, Pallas kernels for 12%

profile of v1, /device:TPU:62, one launch (start us, length us, event | category | flops | bytes accessed | tf_op | source)
XLA Modules:
  0.0 270.9 jit_solution(5360268035761212221)
XLA Ops:
  13.3 11.9 %collective-permute-done.1.refs_1_ = f32[2,128,512]{2,1,0:T(8,128)S(1)} collective-permute-done((f32[2,128,512]{2,1,0:T(8,128)S(1)}, f32[2,128,512]{2,1,0:T(8,128)S(1)}, u32[]{:S(2)}, u32[]{:S(2)}) %collective-permute-start.1) | collective-permute-done | bytes 524320 | tf_op jit(solution)/shard_map/ppermute | solution.py:15
  25.4 3.3 %collective-permute-start.4 = (f32[128,512]{1,0:T(8,128)S(1)}, f32[128,512]{1,0:T(8,128)}, u32[]{:S(2)}, u32[]{:S(2)}) collective-permute-start(f32[128,512]{1,0:T(8,128)S(1)} %slice_bitcast_fusion.8), channel_id=1, source_target_pairs={{0,16},{16,32},{32,48},{48,0},{1,17},{17,33},{33,49},{49,1},{2,18}... | collective-permute-start | bytes 786440 | tf_op jit(solution)/shard_map/ppermute | solution.py:15
  28.7 3.0 %collective-permute-start.5 = (f32[2,128,512]{2,1,0:T(8,128)S(1)}, f32[2,128,512]{2,1,0:T(8,128)S(1)}, u32[]{:S(2)}, u32[]{:S(2)}) collective-permute-start(f32[2,128,512]{2,1,0:T(8,128)S(1)} %pad_maximum_fusion.2.refs_0_), channel_id=1, source_target_pairs={{0,64},{64,0},{1,65},{65,1},{2,66},{66,2},{3,67},{67,3},{4,68},{68... | collective-permute-start | bytes 1572872 | tf_op jit(solution)/shard_map/ppermute | solution.py:15
  32.2 3.0 %collective-permute-start.8 = (f32[2,128,512]{2,1,0:T(8,128)S(1)}, f32[2,128,512]{2,1,0:T(8,128)}, u32[]{:S(2)}, u32[]{:S(2)}) collective-permute-start(f32[2,128,512]{2,1,0:T(8,128)S(1)} %collective-permute-done.3.refs_3_), channel_id=1, source_target_pairs={{0,64},{64,0},{1,65},{65,1},{2,66},{66,2},{3,67},{67,3},{4,68},{68... | collective-permute-start | bytes 1572872 | tf_op jit(solution)/shard_map/ppermute | solution.py:15
  38.2 3.1 %constant_dynamic-slice_fusion.1 = (f32[2,2,256,256]{3,2,1,0:T(8,128)}, f32[2,2,256,256]{3,2,1,0:T(8,128)}) fusion(f32[2,2,256,512]{3,2,1,0:T(8,128)} %param.4, s32[]{:T(128)S(6)} %select_n.98, s32[]{:T(128)S(6)} %select_n.99), kind=kLoop, calls=%fused_computation.83 | loop fusion | bytes 4194312 | tf_op jit(solution)/shard_map/dynamic_slice | solution.py:117
  41.4 31.3 %collective-permute-done.5.refs_4_ = f32[2,128,512]{2,1,0:T(8,128)S(1)} collective-permute-done((f32[2,128,512]{2,1,0:T(8,128)S(1)}, f32[2,128,512]{2,1,0:T(8,128)S(1)}, u32[]{:S(2)}, u32[]{:S(2)}) %collective-permute-start.5) | collective-permute-done | bytes 524320 | tf_op jit(solution)/shard_map/ppermute | solution.py:15
  72.7 11.2 %collective-permute-done.6.refs_5_ = f32[2,128,512]{2,1,0:T(8,128)S(1)} collective-permute-done((f32[2,128,512]{2,1,0:T(8,128)S(1)}, f32[2,128,512]{2,1,0:T(8,128)S(1)}, u32[]{:S(2)}, u32[]{:S(2)}) %collective-permute-start.6) | collective-permute-done | bytes 524320 | tf_op jit(solution)/shard_map/ppermute | solution.py:15
  83.9 11.3 %collective-permute-done.8.refs_7_ = f32[2,128,512]{2,1,0:T(8,128)} collective-permute-done((f32[2,128,512]{2,1,0:T(8,128)S(1)}, f32[2,128,512]{2,1,0:T(8,128)}, u32[]{:S(2)}, u32[]{:S(2)}) %collective-permute-start.8) | collective-permute-done | bytes 524320 | tf_op jit(solution)/shard_map/ppermute | solution.py:15
  95.3 11.1 %collective-permute-done.7.refs_6_ = f32[2,128,512]{2,1,0:T(8,128)} collective-permute-done((f32[2,128,512]{2,1,0:T(8,128)S(1)}, f32[2,128,512]{2,1,0:T(8,128)}, u32[]{:S(2)}, u32[]{:S(2)}) %collective-permute-start.7) | collective-permute-done | bytes 524320 | tf_op jit(solution)/shard_map/ppermute | solution.py:15
  106.4 10.9 %shard_map.37 = f32[2,2,256,512]{3,2,1,0:T(8,128)} custom-call(s32[8]{0:T(128)S(1)} %stack.112.place, f32[2,2,1024,256]{3,2,1,0:T(8,128)} %all-gather.2.cloned.1.call-done.b_ref, f32[2,128,512]{2,1,0:T(8,128)S(1)} %pad_maximum_fusion.2.refs_0_, f32[2,128,512]{2,1,0:T(8,128)S(1)} %collective-permute-done.1.refs_1_, ...), custom_call_target="tpu_custom_call" | custom-call | flops 6442450944 | bytes 10485760 | tf_op jit(solution)/shard_map/pallas_call | solution.py:89
  122.1 3.2 %collective-permute-start.28 = (f32[2,2,512,128]{3,2,1,0:T(8,128)S(1)}, f32[2,2,512,128]{3,2,1,0:T(8,128)}, u32[]{:S(2)}, u32[]{:S(2)}) collective-permute-start(f32[2,2,512,128]{3,2,1,0:T(8,128)S(1)} %get-tuple-element.8.refs_0_), channel_id=1, source_target_pairs={{0,16},{16,32},{32,48},{48,0},{1,17},{17,33},{33,49},{49,1},{2,18}... | collective-permute-start | bytes 3145736 | tf_op jit(solution)/shard_map/ppermute | solution.py:15
  125.4 20.7 %collective-permute-done.11.refs_1_ = f32[2,2,512,128]{3,2,1,0:T(8,128)} collective-permute-done((f32[2,2,512,128]{3,2,1,0:T(8,128)S(1)}, f32[2,2,512,128]{3,2,1,0:T(8,128)}, u32[]{:S(2)}, u32[]{:S(2)}) %collective-permute-start.11) | collective-permute-done | bytes 1048608 | tf_op jit(solution)/shard_map/ppermute | solution.py:15
  148.5 3.3 %collective-permute-start.14 = (f32[2,512,128]{2,1,0:T(8,128)S(1)}, f32[2,512,128]{2,1,0:T(8,128)S(1)}, u32[]{:S(2)}, u32[]{:S(2)}) collective-permute-start(f32[2,512,128]{2,1,0:T(8,128)S(1)} %slice_bitcast_fusion.2), channel_id=1, source_target_pairs={{0,16},{16,32},{32,48},{48,0},{1,17},{17,33},{33,49},{49,1},{2,18}... | collective-permute-start | bytes 1572872 | tf_op jit(solution)/shard_map/ppermute | solution.py:15
  151.8 16.6 %collective-permute-done.27.refs_1_ = f32[2,2,512,128]{3,2,1,0:T(8,128)S(1)} collective-permute-done((f32[2,2,512,128]{3,2,1,0:T(8,128)S(1)}, f32[2,2,512,128]{3,2,1,0:T(8,128)S(1)}, u32[]{:S(2)}, u32[]{:S(2)}) %collective-permute-start.27) | collective-permute-done | bytes 1048608 | tf_op jit(solution)/shard_map/ppermute | solution.py:15
  169.7 3.3 %collective-permute-start.30 = (f32[2,512,128]{2,1,0:T(8,128)S(1)}, f32[2,512,128]{2,1,0:T(8,128)S(1)}, u32[]{:S(2)}, u32[]{:S(2)}) collective-permute-start(f32[2,512,128]{2,1,0:T(8,128)S(1)} %slice_bitcast_fusion), channel_id=1, source_target_pairs={{0,16},{16,32},{32,48},{48,0},{1,17},{17,33},{33,49},{49,1},{2,18}... | collective-permute-start | bytes 1572872 | tf_op jit(solution)/shard_map/ppermute | solution.py:15
  179.7 5.7 %shard_map.38 = f32[4,2,256,128]{3,2,1,0:T(8,128)S(1)} custom-call(s32[4]{0:T(128)S(1)} %pad_add_fusion.place, f32[2,2,256,512]{3,2,1,0:T(8,128)} %pad_maximum_fusion.m_ref, f32[2,2,512,128]{3,2,1,0:T(8,128)S(1)} %get-tuple-element.7.refs_0_, f32[2,2,512,128]{3,2,1,0:T(8,128)} %collective-permute-done.11.refs_1_, ...), custom_call_target="tpu_custom_call" | custom-call | flops 3221225472 | bytes 7340032 | tf_op jit(solution)/shard_map/pallas_call | solution.py:89
  185.5 2.6 collective-permute-start.15
  190.5 5.4 %shard_map.40 = f32[4,2,256,128]{3,2,1,0:T(8,128)S(1)} custom-call(s32[4]{0:T(128)S(1)} %pad_add_fusion.place, f32[2,2,256,512]{3,2,1,0:T(8,128)} %pad_maximum_fusion.m_ref, f32[2,2,512,128]{3,2,1,0:T(8,128)S(1)} %get-tuple-element.8.refs_0_, f32[2,2,512,128]{3,2,1,0:T(8,128)S(1)} %collective-permute-done.27.refs_1_, ...), custom_call_target="tpu_custom_call" | custom-call | flops 3221225472 | bytes 7340032 | tf_op jit(solution)/shard_map/pallas_call | solution.py:89
  196.0 2.6 collective-permute-start.31
  200.3 2.6 collective-permute-start.16
  208.3 5.7 %shard_map.39 = f32[4,2,256,128]{3,2,1,0:T(8,128)S(1)} custom-call(s32[4]{0:T(128)S(1)} %pad_add_fusion.place, f32[2,2,256,512]{3,2,1,0:T(8,128)} %copy-done.2, f32[2,2,512,128]{3,2,1,0:T(8,128)S(1)} %get-tuple-element.7.refs_0_, f32[2,2,512,128]{3,2,1,0:T(8,128)} %collective-permute-done.11.refs_1_, f32[2,2,512,128]{3,2,1,0:T(8,128)} %collective-permute-done.12.refs_2_, ...), custom_call_target="tpu_custom_call" | custom-call | flops 3221225472 | bytes 7340032 | tf_op jit(solution)/shard_map/pallas_call | solution.py:89
  216.2 5.4 %shard_map.41 = f32[4,2,256,128]{3,2,1,0:T(8,128)S(1)} custom-call(s32[4]{0:T(128)S(1)} %pad_add_fusion.place, f32[2,2,256,512]{3,2,1,0:T(8,128)} %copy-done.2, f32[2,2,512,128]{3,2,1,0:T(8,128)S(1)} %get-tuple-element.8.refs_0_, f32[2,2,512,128]{3,2,1,0:T(8,128)S(1)} %collective-permute-done.27.refs_1_, f32[2,2,512,128]{3,2,1,0:T(8,128)} %collective-permute-done.28.refs_2_, ...), custom_call_target="tpu_custom_call" | custom-call | flops 3221225472 | bytes 7340032 | tf_op jit(solution)/shard_map/pallas_call | solution.py:89
  223.8 2.9 %collective-permute-done.35 = f32[256,128]{1,0:T(8,128)S(1)} collective-permute-done((f32[256,128]{1,0:T(8,128)S(1)}, f32[256,128]{1,0:T(8,128)S(1)}, u32[]{:S(2)}, u32[]{:S(2)}) %collective-permute-start.35) | collective-permute-done | bytes 131104 | tf_op jit(solution)/shard_map/ppermute | solution.py:15
  226.7 2.5 collective-permute-start.22
  229.5 3.2 %collective-permute-start.36 = (f32[2,256,128]{2,1,0:T(8,128)S(1)}, f32[2,256,128]{2,1,0:T(8,128)S(1)}, u32[]{:S(2)}, u32[]{:S(2)}) collective-permute-start(f32[2,256,128]{2,1,0:T(8,128)S(1)} %pad_maximum_fusion.11), channel_id=1, source_target_pairs={{0,2},{2,4},{4,6},{6,0},{1,3},{3,5},{5,7},{7,1},{8,10},{10,12},{12... | collective-permute-start | bytes 786440 | tf_op jit(solution)/shard_map/ppermute | solution.py:15
  232.7 3.1 %collective-permute-done.22 = f32[2,256,128]{2,1,0:T(8,128)S(1)} collective-permute-done((f32[2,256,128]{2,1,0:T(8,128)S(1)}, f32[2,256,128]{2,1,0:T(8,128)S(1)}, u32[]{:S(2)}, u32[]{:S(2)}) %collective-permute-start.22) | collective-permute-done | bytes 262176 | tf_op jit(solution)/shard_map/ppermute | solution.py:15
  235.8 3.8 %collective-permute-done.24 = f32[2,256,128]{2,1,0:T(8,128)S(1)} collective-permute-done((f32[2,256,128]{2,1,0:T(8,128)S(1)}, f32[2,256,128]{2,1,0:T(8,128)S(1)}, u32[]{:S(2)}, u32[]{:S(2)}) %collective-permute-start.24) | collective-permute-done | bytes 262176 | tf_op jit(solution)/shard_map/ppermute | solution.py:15
  241.1 3.9 %collective-permute-done.34 = f32[2,256,128]{2,1,0:T(8,128)S(1)} collective-permute-done((f32[2,256,128]{2,1,0:T(8,128)S(1)}, f32[2,256,128]{2,1,0:T(8,128)S(1)}, u32[]{:S(2)}, u32[]{:S(2)}) %collective-permute-start.34) | collective-permute-done | bytes 262176 | tf_op jit(solution)/shard_map/ppermute | solution.py:15
  245.0 2.8 %collective-permute-done.38 = f32[2,256,128]{2,1,0:T(8,128)S(1)} collective-permute-done((f32[2,256,128]{2,1,0:T(8,128)S(1)}, f32[2,256,128]{2,1,0:T(8,128)S(1)}, u32[]{:S(2)}, u32[]{:S(2)}) %collective-permute-start.38) | collective-permute-done | bytes 262176 | tf_op jit(solution)/shard_map/ppermute | solution.py:15
  251.8 2.5 collective-permute-done.39
  256.4 4.0 %collective-permute-done.26 = f32[2,256,128]{2,1,0:T(8,128)S(1)} collective-permute-done((f32[2,256,128]{2,1,0:T(8,128)S(1)}, f32[2,256,128]{2,1,0:T(8,128)S(1)}, u32[]{:S(2)}, u32[]{:S(2)}) %collective-permute-start.26) | collective-permute-done | bytes 262176 | tf_op jit(solution)/shard_map/ppermute | solution.py:177
  260.4 2.9 %collective-permute-done.40 = f32[2,256,128]{2,1,0:T(8,128)S(1)} collective-permute-done((f32[2,256,128]{2,1,0:T(8,128)S(1)}, f32[2,256,128]{2,1,0:T(8,128)S(1)}, u32[]{:S(2)}, u32[]{:S(2)}) %collective-permute-start.40) | collective-permute-done | bytes 262176 | tf_op jit(solution)/shard_map/ppermute | solution.py:177
  (102 shorter events, 47.9 us)
Async XLA Ops:
  6.5 99.9 %all-gather.2.cloned.1.call-start = ((), (), s32[]{:S(2)}) async-start(), calls=%async_computation | async-start | bytes 4718592 | tf_op jit(solution)/shard_map/all_gather | solution.py:138
  10.0 15.2 %collective-permute-start.1 = (f32[2,128,512]{2,1,0:T(8,128)S(1)}, f32[2,128,512]{2,1,0:T(8,128)S(1)}, u32[]{:S(2)}, u32[]{:S(2)}) collective-permute-start(f32[2,128,512]{2,1,0:T(8,128)S(1)} %pad_maximum_fusion.2.refs_0_), channel_id=1, source_target_pairs={{0,48},{16,0},{32,16},{48,32},{1,49},{17,1},{33,17},{49,33},{2,50}... | collective-permute-start | bytes 1572872 | tf_op jit(solution)/shard_map/ppermute | solution.py:15
  10.9 14.5 %collective-permute-start.3 = (f32[2,128,512]{2,1,0:T(8,128)S(1)}, f32[2,128,512]{2,1,0:T(8,128)S(1)}, u32[]{:S(2)}, u32[]{:S(2)}) collective-permute-start(f32[2,128,512]{2,1,0:T(8,128)S(1)} %pad_maximum_fusion.2.refs_0_), channel_id=1, source_target_pairs={{0,16},{16,32},{32,48},{48,0},{1,17},{17,33},{33,49},{49,1},{2,18}... | collective-permute-start | bytes 1572872 | tf_op jit(solution)/shard_map/ppermute | solution.py:15
  25.3 9.9 %collective-permute-start.2 = (f32[128,512]{1,0:T(8,128)S(1)}, f32[128,512]{1,0:T(8,128)S(1)}, u32[]{:S(2)}, u32[]{:S(2)}) collective-permute-start(f32[128,512]{1,0:T(8,128)S(1)} %slice_bitcast_fusion.9), channel_id=1, source_target_pairs={{0,48},{16,0},{32,16},{48,32},{1,49},{17,1},{33,17},{49,33},{2,50}... | collective-permute-start | bytes 786440 | tf_op jit(solution)/shard_map/ppermute | solution.py:15
  25.4 9.8 %collective-permute-start.4 = (f32[128,512]{1,0:T(8,128)S(1)}, f32[128,512]{1,0:T(8,128)}, u32[]{:S(2)}, u32[]{:S(2)}) collective-permute-start(f32[128,512]{1,0:T(8,128)S(1)} %slice_bitcast_fusion.8), channel_id=1, source_target_pairs={{0,16},{16,32},{32,48},{48,0},{1,17},{17,33},{33,49},{49,1},{2,18}... | collective-permute-start | bytes 786440 | tf_op jit(solution)/shard_map/ppermute | solution.py:15
  28.7 44.0 %collective-permute-start.5 = (f32[2,128,512]{2,1,0:T(8,128)S(1)}, f32[2,128,512]{2,1,0:T(8,128)S(1)}, u32[]{:S(2)}, u32[]{:S(2)}) collective-permute-start(f32[2,128,512]{2,1,0:T(8,128)S(1)} %pad_maximum_fusion.2.refs_0_), channel_id=1, source_target_pairs={{0,64},{64,0},{1,65},{65,1},{2,66},{66,2},{3,67},{67,3},{4,68},{68... | collective-permute-start | bytes 1572872 | tf_op jit(solution)/shard_map/ppermute | solution.py:15
  31.7 52.3 %collective-permute-start.6 = (f32[2,128,512]{2,1,0:T(8,128)S(1)}, f32[2,128,512]{2,1,0:T(8,128)S(1)}, u32[]{:S(2)}, u32[]{:S(2)}) collective-permute-start(f32[2,128,512]{2,1,0:T(8,128)S(1)} %collective-permute-done.1.refs_1_), channel_id=1, source_target_pairs={{0,64},{64,0},{1,65},{65,1},{2,66},{66,2},{3,67},{67,3},{4,68},{68... | collective-permute-start | bytes 1572872 | tf_op jit(solution)/shard_map/ppermute | solution.py:15
  32.2 63.1 %collective-permute-start.8 = (f32[2,128,512]{2,1,0:T(8,128)S(1)}, f32[2,128,512]{2,1,0:T(8,128)}, u32[]{:S(2)}, u32[]{:S(2)}) collective-permute-start(f32[2,128,512]{2,1,0:T(8,128)S(1)} %collective-permute-done.3.refs_3_), channel_id=1, source_target_pairs={{0,64},{64,0},{1,65},{65,1},{2,66},{66,2},{3,67},{67,3},{4,68},{68... | collective-permute-start | bytes 1572872 | tf_op jit(solution)/shard_map/ppermute | solution.py:15
  36.2 70.2 %collective-permute-start.7 = (f32[2,128,512]{2,1,0:T(8,128)S(1)}, f32[2,128,512]{2,1,0:T(8,128)}, u32[]{:S(2)}, u32[]{:S(2)}) collective-permute-start(f32[2,128,512]{2,1,0:T(8,128)S(1)} %pad_maximum_fusion.3.refs_2_), channel_id=1, source_target_pairs={{0,64},{64,0},{1,65},{65,1},{2,66},{66,2},{3,67},{67,3},{4,68},{68... | collective-permute-start | bytes 1572872 | tf_op jit(solution)/shard_map/ppermute | solution.py:15
  41.3 76.0 %collective-permute-start.10 = (f32[2,2,256,256]{3,2,1,0:T(8,128)}, f32[2,2,256,256]{3,2,1,0:T(8,128)}, u32[]{:S(2)}, u32[]{:S(2)}) collective-permute-start(f32[2,2,256,256]{3,2,1,0:T(8,128)} %get-tuple-element.10), channel_id=1, source_target_pairs={{0,1},{1,0},{2,3},{3,2},{4,5},{5,4},{6,7},{7,6},{8,9},{9,8},{10,11... | collective-permute-start | bytes 3145736 | tf_op jit(solution)/shard_map/ppermute | solution.py:15
  117.4 55.6 %collective-permute-start.9 = (f32[2,2,256,512]{3,2,1,0:T(8,128)}, f32[2,2,256,512]{3,2,1,0:T(8,128)}, u32[]{:S(2)}, u32[]{:S(2)}) collective-permute-start(f32[2,2,256,512]{3,2,1,0:T(8,128)} %shard_map.37), channel_id=1, source_target_pairs={{0,1},{1,0},{2,3},{3,2},{4,5},{5,4},{6,7},{7,6},{8,9},{9,8},{10,11... | collective-permute-start | bytes 6291464 | tf_op jit(solution)/shard_map/ppermute | solution.py:15
  118.7 27.3 %collective-permute-start.11 = (f32[2,2,512,128]{3,2,1,0:T(8,128)S(1)}, f32[2,2,512,128]{3,2,1,0:T(8,128)}, u32[]{:S(2)}, u32[]{:S(2)}) collective-permute-start(f32[2,2,512,128]{3,2,1,0:T(8,128)S(1)} %get-tuple-element.7.refs_0_), channel_id=1, source_target_pairs={{0,48},{16,0},{32,16},{48,32},{1,49},{17,1},{33,17},{49,33},{2,50}... | collective-permute-start | bytes 3145736 | tf_op jit(solution)/shard_map/ppermute | solution.py:15
  119.6 27.8 %collective-permute-start.12 = (f32[2,2,512,128]{3,2,1,0:T(8,128)S(1)}, f32[2,2,512,128]{3,2,1,0:T(8,128)}, u32[]{:S(2)}, u32[]{:S(2)}) collective-permute-start(f32[2,2,512,128]{3,2,1,0:T(8,128)S(1)} %get-tuple-element.7.refs_0_), channel_id=1, source_target_pairs={{0,16},{16,32},{32,48},{48,0},{1,17},{17,33},{33,49},{49,1},{2,18}... | collective-permute-start | bytes 3145736 | tf_op jit(solution)/shard_map/ppermute | solution.py:15
  122.1 46.4 %collective-permute-start.27 = (f32[2,2,512,128]{3,2,1,0:T(8,128)S(1)}, f32[2,2,512,128]{3,2,1,0:T(8,128)S(1)}, u32[]{:S(2)}, u32[]{:S(2)}) collective-permute-start(f32[2,2,512,128]{3,2,1,0:T(8,128)S(1)} %get-tuple-element.8.refs_0_), channel_id=1, source_target_pairs={{0,48},{16,0},{32,16},{48,32},{1,49},{17,1},{33,17},{49,33},{2,50}... | collective-permute-start | bytes 3145736 | tf_op jit(solution)/shard_map/ppermute | solution.py:15
  122.1 46.5 %collective-permute-start.28 = (f32[2,2,512,128]{3,2,1,0:T(8,128)S(1)}, f32[2,2,512,128]{3,2,1,0:T(8,128)}, u32[]{:S(2)}, u32[]{:S(2)}) collective-permute-start(f32[2,2,512,128]{3,2,1,0:T(8,128)S(1)} %get-tuple-element.8.refs_0_), channel_id=1, source_target_pairs={{0,16},{16,32},{32,48},{48,0},{1,17},{17,33},{33,49},{49,1},{2,18}... | collective-permute-start | bytes 3145736 | tf_op jit(solution)/shard_map/ppermute | solution.py:15
  147.2 32.5 %collective-permute-start.13 = (f32[2,512,128]{2,1,0:T(8,128)S(1)}, f32[2,512,128]{2,1,0:T(8,128)S(1)}, u32[]{:S(2)}, u32[]{:S(2)}) collective-permute-start(f32[2,512,128]{2,1,0:T(8,128)S(1)} %slice_bitcast_fusion.3), channel_id=1, source_target_pairs={{0,48},{16,0},{32,16},{48,32},{1,49},{17,1},{33,17},{49,33},{2,50}... | collective-permute-start | bytes 1572872 | tf_op jit(solution)/shard_map/ppermute | solution.py:15
  148.5 31.2 %collective-permute-start.14 = (f32[2,512,128]{2,1,0:T(8,128)S(1)}, f32[2,512,128]{2,1,0:T(8,128)S(1)}, u32[]{:S(2)}, u32[]{:S(2)}) collective-permute-start(f32[2,512,128]{2,1,0:T(8,128)S(1)} %slice_bitcast_fusion.2), channel_id=1, source_target_pairs={{0,16},{16,32},{32,48},{48,0},{1,17},{17,33},{33,49},{49,1},{2,18}... | collective-permute-start | bytes 1572872 | tf_op jit(solution)/shard_map/ppermute | solution.py:15
  168.5 22.0 %collective-permute-start.29 = (f32[2,512,128]{2,1,0:T(8,128)S(1)}, f32[2,512,128]{2,1,0:T(8,128)S(1)}, u32[]{:S(2)}, u32[]{:S(2)}) collective-permute-start(f32[2,512,128]{2,1,0:T(8,128)S(1)} %slice_bitcast_fusion.1), channel_id=1, source_target_pairs={{0,48},{16,0},{32,16},{48,32},{1,49},{17,1},{33,17},{49,33},{2,50}... | collective-permute-start | bytes 1572872 | tf_op jit(solution)/shard_map/ppermute | solution.py:15
  169.7 20.9 %collective-permute-start.30 = (f32[2,512,128]{2,1,0:T(8,128)S(1)}, f32[2,512,128]{2,1,0:T(8,128)S(1)}, u32[]{:S(2)}, u32[]{:S(2)}) collective-permute-start(f32[2,512,128]{2,1,0:T(8,128)S(1)} %slice_bitcast_fusion), channel_id=1, source_target_pairs={{0,16},{16,32},{32,48},{48,0},{1,17},{17,33},{33,49},{49,1},{2,18}... | collective-permute-start | bytes 1572872 | tf_op jit(solution)/shard_map/ppermute | solution.py:15
  174.8 25.4 %collective-permute-start.19 = (f32[2,2,256,256]{3,2,1,0:T(8,128)S(1)}, f32[2,2,256,256]{3,2,1,0:T(8,128)S(1)}, u32[]{:S(2)}, u32[]{:S(2)}) collective-permute-start(f32[2,2,256,256]{3,2,1,0:T(8,128)S(1)} %get-tuple-element.5), channel_id=1, source_target_pairs={{0,64},{64,0},{1,65},{65,1},{2,66},{66,2},{3,67},{67,3},{4,68},{68... | collective-permute-start | bytes 3145736 | tf_op jit(solution)/shard_map/ppermute | solution.py:15
  185.5 14.7 %collective-permute-start.15 = (f32[256,128]{1,0:T(8,128)S(1)}, f32[256,128]{1,0:T(8,128)S(1)}, u32[]{:S(2)}, u32[]{:S(2)}) collective-permute-start(f32[256,128]{1,0:T(8,128)S(1)} %get-tuple-element.19), channel_id=1, source_target_pairs={{0,2},{2,4},{4,6},{6,0},{1,3},{3,5},{5,7},{7,1},{8,10},{10,12},{12... | collective-permute-start | bytes 393224 | tf_op jit(solution)/shard_map/ppermute | solution.py:15
  188.1 12.1 %collective-permute-start.17 = (f32[256,128]{1,0:T(8,128)S(1)}, f32[256,128]{1,0:T(8,128)S(1)}, u32[]{:S(2)}, u32[]{:S(2)}) collective-permute-start(f32[256,128]{1,0:T(8,128)S(1)} %get-tuple-element.20), channel_id=1, source_target_pairs={{0,6},{2,0},{4,2},{6,4},{1,7},{3,1},{5,3},{7,5},{8,14},{10,8},{12,... | collective-permute-start | bytes 393224 | tf_op jit(solution)/shard_map/ppermute | solution.py:15
  200.3 29.0 %collective-permute-start.16 = (f32[2,256,128]{2,1,0:T(8,128)S(1)}, f32[2,256,128]{2,1,0:T(8,128)S(1)}, u32[]{:S(2)}, u32[]{:S(2)}) collective-permute-start(f32[2,256,128]{2,1,0:T(8,128)S(1)} %pad_maximum_fusion.5), channel_id=1, source_target_pairs={{0,2},{2,4},{4,6},{6,0},{1,3},{3,5},{5,7},{7,1},{8,10},{10,12},{12... | collective-permute-start | bytes 786440 | tf_op jit(solution)/shard_map/ppermute | solution.py:15
  202.9 26.6 %collective-permute-start.18 = (f32[2,256,128]{2,1,0:T(8,128)S(1)}, f32[2,256,128]{2,1,0:T(8,128)S(1)}, u32[]{:S(2)}, u32[]{:S(2)}) collective-permute-start(f32[2,256,128]{2,1,0:T(8,128)S(1)} %pad_maximum_fusion.6), channel_id=1, source_target_pairs={{0,6},{2,0},{4,2},{6,4},{1,7},{3,1},{5,3},{7,5},{8,14},{10,8},{12,... | collective-permute-start | bytes 786440 | tf_op jit(solution)/shard_map/ppermute | solution.py:15
  204.9 36.2 %collective-permute-start.32 = (f32[2,256,128]{2,1,0:T(8,128)S(1)}, f32[2,256,128]{2,1,0:T(8,128)S(1)}, u32[]{:S(2)}, u32[]{:S(2)}) collective-permute-start(f32[2,256,128]{2,1,0:T(8,128)S(1)} %pad_maximum_fusion.9), channel_id=1, source_target_pairs={{0,2},{2,4},{4,6},{6,0},{1,3},{3,5},{5,7},{7,1},{8,10},{10,12},{12... | collective-permute-start | bytes 786440 | tf_op jit(solution)/shard_map/ppermute | solution.py:15
  226.7 9.1 %collective-permute-start.22 = (f32[2,256,128]{2,1,0:T(8,128)S(1)}, f32[2,256,128]{2,1,0:T(8,128)S(1)}, u32[]{:S(2)}, u32[]{:S(2)}) collective-permute-start(f32[2,256,128]{2,1,0:T(8,128)S(1)} %pad_maximum_fusion.7), channel_id=1, source_target_pairs={{0,2},{2,4},{4,6},{6,0},{1,3},{3,5},{5,7},{7,1},{8,10},{10,12},{12... | collective-permute-start | bytes 786440 | tf_op jit(solution)/shard_map/ppermute | solution.py:15
  229.2 10.5 %collective-permute-start.24 = (f32[2,256,128]{2,1,0:T(8,128)S(1)}, f32[2,256,128]{2,1,0:T(8,128)S(1)}, u32[]{:S(2)}, u32[]{:S(2)}) collective-permute-start(f32[2,256,128]{2,1,0:T(8,128)S(1)} %pad_maximum_fusion.8), channel_id=1, source_target_pairs={{0,6},{2,0},{4,2},{6,4},{1,7},{3,1},{5,3},{7,5},{8,14},{10,8},{12,... | collective-permute-start | bytes 786440 | tf_op jit(solution)/shard_map/ppermute | solution.py:15
  229.3 15.7 %collective-permute-start.34 = (f32[2,256,128]{2,1,0:T(8,128)S(1)}, f32[2,256,128]{2,1,0:T(8,128)S(1)}, u32[]{:S(2)}, u32[]{:S(2)}) collective-permute-start(f32[2,256,128]{2,1,0:T(8,128)S(1)} %pad_maximum_fusion.10), channel_id=1, source_target_pairs={{0,6},{2,0},{4,2},{6,4},{1,7},{3,1},{5,3},{7,5},{8,14},{10,8},{12,... | collective-permute-start | bytes 786440 | tf_op jit(solution)/shard_map/ppermute | solution.py:15
  229.5 15.5 %collective-permute-start.36 = (f32[2,256,128]{2,1,0:T(8,128)S(1)}, f32[2,256,128]{2,1,0:T(8,128)S(1)}, u32[]{:S(2)}, u32[]{:S(2)}) collective-permute-start(f32[2,256,128]{2,1,0:T(8,128)S(1)} %pad_maximum_fusion.11), channel_id=1, source_target_pairs={{0,2},{2,4},{4,6},{6,0},{1,3},{3,5},{5,7},{7,1},{8,10},{10,12},{12... | collective-permute-start | bytes 786440 | tf_op jit(solution)/shard_map/ppermute | solution.py:15
  235.8 12.0 %collective-permute-start.38 = (f32[2,256,128]{2,1,0:T(8,128)S(1)}, f32[2,256,128]{2,1,0:T(8,128)S(1)}, u32[]{:S(2)}, u32[]{:S(2)}) collective-permute-start(f32[2,256,128]{2,1,0:T(8,128)S(1)} %pad_maximum_fusion.12), channel_id=1, source_target_pairs={{0,6},{2,0},{4,2},{6,4},{1,7},{3,1},{5,3},{7,5},{8,14},{10,8},{12,... | collective-permute-start | bytes 786440 | tf_op jit(solution)/shard_map/ppermute | solution.py:15
  239.8 9.5 %collective-permute-start.25 = (f32[2,256,128]{2,1,0:T(8,128)S(1)}, f32[2,256,128]{2,1,0:T(8,128)S(1)}, u32[]{:S(2)}, u32[]{:S(2)}) collective-permute-start(f32[2,256,128]{2,1,0:T(8,128)S(1)} %broadcast_select_fusion.1), channel_id=1, source_target_pairs={{0,8},{8,0},{1,9},{9,1},{2,10},{10,2},{3,11},{11,3},{4,12},{12,4},... | collective-permute-start | bytes 786440 | tf_op jit(solution)/shard_map/ppermute | solution.py:15
  249.3 11.0 %collective-permute-start.26 = (f32[2,256,128]{2,1,0:T(8,128)S(1)}, f32[2,256,128]{2,1,0:T(8,128)S(1)}, u32[]{:S(2)}, u32[]{:S(2)}) collective-permute-start(f32[2,256,128]{2,1,0:T(8,128)S(1)} %select_add_fusion.1), channel_id=1, source_target_pairs={{0,0},{8,64},{64,8},{72,72},{1,1},{9,65},{65,9},{73,73},{2,2},{10,... | collective-permute-start | bytes 786440 | tf_op jit(solution)/shard_map/ppermute | solution.py:177
  (13 other events, 124.1 us)
Sparse Core Ops, SparseCore 0:
  9.0 52.0 all-gather.1

commit v2 on v0

v2 whole, which is shorter than its diff:
```python
import functools

import jax
import jax.numpy as jnp
from jax import lax
from jax.experimental import pallas as pl
from jax.experimental.pallas import tpu as pltpu
from jax.sharding import Mesh, PartitionSpec as P

PARTS = {"zh": 2, "x": 4, "zl": 2, "y": 4, "core": 2}
F32 = jnp.float32
BF16 = jnp.bfloat16
COST = 0.02
MIXED_COST = 0.02
VMEM = 24 * 1024 * 1024
MIXED_VMEM = 40 * 1024 * 1024


def move(value, axis, step):
    n = PARTS[axis]
    return lax.ppermute(value, axis, [(i, (i + step) % n) for i in range(n)])


def split(value):
    high = value.astype(BF16)
    return high, (value - high.astype(F32)).astype(BF16)


def dot3(left, right, dims):
    (lh, ll), (rh, rl) = left, right

    def one(a, b):
        return lax.dot_general(a, b, (dims, ((), ())), preferred_element_type=F32)

    return one(lh, rh) + (one(lh, rl) + one(ll, rh))


def mixed_kernel(e_0, e_1, e_3, e_2low, e_2high, b_ref, out_ref, l_hi, l_lo):
    zh, x = lax.axis_index("zh"), lax.axis_index("x")
    depth = e_0.shape[2]

    @pl.when((pl.program_id(0) == 0) & (pl.program_id(1) == 0))
    def _():
        for far in range(2):
            for j in range(4):
                row = 4 * lax.rem(zh + far, 2) + lax.rem(x + j, 4)
                at = pl.ds(pl.multiple_of(row * depth, depth), depth)
                if j == 2:
                    ref, index = (e_2low, e_2high)[far], ()
                else:
                    ref, index = (e_0, e_1, None, e_3)[j], (far,)
                re, im = ref[(*index, 0)], ref[(*index, 1)]
                for part, block in enumerate((re, im, re + im)):
                    l_hi[part, at, :], l_lo[part, at, :] = split(block)

    dims = ((0,), (0,))
    l_re, l_im, l_sum = [(l_hi[part], l_lo[part]) for part in range(3)]
    re, im = [jnp.concatenate([b_ref[r, 0, part] for r in range(8)], axis=0) for part in range(2)]
    first, second = dot3(split(re), l_re, dims), dot3(split(im), l_im, dims)
    out_ref[0, 0] = first + second
    out_ref[0, 1] = dot3(split(re - im), l_sum, dims) - first + second


def update_kernel(own, other, *refs):
    x, y, zh = (lax.axis_index(name) for name in ("x", "y", "zh"))
    a_refs, (out_ref, m_hi, m_lo) = refs[:-3], refs[-3:]
    b, a = own.shape[2:]
    wide = a_refs[0].shape[-1]
    dims = ((1,), (0,))

    for level in range(2):
        for part in range(2):
            turned = other[level, part]
            turned = jnp.concatenate([turned[:, a // 2 :], turned[:, : a // 2]], axis=1)
            m_hi[level, part], m_lo[level, part] = split(own[level, part] + turned)

    def beside(p, q):
        return jnp.concatenate([p, q], axis=1)

    for j in range(4):
        sides = []
        for level in range(2):
            (rh, rl), (ih, il) = [
                split(jnp.concatenate([ref[level, part] for ref in a_refs[2 * j : 2 * j + 2]], axis=0))
                for part in range(2)
            ]
            sides.append(((beside(rh, ih), beside(rl, il)), (beside(-ih, rh), beside(-il, rl))))
        at = lax.rem(x + j + 4 - y, 4)
        for half_at in range(2):
            rows = slice(half_at * (b // 2), (half_at + 1) * (b // 2))
            total = None
            for level in range(2):
                for part in range(2):
                    left = m_hi[level, part, rows, :], m_lo[level, part, rows, :]
                    new = dot3(left, sides[level][part], dims)
                    total = new if total is None else total + new
            to = lax.rem(half_at + zh, 2)
            out_ref[at, to, 0] = total[:, :wide]
            out_ref[at, to, 1] = total[:, wide:]


def cost(flops, *values, scale=1):
    size = sum(v.dtype.itemsize * v.size for v in values)
    return pl.CostEstimate(flops=int(scale * flops), bytes_accessed=size, transcendentals=0)


def whole(n):
    return [pl.BlockSpec(memory_space=pltpu.VMEM)] * n


def mixed_partial(envs, sites):
    _, levels, _, depth, b = sites.shape
    a = envs[0].shape[-1]
    out = jax.ShapeDtypeStruct((levels, 2, 2 * b, a), F32)
    return pl.pallas_call(
        mixed_kernel,
        grid=(levels, 2),
        out_shape=out,
        in_specs=whole(len(envs))
        + [pl.BlockSpec((8, 1, 2, depth, b), lambda level, i: (i, level, 0, 0, 0))],
        out_specs=pl.BlockSpec((1, 2, b, a), lambda level, i: (level, 0, i, 0)),
        scratch_shapes=[pltpu.VMEM((3, 8 * depth, a), BF16)] * 2,
        compiler_params=pltpu.CompilerParams(vmem_limit_bytes=MIXED_VMEM),
        cost_estimate=cost(2 * 3 * 3 * levels * 8 * depth * 2 * b * a, out, sites, scale=MIXED_COST),
    )(*envs, sites)


def update_partial(shares, sites):
    levels, _, b, a = shares[0].shape
    c = sites[0].shape[-1]
    out = jax.ShapeDtypeStruct((4, 2, 2, b // 2, c), F32)
    operands = (*shares, *sites)
    return pl.pallas_call(
        update_kernel,
        out_shape=out,
        in_specs=whole(len(operands)),
        out_specs=pl.BlockSpec(memory_space=pltpu.VMEM),
        scratch_shapes=[pltpu.VMEM((levels, 2, b, a), BF16)] * 2,
        compiler_params=pltpu.CompilerParams(vmem_limit_bytes=VMEM),
        cost_estimate=cost(2 * 3 * 4 * levels * b * a * 4 * c, out, *operands, scale=COST),
    )(*operands)


def half(value, index, axis):
    size = value.shape[axis] // 2
    return lax.dynamic_slice_in_dim(value, index * size, size, axis)


def first_step(parts):
    return [move(parts[2, 0], "y", 1), move(parts[2, 1], "y", -1)]


def second_step(parts, came):
    up = move(jnp.stack([parts[1, 0] + came[0], parts[1, 1]]), "y", 1)
    down = move(jnp.stack([parts[3, 0], parts[3, 1] + came[1]]), "y", -1)
    return [up, down]


def to_place(mine, far, same):
    axes = ("zh", "zl")
    near = lax.ppermute(far, axes, [(1, 2), (2, 1)])
    got = lax.ppermute(jnp.where(same, far, mine), axes, [(0, 2), (1, 0), (2, 3), (3, 1)])
    return jnp.where(same, mine, near) + got


def local(environment, initial_site, compressed_site):
    zh, x, zl, y, core = (lax.axis_index(name) for name in PARTS)
    tie = lax.optimization_barrier

    comp = lax.all_gather(compressed_site, ("zh", "zl", "y"), axis=0)

    rows_other = move(half(environment, 1 - core, 1), "core", 1)
    env = jnp.concatenate([half(environment, core, 1), rows_other], axis=2)
    width = initial_site.shape[3] // 4
    cols_mine = half(initial_site, core, 3)
    cols_other = move(half(initial_site, 1 - core, 3), "core", 1)
    p_0, q_0 = [
        [v[..., i * width : (i + 1) * width] for v in (cols_mine, cols_other)] for i in range(2)
    ]

    env_far = move(env, "zh", 1)
    p_1 = [move(v, "x", -1) for v in p_0]
    p_3 = [move(v, "x", 1) for v in p_0]
    env, env_far, *more = tie((env, env_far, *p_1, *p_3, *q_0))
    p_1, p_3, q_0 = more[:2], more[2:4], more[4:]
    e_0 = jnp.stack([env, env_far])
    e_1 = move(e_0, "x", -1)
    e_3 = move(e_0, "x", 1)
    e_1, e_3, *more = tie((e_1, e_3, *p_1, *p_3))
    p_1, p_3 = more[:2], more[2:]
    e_2low = move(e_1[0], "x", -1)
    e_2high = move(e_3[1], "x", 1)
    p_2 = [move(p_1[0], "x", -1), move(p_3[1], "x", 1)]
    e_2low, e_2high, *more = tie((e_2low, e_2high, *p_2, *q_0))
    p_2, q_0 = more[:2], more[2:]
    q_own = [move(q_0[0], "x", -1), move(q_0[0], "x", 1)]

    share = mixed_partial([e_0, e_1, e_3, e_2low, e_2high], comp)
    share, *more = tie((share, *q_own, *q_0))
    q_own, q_0 = more[:2], more[2:]
    other = move(share, "core", 1)
    q_other = [move(q_0[1], "x", -1), move(q_0[1], "x", 1)]

    parts_0 = update_partial([share, other], [*p_0, *p_1, *p_2, *p_3])
    parts_0, *more = tie((parts_0, *q_own, *q_other))
    q_own, q_other = more[:2], more[2:]
    q_1, q_3 = zip(q_own, q_other)
    q_2 = [move(q_own[0], "x", -1), move(q_other[1], "x", 1)]
    came_0 = first_step(parts_0)
    *q_2, up, down = tie((*q_2, *came_0))
    came_0 = [up, down]
    came_0 = second_step(parts_0, came_0)
    parts_1 = update_partial([share, other], [*q_0, *q_1, *q_2, *q_3])
    came_1 = first_step(parts_1)
    parts_1, *came = tie((parts_1, *came_0, *came_1))
    came_0, came_1 = came[:2], came[2:]
    came_1 = second_step(parts_1, came_1)

    results = []
    for parts, came in ((parts_0, came_0), (parts_1, came_1)):
        mine, far = parts[0] + came[0] + came[1]
        results.append(to_place(mine, far, zl == zh))
    return jnp.concatenate(results, axis=2)


def solution(mesh):
    names = tuple(PARTS)
    parts = Mesh(mesh.devices.reshape(tuple(PARTS.values())), names)
    row, col = names[:2], names[2:]
    return jax.shard_map(
        local,
        mesh=parts,
        in_specs=(P(None, row, col), P(None, None, col, row), P(None, None, col, row)),
        out_specs=P(None, row, col),
        check_vma=False,
    )
```

time: 451 us -> 201 us (0.45)
  waiting for transfers between devices: 368 us -> 95.7 us
  matrix products: 54.6 us -> 0 us
  starting transfers between devices: 0.12 us -> 41.5 us
  Pallas kernels: 0 us -> 28.6 us
  local copies, waits for them, and re-layouts: 5.13 us -> 13.3 us
    all_gather x3 -> x1, waiting for transfers between devices: 297 us -> 0.01 us  [local(): comp = lax.all_gather(compressed_site, ('zh', 'zl', 'y'), axis=0)]
    ppermute x0 -> x32, waiting for transfers between devices: none -> 95 us  [the longest x28 82.5 us: move(): return lax.ppermute(value, axis, [(i, (i + step) % n) for i in range(n)])]
    reduce_scatter x1 -> x0, waiting for transfers between devices: 70.9 us -> none  [local(): lax.psum_scatter(partial_env, 'col', scatter_dimension=2, tiled=True)]
    dot_general x8 -> x0, matrix products: 54.6 us -> none  [contract(): jnp.einsum(form, left, right, precision=lax.Precision.HIGHEST, preferred_...]
    ppermute x0 -> x32, starting transfers between devices: none -> 41.5 us  [the longest x28 34.9 us: move(): return lax.ppermute(value, axis, [(i, (i + step) % n) for i in range(n)])]
    pallas_call x0 -> x3, Pallas kernels: none -> 28.6 us  [the longest x2 14.9 us: update_partial(): pl.pallas_call(update_kernel, out_shape=out, in_specs=whole(len(operands)...]
  transfers between devices with their start and end apart: 4 -> 33, of which waited for: 4 -> 19; matrix products, arithmetic and copies ran while one was open for 5% -> 5% of each run, Pallas kernels for 0% -> 14%
where the time goes in v2:
time: 201 us; the launch traced here: 198 us
  waiting for transfers between devices  95.7 us (48%)
  starting transfers between devices  41.5 us (21%)
  Pallas kernels  28.6 us (14%)
  between operations  13.8 us (7%)
  local copies, waits for them, and re-layouts  13.3 us (7%)
  other arithmetic  4.77 us (2%)
    ppermute x28, waiting for transfers between devices, move(): return lax.ppermute(value, axis, [(i, (i + step) % n) for i in range(n)])  82.5 us
    ppermute x28, starting transfers between devices, move(): return lax.ppermute(value, axis, [(i, (i + step) % n) for i in range(n)])  34.9 us
    pallas_call x2, Pallas kernels, update_partial(): pl.pallas_call(update_kernel, out_shape=out, in_specs=whole(len(operands)...  14.9 us
    pallas_call x1, Pallas kernels, mixed_partial(): pl.pallas_call(mixed_kernel, grid=(levels, 2), out_shape=out, in_specs=wh...  13.8 us
    ppermute x2, waiting for transfers between devices, to_place(): near = lax.ppermute(far, axes, [(1, 2), (2, 1)])  12.5 us
    ppermute x2, starting transfers between devices, to_place(): near = lax.ppermute(far, axes, [(1, 2), (2, 1)])  6.47 us
    unnamed x46, local copies, waits for them, and re-layouts  6.2 us
  transfers between devices with their start and end apart: 33, of which 19 were waited for; matrix products, arithmetic and copies ran while one was open for 5% of the time, Pallas kernels for 14%

profile of v2, /device:TPU:62, one launch (start us, length us, event | category | flops | bytes accessed | tf_op | source)
XLA Modules:
  0.0 197.8 jit_solution(1060506743276258615)
XLA Ops:
  8.7 1.8 constant_dynamic-slice_fusion.4
  14.9 3.1 %collective-permute-start.1 = (f32[2,128,512]{2,1,0:T(8,128)S(1)}, f32[2,128,512]{2,1,0:T(8,128)S(1)}, u32[]{:S(2)}, u32[]{:S(2)}) collective-permute-start(f32[2,128,512]{2,1,0:T(8,128)S(1)} %pad_maximum_fusion.1), channel_id=1, source_target_pairs={{0,64},{64,0},{1,65},{65,1},{2,66},{66,2},{3,67},{67,3},{4,68},{68... | collective-permute-start | bytes 1572872 | tf_op jit(solution)/shard_map/ppermute | solution.py:21
  18.0 2.1 %fusion.8 = (f32[2,2,256,128]{3,2,1,0:T(8,128)}, f32[2,2,256,128]{3,2,1,0:T(8,128)S(1)}) fusion(f32[2,2,256,256]{3,2,1,0:T(8,128)} %collective-permute-done.3), kind=kLoop, calls=%fused_computation.42 | loop fusion | bytes 2097152 | tf_op jit(solution)/shard_map/slice | solution.py:178
  20.1 1.7 collective-permute-start.6
  22.1 4.6 %collective-permute-done.5.refs_6_ = f32[2,2,256,128]{3,2,1,0:T(8,128)S(1)} collective-permute-done((f32[2,2,256,128]{3,2,1,0:T(8,128)S(1)}, f32[2,2,256,128]{3,2,1,0:T(8,128)S(1)}, u32[]{:S(2)}, u32[]{:S(2)}) %collective-permute-start.5) | collective-permute-done | bytes 524320 | tf_op jit(solution)/shard_map/ppermute | solution.py:21
  26.7 1.7 collective-permute-done.2.refs_2_
  28.4 8.2 %collective-permute-done.1 = f32[2,128,512]{2,1,0:T(8,128)S(1)} collective-permute-done((f32[2,128,512]{2,1,0:T(8,128)S(1)}, f32[2,128,512]{2,1,0:T(8,128)S(1)}, u32[]{:S(2)}, u32[]{:S(2)}) %collective-permute-start.1) | collective-permute-done | bytes 524320 | tf_op jit(solution)/shard_map/ppermute | solution.py:21
  41.4 22.0 %collective-permute-done.8.e_3 = f32[2,2,128,512]{3,2,1,0:T(8,128)S(1)} collective-permute-done((f32[2,2,128,512]{3,2,1,0:T(8,128)S(1)}, f32[2,2,128,512]{3,2,1,0:T(8,128)S(1)}, u32[]{:S(2)}, u32[]{:S(2)}) %collective-permute-start.8) | collective-permute-done | bytes 1048608 | tf_op jit(solution)/shard_map/ppermute | solution.py:21
  63.4 1.6 collective-permute-done.7.e_1
  65.4 1.8 collective-permute-start.9
  67.4 3.0 %collective-permute-start.12 = (f32[2,2,256,128]{3,2,1,0:T(8,128)S(1)}, f32[2,2,256,128]{3,2,1,0:T(8,128)S(1)}, u32[]{:S(2)}, u32[]{:S(2)}) collective-permute-start(f32[2,2,256,128]{3,2,1,0:T(8,128)S(1)} %collective-permute-done.6.refs_7_), channel_id=1, source_target_pairs={{0,16},{16,32},{32,48},{48,0},{1,17},{17,33},{33,49},{49,1},{2,18}... | collective-permute-start | bytes 1572872 | tf_op jit(solution)/shard_map/ppermute | solution.py:21
  70.5 9.5 %collective-permute-done.10.e_2high = f32[2,128,512]{2,1,0:T(8,128)S(1)} collective-permute-done((f32[2,128,512]{2,1,0:T(8,128)S(1)}, f32[2,128,512]{2,1,0:T(8,128)S(1)}, u32[]{:S(2)}, u32[]{:S(2)}) %collective-permute-start.10) | collective-permute-done | bytes 524320 | tf_op jit(solution)/shard_map/ppermute | solution.py:21
  82.4 7.4 %collective-permute-done.11.refs_4_ = f32[2,2,256,128]{3,2,1,0:T(8,128)S(1)} collective-permute-done((f32[2,2,256,128]{3,2,1,0:T(8,128)S(1)}, f32[2,2,256,128]{3,2,1,0:T(8,128)S(1)}, u32[]{:S(2)}, u32[]{:S(2)}) %collective-permute-start.11) | collective-permute-done | bytes 524320 | tf_op jit(solution)/shard_map/ppermute | solution.py:21
  91.4 2.0 %collective-permute-start.13 = (f32[2,2,256,128]{3,2,1,0:T(8,128)}, f32[2,2,256,128]{3,2,1,0:T(8,128)}, u32[]{:S(2)}, u32[]{:S(2)}) collective-permute-start(f32[2,2,256,128]{3,2,1,0:T(8,128)} %get-tuple-element.69.refs_0_), channel_id=1, source_target_pairs={{0,48},{16,0},{32,16},{48,32},{1,49},{17,1},{33,17},{49,33},{2,50}... | collective-permute-start | bytes 1572872 | tf_op jit(solution)/shard_map/ppermute | solution.py:21
  95.5 13.8 %shard_map.37.own = f32[2,2,512,512]{3,2,1,0:T(8,128)S(1)} custom-call(f32[2,2,128,512]{3,2,1,0:T(8,128)S(1)} %pad_maximum_fusion.e_0, f32[2,2,128,512]{3,2,1,0:T(8,128)S(1)} %collective-permute-done.7.e_1, f32[2,2,128,512]{3,2,1,0:T(8,128)S(1)} %collective-permute-done.8.e_3, f32[2,128,512]{2,1,0:T(8,128)S(1)} %copy-done.21, f32[2,128,512]{2,1,0:T(8,128)S(1)} %copy-done.19, ...), custom_call_target="tpu_custom_call" | custom-call | flops 193273536 | bytes 12582912 | tf_op jit(solution)/shard_map/pallas_call | solution.py:115
  111.5 5.0 %collective-permute-done.15.other = f32[2,2,512,512]{3,2,1,0:T(8,128)S(1)} collective-permute-done((f32[2,2,512,512]{3,2,1,0:T(8,128)S(1)}, f32[2,2,512,512]{3,2,1,0:T(8,128)S(1)}, u32[]{:S(2)}, u32[]{:S(2)}) %collective-permute-start.15) | collective-permute-done | bytes 4194336 | tf_op jit(solution)/shard_map/ppermute | solution.py:21
  116.6 6.8 %shard_map.38 = f32[4,2,2,256,128]{4,3,2,1,0:T(8,128)S(1)} custom-call(f32[2,2,512,512]{3,2,1,0:T(8,128)S(1)} %shard_map.37.own, f32[2,2,512,512]{3,2,1,0:T(8,128)S(1)} %collective-permute-done.15.other, f32[2,2,256,128]{3,2,1,0:T(8,128)S(1)} %copy-done.3, f32[2,2,256,128]{3,2,1,0:T(8,128)S(1)} %copy-done.5, f32[2,2,256,128]{3,2,1,0:T(8,128)S(1)} %copy-done.9, ...), custom_call_target="tpu_custom_call" | custom-call | flops 128849016 | bytes 14680064 | tf_op jit(solution)/shard_map/pallas_call | solution.py:133
  123.8 2.1 %collective-permute-done.16.refs_3_ = f32[2,2,256,128]{3,2,1,0:T(8,128)S(1)} collective-permute-done((f32[2,2,256,128]{3,2,1,0:T(8,128)S(1)}, f32[2,2,256,128]{3,2,1,0:T(8,128)S(1)}, u32[]{:S(2)}, u32[]{:S(2)}) %collective-permute-start.16) | collective-permute-done | bytes 524320 | tf_op jit(solution)/shard_map/ppermute | solution.py:21
  125.9 3.2 %collective-permute-start.19 = (f32[2,2,256,128]{3,2,1,0:T(8,128)S(1)}, f32[2,2,256,128]{3,2,1,0:T(8,128)S(1)}, u32[]{:S(2)}, u32[]{:S(2)}) collective-permute-start(f32[2,2,256,128]{3,2,1,0:T(8,128)S(1)} %collective-permute-done.17.refs_7_), channel_id=1, source_target_pairs={{0,16},{16,32},{32,48},{48,0},{1,17},{17,33},{33,49},{49,1},{2,18}... | collective-permute-start | bytes 1572872 | tf_op jit(solution)/shard_map/ppermute | solution.py:21
  129.7 2.8 %collective-permute-start.20 = (f32[2,256,128]{2,1,0:T(8,128)S(1)}, f32[2,256,128]{2,1,0:T(8,128)S(1)}, u32[]{:S(2)}, u32[]{:S(2)}) collective-permute-start(f32[2,256,128]{2,1,0:T(8,128)S(1)} %get-tuple-element.92), channel_id=1, source_target_pairs={{0,2},{2,4},{4,6},{6,0},{1,3},{3,5},{5,7},{7,1},{8,10},{10,12},{12... | collective-permute-start | bytes 786440 | tf_op jit(solution)/shard_map/ppermute | solution.py:21
  132.5 4.9 %collective-permute-done.21 = f32[2,256,128]{2,1,0:T(8,128)S(1)} collective-permute-done((f32[2,256,128]{2,1,0:T(8,128)S(1)}, f32[2,256,128]{2,1,0:T(8,128)S(1)}, u32[]{:S(2)}, u32[]{:S(2)}) %collective-permute-start.21) | collective-permute-done | bytes 262176 | tf_op jit(solution)/shard_map/ppermute | solution.py:21
  137.5 3.0 %collective-permute-done.18.refs_4_ = f32[2,2,256,128]{3,2,1,0:T(8,128)S(1)} collective-permute-done((f32[2,2,256,128]{3,2,1,0:T(8,128)}, f32[2,2,256,128]{3,2,1,0:T(8,128)S(1)}, u32[]{:S(2)}, u32[]{:S(2)}) %collective-permute-start.18) | collective-permute-done | bytes 524320 | tf_op jit(solution)/shard_map/ppermute | solution.py:21
  140.7 2.3 %collective-permute-start.23 = (f32[2,2,256,128]{3,2,1,0:T(8,128)S(1)}, f32[2,2,256,128]{3,2,1,0:T(8,128)}, u32[]{:S(2)}, u32[]{:S(2)}) collective-permute-start(f32[2,2,256,128]{3,2,1,0:T(8,128)S(1)} %pad_maximum_fusion.3), channel_id=1, source_target_pairs={{0,6},{2,0},{4,2},{6,4},{1,7},{3,1},{5,3},{7,5},{8,14},{10,8},{12,... | collective-permute-start | bytes 1572872 | tf_op jit(solution)/shard_map/ppermute | solution.py:21
  143.0 8.1 %shard_map.39 = f32[4,2,2,256,128]{4,3,2,1,0:T(8,128)S(1)} custom-call(f32[2,2,512,512]{3,2,1,0:T(8,128)S(1)} %shard_map.37.own, f32[2,2,512,512]{3,2,1,0:T(8,128)S(1)} %collective-permute-done.15.other, f32[2,2,256,128]{3,2,1,0:T(8,128)} %get-tuple-element.69.refs_0_, f32[2,2,256,128]{3,2,1,0:T(8,128)S(1)} %copy-done.1, ...), custom_call_target="tpu_custom_call" | custom-call | flops 128849016 | bytes 14680064 | tf_op jit(solution)/shard_map/pallas_call | solution.py:133
  152.4 2.8 %collective-permute-start.24 = (f32[2,256,128]{2,1,0:T(8,128)}, f32[2,256,128]{2,1,0:T(8,128)}, u32[]{:S(2)}, u32[]{:S(2)}) collective-permute-start(f32[2,256,128]{2,1,0:T(8,128)} %get-tuple-element.88), channel_id=1, source_target_pairs={{0,2},{2,4},{4,6},{6,0},{1,3},{3,5},{5,7},{7,1},{8,10},{10,12},{12... | collective-permute-start | bytes 786440 | tf_op jit(solution)/shard_map/ppermute | solution.py:21
  155.2 4.9 %collective-permute-done.25 = f32[2,256,128]{2,1,0:T(8,128)S(1)} collective-permute-done((f32[2,256,128]{2,1,0:T(8,128)}, f32[2,256,128]{2,1,0:T(8,128)S(1)}, u32[]{:S(2)}, u32[]{:S(2)}) %collective-permute-start.25) | collective-permute-done | bytes 262176 | tf_op jit(solution)/shard_map/ppermute | solution.py:21
  161.8 2.8 %collective-permute-start.28 = (f32[2,2,256,128]{3,2,1,0:T(8,128)S(1)}, f32[2,2,256,128]{3,2,1,0:T(8,128)S(1)}, u32[]{:S(2)}, u32[]{:S(2)}) collective-permute-start(f32[2,2,256,128]{3,2,1,0:T(8,128)S(1)} %pad_maximum_fusion.4), channel_id=1, source_target_pairs={{0,2},{2,4},{4,6},{6,0},{1,3},{3,5},{5,7},{7,1},{8,10},{10,12},{12... | collective-permute-start | bytes 1572872 | tf_op jit(solution)/shard_map/ppermute | solution.py:21
  166.1 3.1 %collective-permute-start.26 = (f32[2,256,128]{2,1,0:T(8,128)S(1)}, f32[2,256,128]{2,1,0:T(8,128)S(1)}, u32[]{:S(2)}, u32[]{:S(2)}) collective-permute-start(f32[2,256,128]{2,1,0:T(8,128)S(1)} %slice_bitcast_fusion.4), channel_id=1, source_target_pairs={{8,64},{64,8},{9,65},{65,9},{10,66},{66,10},{11,67},{67,11},{12,68... | collective-permute-start | bytes 786440 | tf_op jit(solution)/shard_map/ppermute | solution.py:161
  169.3 4.6 %collective-permute-done.29 = f32[2,2,256,128]{3,2,1,0:T(8,128)S(1)} collective-permute-done((f32[2,2,256,128]{3,2,1,0:T(8,128)S(1)}, f32[2,2,256,128]{3,2,1,0:T(8,128)S(1)}, u32[]{:S(2)}, u32[]{:S(2)}) %collective-permute-start.29) | collective-permute-done | bytes 524320 | tf_op jit(solution)/shard_map/ppermute | solution.py:21
  174.0 3.3 %collective-permute-start.30 = (f32[2,256,128]{2,1,0:T(8,128)S(1)}, f32[2,256,128]{2,1,0:T(8,128)S(1)}, u32[]{:S(2)}, u32[]{:S(2)}) collective-permute-start(f32[2,256,128]{2,1,0:T(8,128)S(1)} %slice_bitcast_fusion.2), channel_id=1, source_target_pairs={{8,64},{64,8},{9,65},{65,9},{10,66},{66,10},{11,67},{67,11},{12,68... | collective-permute-start | bytes 786440 | tf_op jit(solution)/shard_map/ppermute | solution.py:161
  177.5 8.4 %collective-permute-done.26 = f32[2,256,128]{2,1,0:T(8,128)S(1)} collective-permute-done((f32[2,256,128]{2,1,0:T(8,128)S(1)}, f32[2,256,128]{2,1,0:T(8,128)S(1)}, u32[]{:S(2)}, u32[]{:S(2)}) %collective-permute-start.26) | collective-permute-done | bytes 262176 | tf_op jit(solution)/shard_map/ppermute | solution.py:161
  185.9 4.1 %collective-permute-done.30 = f32[2,256,128]{2,1,0:T(8,128)S(1)} collective-permute-done((f32[2,256,128]{2,1,0:T(8,128)S(1)}, f32[2,256,128]{2,1,0:T(8,128)S(1)}, u32[]{:S(2)}, u32[]{:S(2)}) %collective-permute-start.30) | collective-permute-done | bytes 262176 | tf_op jit(solution)/shard_map/ppermute | solution.py:161
  (110 shorter events, 27.5 us)
Async XLA Ops:
  6.5 86.9 %all-gather.3.cloned.1.call-start = ((), (), s32[]{:S(2)}) async-start(), calls=%async_computation | async-start | bytes 8912896 | tf_op jit(solution)/shard_map/all_gather | solution.py:170
  8.6 9.4 %collective-permute-start.3 = (f32[2,2,256,256]{3,2,1,0:T(8,128)S(1)}, f32[2,2,256,256]{3,2,1,0:T(8,128)}, u32[]{:S(2)}, u32[]{:S(2)}) collective-permute-start(f32[2,2,256,256]{3,2,1,0:T(8,128)S(1)} %constant_dynamic-slice_fusion.1), channel_id=1, source_target_pairs={{0,1},{1,0},{2,3},{3,2},{4,5},{5,4},{6,7},{7,6},{8,9},{9,8},{10,11... | collective-permute-start | bytes 3145736 | tf_op jit(solution)/shard_map/ppermute | solution.py:21
  11.9 14.8 %collective-permute-start.5 = (f32[2,2,256,128]{3,2,1,0:T(8,128)S(1)}, f32[2,2,256,128]{3,2,1,0:T(8,128)S(1)}, u32[]{:S(2)}, u32[]{:S(2)}) collective-permute-start(f32[2,2,256,128]{3,2,1,0:T(8,128)S(1)} %get-tuple-element.96.refs_0_), channel_id=1, source_target_pairs={{0,16},{16,32},{32,48},{48,0},{1,17},{17,33},{33,49},{49,1},{2,18}... | collective-permute-start | bytes 1572872 | tf_op jit(solution)/shard_map/ppermute | solution.py:21
  12.4 16.0 %collective-permute-start.2 = (f32[2,2,256,128]{3,2,1,0:T(8,128)S(1)}, f32[2,2,256,128]{3,2,1,0:T(8,128)S(1)}, u32[]{:S(2)}, u32[]{:S(2)}) collective-permute-start(f32[2,2,256,128]{3,2,1,0:T(8,128)S(1)} %get-tuple-element.96.refs_0_), channel_id=1, source_target_pairs={{0,48},{16,0},{32,16},{48,32},{1,49},{17,1},{33,17},{49,33},{2,50}... | collective-permute-start | bytes 1572872 | tf_op jit(solution)/shard_map/ppermute | solution.py:21
  14.9 21.7 %collective-permute-start.1 = (f32[2,128,512]{2,1,0:T(8,128)S(1)}, f32[2,128,512]{2,1,0:T(8,128)S(1)}, u32[]{:S(2)}, u32[]{:S(2)}) collective-permute-start(f32[2,128,512]{2,1,0:T(8,128)S(1)} %pad_maximum_fusion.1), channel_id=1, source_target_pairs={{0,64},{64,0},{1,65},{65,1},{2,66},{66,2},{3,67},{67,3},{4,68},{68... | collective-permute-start | bytes 1572872 | tf_op jit(solution)/shard_map/ppermute | solution.py:21
  20.1 16.9 %collective-permute-start.6 = (f32[2,2,256,128]{3,2,1,0:T(8,128)S(1)}, f32[2,2,256,128]{3,2,1,0:T(8,128)S(1)}, u32[]{:S(2)}, u32[]{:S(2)}) collective-permute-start(f32[2,2,256,128]{3,2,1,0:T(8,128)S(1)} %get-tuple-element.98.refs_1_), channel_id=1, source_target_pairs={{0,16},{16,32},{32,48},{48,0},{1,17},{17,33},{33,49},{49,1},{2,18}... | collective-permute-start | bytes 1572872 | tf_op jit(solution)/shard_map/ppermute | solution.py:21
  21.7 16.7 %collective-permute-start.4 = (f32[2,2,256,128]{3,2,1,0:T(8,128)S(1)}, f32[2,2,256,128]{3,2,1,0:T(8,128)S(1)}, u32[]{:S(2)}, u32[]{:S(2)}) collective-permute-start(f32[2,2,256,128]{3,2,1,0:T(8,128)S(1)} %get-tuple-element.98.refs_1_), channel_id=1, source_target_pairs={{0,48},{16,0},{32,16},{48,32},{1,49},{17,1},{33,17},{49,33},{2,50}... | collective-permute-start | bytes 1572872 | tf_op jit(solution)/shard_map/ppermute | solution.py:21
  39.3 24.1 %collective-permute-start.8 = (f32[2,2,128,512]{3,2,1,0:T(8,128)S(1)}, f32[2,2,128,512]{3,2,1,0:T(8,128)S(1)}, u32[]{:S(2)}, u32[]{:S(2)}) collective-permute-start(f32[2,2,128,512]{3,2,1,0:T(8,128)S(1)} %pad_maximum_fusion.e_0), channel_id=1, source_target_pairs={{0,16},{16,32},{32,48},{48,0},{1,17},{17,33},{33,49},{49,1},{2,18}... | collective-permute-start | bytes 3145736 | tf_op jit(solution)/shard_map/ppermute | solution.py:21
  39.9 25.0 %collective-permute-start.7 = (f32[2,2,128,512]{3,2,1,0:T(8,128)S(1)}, f32[2,2,128,512]{3,2,1,0:T(8,128)S(1)}, u32[]{:S(2)}, u32[]{:S(2)}) collective-permute-start(f32[2,2,128,512]{3,2,1,0:T(8,128)S(1)} %pad_maximum_fusion.e_0), channel_id=1, source_target_pairs={{0,48},{16,0},{32,16},{48,32},{1,49},{17,1},{33,17},{49,33},{2,50}... | collective-permute-start | bytes 3145736 | tf_op jit(solution)/shard_map/ppermute | solution.py:21
  65.0 14.9 %collective-permute-start.10 = (f32[2,128,512]{2,1,0:T(8,128)S(1)}, f32[2,128,512]{2,1,0:T(8,128)S(1)}, u32[]{:S(2)}, u32[]{:S(2)}) collective-permute-start(f32[2,128,512]{2,1,0:T(8,128)S(1)} %slice_bitcast_fusion), channel_id=1, source_target_pairs={{0,16},{16,32},{32,48},{48,0},{1,17},{17,33},{33,49},{49,1},{2,18}... | collective-permute-start | bytes 1572872 | tf_op jit(solution)/shard_map/ppermute | solution.py:21
  65.4 16.1 %collective-permute-start.9 = (f32[2,128,512]{2,1,0:T(8,128)S(1)}, f32[2,128,512]{2,1,0:T(8,128)S(1)}, u32[]{:S(2)}, u32[]{:S(2)}) collective-permute-start(f32[2,128,512]{2,1,0:T(8,128)S(1)} %slice_bitcast_fusion.1), channel_id=1, source_target_pairs={{0,48},{16,0},{32,16},{48,32},{1,49},{17,1},{33,17},{49,33},{2,50}... | collective-permute-start | bytes 1572872 | tf_op jit(solution)/shard_map/ppermute | solution.py:21
  67.2 22.5 %collective-permute-start.11 = (f32[2,2,256,128]{3,2,1,0:T(8,128)S(1)}, f32[2,2,256,128]{3,2,1,0:T(8,128)S(1)}, u32[]{:S(2)}, u32[]{:S(2)}) collective-permute-start(f32[2,2,256,128]{3,2,1,0:T(8,128)S(1)} %collective-permute-done.2.refs_2_), channel_id=1, source_target_pairs={{0,48},{16,0},{32,16},{48,32},{1,49},{17,1},{33,17},{49,33},{2,50}... | collective-permute-start | bytes 1572872 | tf_op jit(solution)/shard_map/ppermute | solution.py:21
  67.4 23.1 %collective-permute-start.12 = (f32[2,2,256,128]{3,2,1,0:T(8,128)S(1)}, f32[2,2,256,128]{3,2,1,0:T(8,128)S(1)}, u32[]{:S(2)}, u32[]{:S(2)}) collective-permute-start(f32[2,2,256,128]{3,2,1,0:T(8,128)S(1)} %collective-permute-done.6.refs_7_), channel_id=1, source_target_pairs={{0,16},{16,32},{32,48},{48,0},{1,17},{17,33},{33,49},{49,1},{2,18}... | collective-permute-start | bytes 1572872 | tf_op jit(solution)/shard_map/ppermute | solution.py:21
  91.4 18.0 %collective-permute-start.14 = (f32[2,2,256,128]{3,2,1,0:T(8,128)}, f32[2,2,256,128]{3,2,1,0:T(8,128)}, u32[]{:S(2)}, u32[]{:S(2)}) collective-permute-start(f32[2,2,256,128]{3,2,1,0:T(8,128)} %get-tuple-element.69.refs_0_), channel_id=1, source_target_pairs={{0,16},{16,32},{32,48},{48,0},{1,17},{17,33},{33,49},{49,1},{2,18}... | collective-permute-start | bytes 1572872 | tf_op jit(solution)/shard_map/ppermute | solution.py:21
  91.4 18.0 %collective-permute-start.13 = (f32[2,2,256,128]{3,2,1,0:T(8,128)}, f32[2,2,256,128]{3,2,1,0:T(8,128)}, u32[]{:S(2)}, u32[]{:S(2)}) collective-permute-start(f32[2,2,256,128]{3,2,1,0:T(8,128)} %get-tuple-element.69.refs_0_), channel_id=1, source_target_pairs={{0,48},{16,0},{32,16},{48,32},{1,49},{17,1},{33,17},{49,33},{2,50}... | collective-permute-start | bytes 1572872 | tf_op jit(solution)/shard_map/ppermute | solution.py:21
  109.3 7.2 %collective-permute-start.15 = (f32[2,2,512,512]{3,2,1,0:T(8,128)S(1)}, f32[2,2,512,512]{3,2,1,0:T(8,128)S(1)}, u32[]{:S(2)}, u32[]{:S(2)}) collective-permute-start(f32[2,2,512,512]{3,2,1,0:T(8,128)S(1)} %shard_map.37.own), channel_id=1, source_target_pairs={{0,1},{1,0},{2,3},{3,2},{4,5},{5,4},{6,7},{7,6},{8,9},{9,8},{10,11... | collective-permute-start | bytes 12582920 | tf_op jit(solution)/shard_map/ppermute | solution.py:21
  109.4 14.3 %collective-permute-start.17 = (f32[2,2,256,128]{3,2,1,0:T(8,128)S(1)}, f32[2,2,256,128]{3,2,1,0:T(8,128)S(1)}, u32[]{:S(2)}, u32[]{:S(2)}) collective-permute-start(f32[2,2,256,128]{3,2,1,0:T(8,128)S(1)} %copy-done.1), channel_id=1, source_target_pairs={{0,16},{16,32},{32,48},{48,0},{1,17},{17,33},{33,49},{49,1},{2,18}... | collective-permute-start | bytes 1572872 | tf_op jit(solution)/shard_map/ppermute | solution.py:21
  110.7 15.2 %collective-permute-start.16 = (f32[2,2,256,128]{3,2,1,0:T(8,128)S(1)}, f32[2,2,256,128]{3,2,1,0:T(8,128)S(1)}, u32[]{:S(2)}, u32[]{:S(2)}) collective-permute-start(f32[2,2,256,128]{3,2,1,0:T(8,128)S(1)} %copy-done.1), channel_id=1, source_target_pairs={{0,48},{16,0},{32,16},{48,32},{1,49},{17,1},{33,17},{49,33},{2,50}... | collective-permute-start | bytes 1572872 | tf_op jit(solution)/shard_map/ppermute | solution.py:21
  125.9 14.6 %collective-permute-start.18 = (f32[2,2,256,128]{3,2,1,0:T(8,128)}, f32[2,2,256,128]{3,2,1,0:T(8,128)S(1)}, u32[]{:S(2)}, u32[]{:S(2)}) collective-permute-start(f32[2,2,256,128]{3,2,1,0:T(8,128)} %collective-permute-done.13.refs_2_), channel_id=1, source_target_pairs={{0,48},{16,0},{32,16},{48,32},{1,49},{17,1},{33,17},{49,33},{2,50}... | collective-permute-start | bytes 1572872 | tf_op jit(solution)/shard_map/ppermute | solution.py:21
  125.9 14.6 %collective-permute-start.19 = (f32[2,2,256,128]{3,2,1,0:T(8,128)S(1)}, f32[2,2,256,128]{3,2,1,0:T(8,128)S(1)}, u32[]{:S(2)}, u32[]{:S(2)}) collective-permute-start(f32[2,2,256,128]{3,2,1,0:T(8,128)S(1)} %collective-permute-done.17.refs_7_), channel_id=1, source_target_pairs={{0,16},{16,32},{32,48},{48,0},{1,17},{17,33},{33,49},{49,1},{2,18}... | collective-permute-start | bytes 1572872 | tf_op jit(solution)/shard_map/ppermute | solution.py:21
  129.2 8.3 %collective-permute-start.21 = (f32[2,256,128]{2,1,0:T(8,128)S(1)}, f32[2,256,128]{2,1,0:T(8,128)S(1)}, u32[]{:S(2)}, u32[]{:S(2)}) collective-permute-start(f32[2,256,128]{2,1,0:T(8,128)S(1)} %get-tuple-element.91), channel_id=1, source_target_pairs={{0,6},{2,0},{4,2},{6,4},{1,7},{3,1},{5,3},{7,5},{8,14},{10,8},{12,... | collective-permute-start | bytes 786440 | tf_op jit(solution)/shard_map/ppermute | solution.py:21
  129.7 7.8 %collective-permute-start.20 = (f32[2,256,128]{2,1,0:T(8,128)S(1)}, f32[2,256,128]{2,1,0:T(8,128)S(1)}, u32[]{:S(2)}, u32[]{:S(2)}) collective-permute-start(f32[2,256,128]{2,1,0:T(8,128)S(1)} %get-tuple-element.92), channel_id=1, source_target_pairs={{0,2},{2,4},{4,6},{6,0},{1,3},{3,5},{5,7},{7,1},{8,10},{10,12},{12... | collective-permute-start | bytes 786440 | tf_op jit(solution)/shard_map/ppermute | solution.py:21
  140.6 19.5 %collective-permute-start.22 = (f32[2,2,256,128]{3,2,1,0:T(8,128)S(1)}, f32[2,2,256,128]{3,2,1,0:T(8,128)}, u32[]{:S(2)}, u32[]{:S(2)}) collective-permute-start(f32[2,2,256,128]{3,2,1,0:T(8,128)S(1)} %pad_maximum_fusion.2), channel_id=1, source_target_pairs={{0,2},{2,4},{4,6},{6,0},{1,3},{3,5},{5,7},{7,1},{8,10},{10,12},{12... | collective-permute-start | bytes 1572872 | tf_op jit(solution)/shard_map/ppermute | solution.py:21
  140.7 19.4 %collective-permute-start.23 = (f32[2,2,256,128]{3,2,1,0:T(8,128)S(1)}, f32[2,2,256,128]{3,2,1,0:T(8,128)}, u32[]{:S(2)}, u32[]{:S(2)}) collective-permute-start(f32[2,2,256,128]{3,2,1,0:T(8,128)S(1)} %pad_maximum_fusion.3), channel_id=1, source_target_pairs={{0,6},{2,0},{4,2},{6,4},{1,7},{3,1},{5,3},{7,5},{8,14},{10,8},{12,... | collective-permute-start | bytes 1572872 | tf_op jit(solution)/shard_map/ppermute | solution.py:21
  152.0 8.1 %collective-permute-start.25 = (f32[2,256,128]{2,1,0:T(8,128)}, f32[2,256,128]{2,1,0:T(8,128)S(1)}, u32[]{:S(2)}, u32[]{:S(2)}) collective-permute-start(f32[2,256,128]{2,1,0:T(8,128)} %get-tuple-element.87), channel_id=1, source_target_pairs={{0,6},{2,0},{4,2},{6,4},{1,7},{3,1},{5,3},{7,5},{8,14},{10,8},{12,... | collective-permute-start | bytes 786440 | tf_op jit(solution)/shard_map/ppermute | solution.py:21
  152.4 7.7 %collective-permute-start.24 = (f32[2,256,128]{2,1,0:T(8,128)}, f32[2,256,128]{2,1,0:T(8,128)}, u32[]{:S(2)}, u32[]{:S(2)}) collective-permute-start(f32[2,256,128]{2,1,0:T(8,128)} %get-tuple-element.88), channel_id=1, source_target_pairs={{0,2},{2,4},{4,6},{6,0},{1,3},{3,5},{5,7},{7,1},{8,10},{10,12},{12... | collective-permute-start | bytes 786440 | tf_op jit(solution)/shard_map/ppermute | solution.py:21
  161.2 12.7 %collective-permute-start.29 = (f32[2,2,256,128]{3,2,1,0:T(8,128)S(1)}, f32[2,2,256,128]{3,2,1,0:T(8,128)S(1)}, u32[]{:S(2)}, u32[]{:S(2)}) collective-permute-start(f32[2,2,256,128]{3,2,1,0:T(8,128)S(1)} %pad_maximum_fusion.5), channel_id=1, source_target_pairs={{0,6},{2,0},{4,2},{6,4},{1,7},{3,1},{5,3},{7,5},{8,14},{10,8},{12,... | collective-permute-start | bytes 1572872 | tf_op jit(solution)/shard_map/ppermute | solution.py:21
  161.8 12.1 %collective-permute-start.28 = (f32[2,2,256,128]{3,2,1,0:T(8,128)S(1)}, f32[2,2,256,128]{3,2,1,0:T(8,128)S(1)}, u32[]{:S(2)}, u32[]{:S(2)}) collective-permute-start(f32[2,2,256,128]{3,2,1,0:T(8,128)S(1)} %pad_maximum_fusion.4), channel_id=1, source_target_pairs={{0,2},{2,4},{4,6},{6,0},{1,3},{3,5},{5,7},{7,1},{8,10},{10,12},{12... | collective-permute-start | bytes 1572872 | tf_op jit(solution)/shard_map/ppermute | solution.py:21
  166.1 19.8 %collective-permute-start.26 = (f32[2,256,128]{2,1,0:T(8,128)S(1)}, f32[2,256,128]{2,1,0:T(8,128)S(1)}, u32[]{:S(2)}, u32[]{:S(2)}) collective-permute-start(f32[2,256,128]{2,1,0:T(8,128)S(1)} %slice_bitcast_fusion.4), channel_id=1, source_target_pairs={{8,64},{64,8},{9,65},{65,9},{10,66},{66,10},{11,67},{67,11},{12,68... | collective-permute-start | bytes 786440 | tf_op jit(solution)/shard_map/ppermute | solution.py:161
  169.2 16.6 %collective-permute-start.27 = (f32[2,256,128]{2,1,0:T(8,128)S(1)}, f32[2,256,128]{2,1,0:T(8,128)S(1)}, u32[]{:S(2)}, u32[]{:S(2)}) collective-permute-start(f32[2,256,128]{2,1,0:T(8,128)S(1)} %fusion.6), channel_id=1, source_target_pairs={{0,64},{8,0},{64,72},{72,8},{1,65},{9,1},{65,73},{73,9},{2,66},{10... | collective-permute-start | bytes 786440 | tf_op jit(solution)/shard_map/ppermute | solution.py:162
  174.0 16.0 %collective-permute-start.30 = (f32[2,256,128]{2,1,0:T(8,128)S(1)}, f32[2,256,128]{2,1,0:T(8,128)S(1)}, u32[]{:S(2)}, u32[]{:S(2)}) collective-permute-start(f32[2,256,128]{2,1,0:T(8,128)S(1)} %slice_bitcast_fusion.2), channel_id=1, source_target_pairs={{8,64},{64,8},{9,65},{65,9},{10,66},{66,10},{11,67},{67,11},{12,68... | collective-permute-start | bytes 786440 | tf_op jit(solution)/shard_map/ppermute | solution.py:161
  177.4 12.7 %collective-permute-start.31 = (f32[2,256,128]{2,1,0:T(8,128)S(1)}, f32[2,256,128]{2,1,0:T(8,128)S(1)}, u32[]{:S(2)}, u32[]{:S(2)}) collective-permute-start(f32[2,256,128]{2,1,0:T(8,128)S(1)} %fusion.7), channel_id=1, source_target_pairs={{0,64},{8,0},{64,72},{72,8},{1,65},{9,1},{65,73},{73,9},{2,66},{10... | collective-permute-start | bytes 786440 | tf_op jit(solution)/shard_map/ppermute | solution.py:162
  (24 other events, 394.7 us)
Sparse Core Ops, SparseCore 0:
  9.5 74.9 all-gather.2

commit v3 on v2

--- a/solution.py
+++ b/solution.py
@@ -191,24 +191,20 @@
     e_2low = move(e_1[0], "x", -1)
     e_2high = move(e_3[1], "x", 1)
     p_2 = [move(p_1[0], "x", -1), move(p_3[1], "x", 1)]
-    e_2low, e_2high, *more = tie((e_2low, e_2high, *p_2, *q_0))
-    p_2, q_0 = more[:2], more[2:]
+    e_2low, e_2high, *q_0 = tie((e_2low, e_2high, *q_0))
     q_own = [move(q_0[0], "x", -1), move(q_0[0], "x", 1)]
 
     share = mixed_partial([e_0, e_1, e_3, e_2low, e_2high], comp)
-    share, *more = tie((share, *q_own, *q_0))
-    q_own, q_0 = more[:2], more[2:]
+    share, *more = tie((share, *p_2, *q_own, *q_0))
+    p_2, q_own, q_0 = more[:2], more[2:4], more[4:]
     other = move(share, "core", 1)
     q_other = [move(q_0[1], "x", -1), move(q_0[1], "x", 1)]
 
     parts_0 = update_partial([share, other], [*p_0, *p_1, *p_2, *p_3])
-    parts_0, *more = tie((parts_0, *q_own, *q_other))
-    q_own, q_other = more[:2], more[2:]
+    came_0 = first_step(parts_0)
+    *q_own, q_other[0], q_other[1], parts_0 = tie((*q_own, *q_other, parts_0))
     q_1, q_3 = zip(q_own, q_other)
     q_2 = [move(q_own[0], "x", -1), move(q_other[1], "x", 1)]
-    came_0 = first_step(parts_0)
-    *q_2, up, down = tie((*q_2, *came_0))
-    came_0 = [up, down]
     came_0 = second_step(parts_0, came_0)
     parts_1 = update_partial([share, other], [*q_0, *q_1, *q_2, *q_3])
     came_1 = first_step(parts_1)

time: 201 us -> 193 us (0.960)
  waiting for transfers between devices: 95.7 us -> 87.3 us
    ppermute x28, waiting for transfers between devices: 82.5 us -> 73.6 us  [move(): return lax.ppermute(value, axis, [(i, (i + step) % n) for i in range(n)])]
    unnamed x46 -> x30, local copies, waits for them, and re-layouts: 6.2 us -> 4.53 us
  transfers between devices with their start and end apart: 33 -> 33, of which waited for: 19 -> 18; matrix products, arithmetic and copies ran while one was open for 5% -> 5% of each run, Pallas kernels for 14% -> 16%
where the time goes in v3:
time: 193 us; the launch traced here: 190 us
  waiting for transfers between devices  87.3 us (45%)
  starting transfers between devices  42.1 us (22%)
  Pallas kernels  30.2 us (16%)
  between operations  13.7 us (7%)
  local copies, waits for them, and re-layouts  11.7 us (6%)
  other arithmetic  4.77 us (2%)
    ppermute x28, waiting for transfers between devices, move(): return lax.ppermute(value, axis, [(i, (i + step) % n) for i in range(n)])  73.6 us
    ppermute x28, starting transfers between devices, move(): return lax.ppermute(value, axis, [(i, (i + step) % n) for i in range(n)])  35.6 us
    pallas_call x2, Pallas kernels, update_partial(): pl.pallas_call(update_kernel, out_shape=out, in_specs=whole(len(operands)...  16.4 us
    pallas_call x1, Pallas kernels, mixed_partial(): pl.pallas_call(mixed_kernel, grid=(levels, 2), out_shape=out, in_specs=wh...  13.8 us
    ppermute x2, waiting for transfers between devices, to_place(): near = lax.ppermute(far, axes, [(1, 2), (2, 1)])  12.7 us
    ppermute x2, starting transfers between devices, to_place(): near = lax.ppermute(far, axes, [(1, 2), (2, 1)])  6.33 us
    unnamed x30, local copies, waits for them, and re-layouts  4.53 us
  transfers between devices with their start and end apart: 33, of which 18 were waited for; matrix products, arithmetic and copies ran while one was open for 5% of the time, Pallas kernels for 16%

profile of v3, /device:TPU:62, one launch (start us, length us, event | category | flops | bytes accessed | tf_op | source)
XLA Modules:
  0.0 189.7 jit_solution(15607843474306956019)
XLA Ops:
  8.7 1.8 constant_dynamic-slice_fusion.4
  12.4 1.5 collective-permute-start.2
  15.0 3.1 %collective-permute-start.1 = (f32[2,128,512]{2,1,0:T(8,128)S(1)}, f32[2,128,512]{2,1,0:T(8,128)S(1)}, u32[]{:S(2)}, u32[]{:S(2)}) collective-permute-start(f32[2,128,512]{2,1,0:T(8,128)S(1)} %pad_maximum_fusion.1), channel_id=1, source_target_pairs={{0,64},{64,0},{1,65},{65,1},{2,66},{66,2},{3,67},{67,3},{4,68},{68... | collective-permute-start | bytes 1572872 | tf_op jit(solution)/shard_map/ppermute | solution.py:21
  18.0 2.1 %fusion.8 = (f32[2,2,256,128]{3,2,1,0:T(8,128)}, f32[2,2,256,128]{3,2,1,0:T(8,128)S(1)}) fusion(f32[2,2,256,256]{3,2,1,0:T(8,128)} %collective-permute-done.3), kind=kLoop, calls=%fused_computation.42 | loop fusion | bytes 2097152 | tf_op jit(solution)/shard_map/slice | solution.py:178
  20.1 1.7 collective-permute-start.6
  22.1 4.6 %collective-permute-done.5.refs_6_ = f32[2,2,256,128]{3,2,1,0:T(8,128)S(1)} collective-permute-done((f32[2,2,256,128]{3,2,1,0:T(8,128)S(1)}, f32[2,2,256,128]{3,2,1,0:T(8,128)S(1)}, u32[]{:S(2)}, u32[]{:S(2)}) %collective-permute-start.5) | collective-permute-done | bytes 524320 | tf_op jit(solution)/shard_map/ppermute | solution.py:21
  26.7 1.8 collective-permute-done.2.refs_2_
  28.5 8.1 %collective-permute-done.1 = f32[2,128,512]{2,1,0:T(8,128)S(1)} collective-permute-done((f32[2,128,512]{2,1,0:T(8,128)S(1)}, f32[2,128,512]{2,1,0:T(8,128)S(1)}, u32[]{:S(2)}, u32[]{:S(2)}) %collective-permute-start.1) | collective-permute-done | bytes 524320 | tf_op jit(solution)/shard_map/ppermute | solution.py:21
  39.9 1.5 collective-permute-start.7
  41.4 22.0 %collective-permute-done.8.e_3 = f32[2,2,128,512]{3,2,1,0:T(8,128)S(1)} collective-permute-done((f32[2,2,128,512]{3,2,1,0:T(8,128)S(1)}, f32[2,2,128,512]{3,2,1,0:T(8,128)S(1)}, u32[]{:S(2)}, u32[]{:S(2)}) %collective-permute-start.8) | collective-permute-done | bytes 1048608 | tf_op jit(solution)/shard_map/ppermute | solution.py:21
  63.4 1.5 collective-permute-done.7.e_1
  65.4 1.7 collective-permute-start.9
  67.4 3.0 %collective-permute-start.12 = (f32[2,2,256,128]{3,2,1,0:T(8,128)}, f32[2,2,256,128]{3,2,1,0:T(8,128)}, u32[]{:S(2)}, u32[]{:S(2)}) collective-permute-start(f32[2,2,256,128]{3,2,1,0:T(8,128)} %collective-permute-done.6.refs_7_), channel_id=1, source_target_pairs={{0,16},{16,32},{32,48},{48,0},{1,17},{17,33},{33,49},{49,1},{2,18}... | collective-permute-start | bytes 1572872 | tf_op jit(solution)/shard_map/ppermute | solution.py:21
  70.4 9.6 %collective-permute-done.10.e_2high = f32[2,128,512]{2,1,0:T(8,128)S(1)} collective-permute-done((f32[2,128,512]{2,1,0:T(8,128)S(1)}, f32[2,128,512]{2,1,0:T(8,128)S(1)}, u32[]{:S(2)}, u32[]{:S(2)}) %collective-permute-start.10) | collective-permute-done | bytes 524320 | tf_op jit(solution)/shard_map/ppermute | solution.py:21
  86.7 13.8 %shard_map.37.own = f32[2,2,512,512]{3,2,1,0:T(8,128)S(1)} custom-call(f32[2,2,128,512]{3,2,1,0:T(8,128)S(1)} %pad_maximum_fusion.e_0, f32[2,2,128,512]{3,2,1,0:T(8,128)S(1)} %collective-permute-done.7.e_1, f32[2,2,128,512]{3,2,1,0:T(8,128)S(1)} %collective-permute-done.8.e_3, f32[2,128,512]{2,1,0:T(8,128)S(1)} %copy-done.13, f32[2,128,512]{2,1,0:T(8,128)S(1)} %copy-done.11, ...), custom_call_target="tpu_custom_call" | custom-call | flops 193273536 | bytes 12582912 | tf_op jit(solution)/shard_map/pallas_call | solution.py:115
  101.0 1.4 collective-permute-start.16
  103.0 5.1 %collective-permute-done.17.other = f32[2,2,512,512]{3,2,1,0:T(8,128)S(1)} collective-permute-done((f32[2,2,512,512]{3,2,1,0:T(8,128)S(1)}, f32[2,2,512,512]{3,2,1,0:T(8,128)S(1)}, u32[]{:S(2)}, u32[]{:S(2)}) %collective-permute-start.17) | collective-permute-done | bytes 4194336 | tf_op jit(solution)/shard_map/ppermute | solution.py:21
  108.1 8.3 %shard_map.38 = f32[4,2,2,256,128]{4,3,2,1,0:T(8,128)S(1)} custom-call(f32[2,2,512,512]{3,2,1,0:T(8,128)S(1)} %shard_map.37.own, f32[2,2,512,512]{3,2,1,0:T(8,128)S(1)} %collective-permute-done.17.other, f32[2,2,256,128]{3,2,1,0:T(8,128)S(1)} %copy-done.3, f32[2,2,256,128]{3,2,1,0:T(8,128)S(1)} %copy-done.5, ...), custom_call_target="tpu_custom_call" | custom-call | flops 128849016 | bytes 14680064 | tf_op jit(solution)/shard_map/pallas_call | solution.py:133
  117.2 2.6 %collective-permute-start.20 = (f32[2,256,128]{2,1,0:T(8,128)S(1)}, f32[2,256,128]{2,1,0:T(8,128)S(1)}, u32[]{:S(2)}, u32[]{:S(2)}) collective-permute-start(f32[2,256,128]{2,1,0:T(8,128)S(1)} %get-tuple-element.86), channel_id=1, source_target_pairs={{0,2},{2,4},{4,6},{6,0},{1,3},{3,5},{5,7},{7,1},{8,10},{10,12},{12... | collective-permute-start | bytes 786440 | tf_op jit(solution)/shard_map/ppermute | solution.py:21
  120.3 2.8 %collective-permute-start.19 = (f32[2,2,256,128]{3,2,1,0:T(8,128)S(1)}, f32[2,2,256,128]{3,2,1,0:T(8,128)S(1)}, u32[]{:S(2)}, u32[]{:S(2)}) collective-permute-start(f32[2,2,256,128]{3,2,1,0:T(8,128)S(1)} %collective-permute-done.16.refs_7_), channel_id=1, source_target_pairs={{0,16},{16,32},{32,48},{48,0},{1,17},{17,33},{33,49},{49,1},{2,18}... | collective-permute-start | bytes 1572872 | tf_op jit(solution)/shard_map/ppermute | solution.py:21
  123.1 3.0 %collective-permute-done.22 = f32[2,256,128]{2,1,0:T(8,128)S(1)} collective-permute-done((f32[2,256,128]{2,1,0:T(8,128)S(1)}, f32[2,256,128]{2,1,0:T(8,128)S(1)}, u32[]{:S(2)}, u32[]{:S(2)}) %collective-permute-start.22) | collective-permute-done | bytes 262176 | tf_op jit(solution)/shard_map/ppermute | solution.py:21
  126.2 3.0 %collective-permute-start.21 = (f32[2,2,256,128]{3,2,1,0:T(8,128)S(1)}, f32[2,2,256,128]{3,2,1,0:T(8,128)}, u32[]{:S(2)}, u32[]{:S(2)}) collective-permute-start(f32[2,2,256,128]{3,2,1,0:T(8,128)S(1)} %pad_maximum_fusion.2), channel_id=1, source_target_pairs={{0,2},{2,4},{4,6},{6,0},{1,3},{3,5},{5,7},{7,1},{8,10},{10,12},{12... | collective-permute-start | bytes 1572872 | tf_op jit(solution)/shard_map/ppermute | solution.py:21
  129.6 5.0 %collective-permute-done.18.refs_4_ = f32[2,2,256,128]{3,2,1,0:T(8,128)S(1)} collective-permute-done((f32[2,2,256,128]{3,2,1,0:T(8,128)}, f32[2,2,256,128]{3,2,1,0:T(8,128)S(1)}, u32[]{:S(2)}, u32[]{:S(2)}) %collective-permute-start.18) | collective-permute-done | bytes 524320 | tf_op jit(solution)/shard_map/ppermute | solution.py:21
  134.6 8.1 %shard_map.39 = f32[4,2,2,256,128]{4,3,2,1,0:T(8,128)S(1)} custom-call(f32[2,2,512,512]{3,2,1,0:T(8,128)S(1)} %shard_map.37.own, f32[2,2,512,512]{3,2,1,0:T(8,128)S(1)} %collective-permute-done.17.other, f32[2,2,256,128]{3,2,1,0:T(8,128)} %get-tuple-element.65.refs_0_, f32[2,2,256,128]{3,2,1,0:T(8,128)S(1)} %copy-done.1, ...), custom_call_target="tpu_custom_call" | custom-call | flops 128849016 | bytes 14680064 | tf_op jit(solution)/shard_map/pallas_call | solution.py:133
  143.6 3.2 %collective-permute-start.24 = (f32[2,256,128]{2,1,0:T(8,128)}, f32[2,256,128]{2,1,0:T(8,128)}, u32[]{:S(2)}, u32[]{:S(2)}) collective-permute-start(f32[2,256,128]{2,1,0:T(8,128)} %get-tuple-element.80), channel_id=1, source_target_pairs={{0,2},{2,4},{4,6},{6,0},{1,3},{3,5},{5,7},{7,1},{8,10},{10,12},{12... | collective-permute-start | bytes 786440 | tf_op jit(solution)/shard_map/ppermute | solution.py:21
  146.8 5.0 %collective-permute-done.25 = f32[2,256,128]{2,1,0:T(8,128)S(1)} collective-permute-done((f32[2,256,128]{2,1,0:T(8,128)}, f32[2,256,128]{2,1,0:T(8,128)S(1)}, u32[]{:S(2)}, u32[]{:S(2)}) %collective-permute-start.25) | collective-permute-done | bytes 262176 | tf_op jit(solution)/shard_map/ppermute | solution.py:21
  153.1 3.3 %collective-permute-start.28 = (f32[2,2,256,128]{3,2,1,0:T(8,128)S(1)}, f32[2,2,256,128]{3,2,1,0:T(8,128)S(1)}, u32[]{:S(2)}, u32[]{:S(2)}) collective-permute-start(f32[2,2,256,128]{3,2,1,0:T(8,128)S(1)} %pad_maximum_fusion.4), channel_id=1, source_target_pairs={{0,2},{2,4},{4,6},{6,0},{1,3},{3,5},{5,7},{7,1},{8,10},{10,12},{12... | collective-permute-start | bytes 1572872 | tf_op jit(solution)/shard_map/ppermute | solution.py:21
  157.8 3.2 %collective-permute-start.26 = (f32[2,256,128]{2,1,0:T(8,128)S(1)}, f32[2,256,128]{2,1,0:T(8,128)S(1)}, u32[]{:S(2)}, u32[]{:S(2)}) collective-permute-start(f32[2,256,128]{2,1,0:T(8,128)S(1)} %slice_bitcast_fusion.4), channel_id=1, source_target_pairs={{8,64},{64,8},{9,65},{65,9},{10,66},{66,10},{11,67},{67,11},{12,68... | collective-permute-start | bytes 786440 | tf_op jit(solution)/shard_map/ppermute | solution.py:161
  161.1 4.7 %collective-permute-done.29 = f32[2,2,256,128]{3,2,1,0:T(8,128)S(1)} collective-permute-done((f32[2,2,256,128]{3,2,1,0:T(8,128)S(1)}, f32[2,2,256,128]{3,2,1,0:T(8,128)S(1)}, u32[]{:S(2)}, u32[]{:S(2)}) %collective-permute-start.29) | collective-permute-done | bytes 524320 | tf_op jit(solution)/shard_map/ppermute | solution.py:21
  165.9 3.2 %collective-permute-start.30 = (f32[2,256,128]{2,1,0:T(8,128)S(1)}, f32[2,256,128]{2,1,0:T(8,128)S(1)}, u32[]{:S(2)}, u32[]{:S(2)}) collective-permute-start(f32[2,256,128]{2,1,0:T(8,128)S(1)} %slice_bitcast_fusion.2), channel_id=1, source_target_pairs={{8,64},{64,8},{9,65},{65,9},{10,66},{66,10},{11,67},{67,11},{12,68... | collective-permute-start | bytes 786440 | tf_op jit(solution)/shard_map/ppermute | solution.py:161
  169.2 8.7 %collective-permute-done.26 = f32[2,256,128]{2,1,0:T(8,128)S(1)} collective-permute-done((f32[2,256,128]{2,1,0:T(8,128)S(1)}, f32[2,256,128]{2,1,0:T(8,128)S(1)}, u32[]{:S(2)}, u32[]{:S(2)}) %collective-permute-start.26) | collective-permute-done | bytes 262176 | tf_op jit(solution)/shard_map/ppermute | solution.py:161
  178.0 4.0 %collective-permute-done.30 = f32[2,256,128]{2,1,0:T(8,128)S(1)} collective-permute-done((f32[2,256,128]{2,1,0:T(8,128)S(1)}, f32[2,256,128]{2,1,0:T(8,128)S(1)}, u32[]{:S(2)}, u32[]{:S(2)}) %collective-permute-start.30) | collective-permute-done | bytes 262176 | tf_op jit(solution)/shard_map/ppermute | solution.py:161
  (95 shorter events, 23.4 us)
Async XLA Ops:
  6.5 78.0 %all-gather.3.cloned.1.call-start = ((), (), s32[]{:S(2)}) async-start(), calls=%async_computation | async-start | bytes 8912896 | tf_op jit(solution)/shard_map/all_gather | solution.py:170
  8.6 9.4 %collective-permute-start.3 = (f32[2,2,256,256]{3,2,1,0:T(8,128)S(1)}, f32[2,2,256,256]{3,2,1,0:T(8,128)}, u32[]{:S(2)}, u32[]{:S(2)}) collective-permute-start(f32[2,2,256,256]{3,2,1,0:T(8,128)S(1)} %constant_dynamic-slice_fusion.1), channel_id=1, source_target_pairs={{0,1},{1,0},{2,3},{3,2},{4,5},{5,4},{6,7},{7,6},{8,9},{9,8},{10,11... | collective-permute-start | bytes 3145736 | tf_op jit(solution)/shard_map/ppermute | solution.py:21
  11.9 14.8 %collective-permute-start.5 = (f32[2,2,256,128]{3,2,1,0:T(8,128)S(1)}, f32[2,2,256,128]{3,2,1,0:T(8,128)S(1)}, u32[]{:S(2)}, u32[]{:S(2)}) collective-permute-start(f32[2,2,256,128]{3,2,1,0:T(8,128)S(1)} %get-tuple-element.88.refs_0_), channel_id=1, source_target_pairs={{0,16},{16,32},{32,48},{48,0},{1,17},{17,33},{33,49},{49,1},{2,18}... | collective-permute-start | bytes 1572872 | tf_op jit(solution)/shard_map/ppermute | solution.py:21
  12.4 16.1 %collective-permute-start.2 = (f32[2,2,256,128]{3,2,1,0:T(8,128)S(1)}, f32[2,2,256,128]{3,2,1,0:T(8,128)}, u32[]{:S(2)}, u32[]{:S(2)}) collective-permute-start(f32[2,2,256,128]{3,2,1,0:T(8,128)S(1)} %get-tuple-element.88.refs_0_), channel_id=1, source_target_pairs={{0,48},{16,0},{32,16},{48,32},{1,49},{17,1},{33,17},{49,33},{2,50}... | collective-permute-start | bytes 1572872 | tf_op jit(solution)/shard_map/ppermute | solution.py:21
  15.0 21.7 %collective-permute-start.1 = (f32[2,128,512]{2,1,0:T(8,128)S(1)}, f32[2,128,512]{2,1,0:T(8,128)S(1)}, u32[]{:S(2)}, u32[]{:S(2)}) collective-permute-start(f32[2,128,512]{2,1,0:T(8,128)S(1)} %pad_maximum_fusion.1), channel_id=1, source_target_pairs={{0,64},{64,0},{1,65},{65,1},{2,66},{66,2},{3,67},{67,3},{4,68},{68... | collective-permute-start | bytes 1572872 | tf_op jit(solution)/shard_map/ppermute | solution.py:21
  20.1 17.0 %collective-permute-start.6 = (f32[2,2,256,128]{3,2,1,0:T(8,128)S(1)}, f32[2,2,256,128]{3,2,1,0:T(8,128)}, u32[]{:S(2)}, u32[]{:S(2)}) collective-permute-start(f32[2,2,256,128]{3,2,1,0:T(8,128)S(1)} %get-tuple-element.90.refs_1_), channel_id=1, source_target_pairs={{0,16},{16,32},{32,48},{48,0},{1,17},{17,33},{33,49},{49,1},{2,18}... | collective-permute-start | bytes 1572872 | tf_op jit(solution)/shard_map/ppermute | solution.py:21
  21.8 16.6 %collective-permute-start.4 = (f32[2,2,256,128]{3,2,1,0:T(8,128)S(1)}, f32[2,2,256,128]{3,2,1,0:T(8,128)S(1)}, u32[]{:S(2)}, u32[]{:S(2)}) collective-permute-start(f32[2,2,256,128]{3,2,1,0:T(8,128)S(1)} %get-tuple-element.90.refs_1_), channel_id=1, source_target_pairs={{0,48},{16,0},{32,16},{48,32},{1,49},{17,1},{33,17},{49,33},{2,50}... | collective-permute-start | bytes 1572872 | tf_op jit(solution)/shard_map/ppermute | solution.py:21
  39.3 24.1 %collective-permute-start.8 = (f32[2,2,128,512]{3,2,1,0:T(8,128)S(1)}, f32[2,2,128,512]{3,2,1,0:T(8,128)S(1)}, u32[]{:S(2)}, u32[]{:S(2)}) collective-permute-start(f32[2,2,128,512]{3,2,1,0:T(8,128)S(1)} %pad_maximum_fusion.e_0), channel_id=1, source_target_pairs={{0,16},{16,32},{32,48},{48,0},{1,17},{17,33},{33,49},{49,1},{2,18}... | collective-permute-start | bytes 3145736 | tf_op jit(solution)/shard_map/ppermute | solution.py:21
  39.9 25.0 %collective-permute-start.7 = (f32[2,2,128,512]{3,2,1,0:T(8,128)S(1)}, f32[2,2,128,512]{3,2,1,0:T(8,128)S(1)}, u32[]{:S(2)}, u32[]{:S(2)}) collective-permute-start(f32[2,2,128,512]{3,2,1,0:T(8,128)S(1)} %pad_maximum_fusion.e_0), channel_id=1, source_target_pairs={{0,48},{16,0},{32,16},{48,32},{1,49},{17,1},{33,17},{49,33},{2,50}... | collective-permute-start | bytes 3145736 | tf_op jit(solution)/shard_map/ppermute | solution.py:21
  65.1 14.9 %collective-permute-start.10 = (f32[2,128,512]{2,1,0:T(8,128)S(1)}, f32[2,128,512]{2,1,0:T(8,128)S(1)}, u32[]{:S(2)}, u32[]{:S(2)}) collective-permute-start(f32[2,128,512]{2,1,0:T(8,128)S(1)} %slice_bitcast_fusion), channel_id=1, source_target_pairs={{0,16},{16,32},{32,48},{48,0},{1,17},{17,33},{33,49},{49,1},{2,18}... | collective-permute-start | bytes 1572872 | tf_op jit(solution)/shard_map/ppermute | solution.py:21
  65.4 16.1 %collective-permute-start.9 = (f32[2,128,512]{2,1,0:T(8,128)S(1)}, f32[2,128,512]{2,1,0:T(8,128)S(1)}, u32[]{:S(2)}, u32[]{:S(2)}) collective-permute-start(f32[2,128,512]{2,1,0:T(8,128)S(1)} %slice_bitcast_fusion.1), channel_id=1, source_target_pairs={{0,48},{16,0},{32,16},{48,32},{1,49},{17,1},{33,17},{49,33},{2,50}... | collective-permute-start | bytes 1572872 | tf_op jit(solution)/shard_map/ppermute | solution.py:21
  67.1 33.3 %collective-permute-start.11 = (f32[2,2,256,128]{3,2,1,0:T(8,128)}, f32[2,2,256,128]{3,2,1,0:T(8,128)}, u32[]{:S(2)}, u32[]{:S(2)}) collective-permute-start(f32[2,2,256,128]{3,2,1,0:T(8,128)} %collective-permute-done.2.refs_2_), channel_id=1, source_target_pairs={{0,48},{16,0},{32,16},{48,32},{1,49},{17,1},{33,17},{49,33},{2,50}... | collective-permute-start | bytes 1572872 | tf_op jit(solution)/shard_map/ppermute | solution.py:21
  67.4 33.1 %collective-permute-start.12 = (f32[2,2,256,128]{3,2,1,0:T(8,128)}, f32[2,2,256,128]{3,2,1,0:T(8,128)}, u32[]{:S(2)}, u32[]{:S(2)}) collective-permute-start(f32[2,2,256,128]{3,2,1,0:T(8,128)} %collective-permute-done.6.refs_7_), channel_id=1, source_target_pairs={{0,16},{16,32},{32,48},{48,0},{1,17},{17,33},{33,49},{49,1},{2,18}... | collective-permute-start | bytes 1572872 | tf_op jit(solution)/shard_map/ppermute | solution.py:21
  82.3 18.2 %collective-permute-start.14 = (f32[2,2,256,128]{3,2,1,0:T(8,128)}, f32[2,2,256,128]{3,2,1,0:T(8,128)}, u32[]{:S(2)}, u32[]{:S(2)}) collective-permute-start(f32[2,2,256,128]{3,2,1,0:T(8,128)} %get-tuple-element.65.refs_0_), channel_id=1, source_target_pairs={{0,16},{16,32},{32,48},{48,0},{1,17},{17,33},{33,49},{49,1},{2,18}... | collective-permute-start | bytes 1572872 | tf_op jit(solution)/shard_map/ppermute | solution.py:21
  83.1 17.9 %collective-permute-start.13 = (f32[2,2,256,128]{3,2,1,0:T(8,128)}, f32[2,2,256,128]{3,2,1,0:T(8,128)}, u32[]{:S(2)}, u32[]{:S(2)}) collective-permute-start(f32[2,2,256,128]{3,2,1,0:T(8,128)} %get-tuple-element.65.refs_0_), channel_id=1, source_target_pairs={{0,48},{16,0},{32,16},{48,32},{1,49},{17,1},{33,17},{49,33},{2,50}... | collective-permute-start | bytes 1572872 | tf_op jit(solution)/shard_map/ppermute | solution.py:21
  101.0 7.2 %collective-permute-start.17 = (f32[2,2,512,512]{3,2,1,0:T(8,128)S(1)}, f32[2,2,512,512]{3,2,1,0:T(8,128)S(1)}, u32[]{:S(2)}, u32[]{:S(2)}) collective-permute-start(f32[2,2,512,512]{3,2,1,0:T(8,128)S(1)} %shard_map.37.own), channel_id=1, source_target_pairs={{0,1},{1,0},{2,3},{3,2},{4,5},{5,4},{6,7},{7,6},{8,9},{9,8},{10,11... | collective-permute-start | bytes 12582920 | tf_op jit(solution)/shard_map/ppermute | solution.py:21
  101.0 18.8 %collective-permute-start.16 = (f32[2,2,256,128]{3,2,1,0:T(8,128)S(1)}, f32[2,2,256,128]{3,2,1,0:T(8,128)S(1)}, u32[]{:S(2)}, u32[]{:S(2)}) collective-permute-start(f32[2,2,256,128]{3,2,1,0:T(8,128)S(1)} %copy-done.1), channel_id=1, source_target_pairs={{0,16},{16,32},{32,48},{48,0},{1,17},{17,33},{33,49},{49,1},{2,18}... | collective-permute-start | bytes 1572872 | tf_op jit(solution)/shard_map/ppermute | solution.py:21
  102.4 17.4 %collective-permute-start.15 = (f32[2,2,256,128]{3,2,1,0:T(8,128)S(1)}, f32[2,2,256,128]{3,2,1,0:T(8,128)S(1)}, u32[]{:S(2)}, u32[]{:S(2)}) collective-permute-start(f32[2,2,256,128]{3,2,1,0:T(8,128)S(1)} %copy-done.1), channel_id=1, source_target_pairs={{0,48},{16,0},{32,16},{48,32},{1,49},{17,1},{33,17},{49,33},{2,50}... | collective-permute-start | bytes 1572872 | tf_op jit(solution)/shard_map/ppermute | solution.py:21
  116.5 9.6 %collective-permute-start.22 = (f32[2,256,128]{2,1,0:T(8,128)S(1)}, f32[2,256,128]{2,1,0:T(8,128)S(1)}, u32[]{:S(2)}, u32[]{:S(2)}) collective-permute-start(f32[2,256,128]{2,1,0:T(8,128)S(1)} %get-tuple-element.85), channel_id=1, source_target_pairs={{0,6},{2,0},{4,2},{6,4},{1,7},{3,1},{5,3},{7,5},{8,14},{10,8},{12,... | collective-permute-start | bytes 786440 | tf_op jit(solution)/shard_map/ppermute | solution.py:21
  117.2 8.9 %collective-permute-start.20 = (f32[2,256,128]{2,1,0:T(8,128)S(1)}, f32[2,256,128]{2,1,0:T(8,128)S(1)}, u32[]{:S(2)}, u32[]{:S(2)}) collective-permute-start(f32[2,256,128]{2,1,0:T(8,128)S(1)} %get-tuple-element.86), channel_id=1, source_target_pairs={{0,2},{2,4},{4,6},{6,0},{1,3},{3,5},{5,7},{7,1},{8,10},{10,12},{12... | collective-permute-start | bytes 786440 | tf_op jit(solution)/shard_map/ppermute | solution.py:21
  119.8 14.8 %collective-permute-start.18 = (f32[2,2,256,128]{3,2,1,0:T(8,128)}, f32[2,2,256,128]{3,2,1,0:T(8,128)S(1)}, u32[]{:S(2)}, u32[]{:S(2)}) collective-permute-start(f32[2,2,256,128]{3,2,1,0:T(8,128)} %collective-permute-done.13.refs_2_), channel_id=1, source_target_pairs={{0,48},{16,0},{32,16},{48,32},{1,49},{17,1},{33,17},{49,33},{2,50}... | collective-permute-start | bytes 1572872 | tf_op jit(solution)/shard_map/ppermute | solution.py:21
  120.3 14.4 %collective-permute-start.19 = (f32[2,2,256,128]{3,2,1,0:T(8,128)S(1)}, f32[2,2,256,128]{3,2,1,0:T(8,128)S(1)}, u32[]{:S(2)}, u32[]{:S(2)}) collective-permute-start(f32[2,2,256,128]{3,2,1,0:T(8,128)S(1)} %collective-permute-done.16.refs_7_), channel_id=1, source_target_pairs={{0,16},{16,32},{32,48},{48,0},{1,17},{17,33},{33,49},{49,1},{2,18}... | collective-permute-start | bytes 1572872 | tf_op jit(solution)/shard_map/ppermute | solution.py:21
  126.2 20.6 %collective-permute-start.21 = (f32[2,2,256,128]{3,2,1,0:T(8,128)S(1)}, f32[2,2,256,128]{3,2,1,0:T(8,128)}, u32[]{:S(2)}, u32[]{:S(2)}) collective-permute-start(f32[2,2,256,128]{3,2,1,0:T(8,128)S(1)} %pad_maximum_fusion.2), channel_id=1, source_target_pairs={{0,2},{2,4},{4,6},{6,0},{1,3},{3,5},{5,7},{7,1},{8,10},{10,12},{12... | collective-permute-start | bytes 1572872 | tf_op jit(solution)/shard_map/ppermute | solution.py:21
  129.3 17.5 %collective-permute-start.23 = (f32[2,2,256,128]{3,2,1,0:T(8,128)S(1)}, f32[2,2,256,128]{3,2,1,0:T(8,128)}, u32[]{:S(2)}, u32[]{:S(2)}) collective-permute-start(f32[2,2,256,128]{3,2,1,0:T(8,128)S(1)} %pad_maximum_fusion.3), channel_id=1, source_target_pairs={{0,6},{2,0},{4,2},{6,4},{1,7},{3,1},{5,3},{7,5},{8,14},{10,8},{12,... | collective-permute-start | bytes 1572872 | tf_op jit(solution)/shard_map/ppermute | solution.py:21
  143.6 8.3 %collective-permute-start.25 = (f32[2,256,128]{2,1,0:T(8,128)}, f32[2,256,128]{2,1,0:T(8,128)S(1)}, u32[]{:S(2)}, u32[]{:S(2)}) collective-permute-start(f32[2,256,128]{2,1,0:T(8,128)} %get-tuple-element.79), channel_id=1, source_target_pairs={{0,6},{2,0},{4,2},{6,4},{1,7},{3,1},{5,3},{7,5},{8,14},{10,8},{12,... | collective-permute-start | bytes 786440 | tf_op jit(solution)/shard_map/ppermute | solution.py:21
  143.6 8.3 %collective-permute-start.24 = (f32[2,256,128]{2,1,0:T(8,128)}, f32[2,256,128]{2,1,0:T(8,128)}, u32[]{:S(2)}, u32[]{:S(2)}) collective-permute-start(f32[2,256,128]{2,1,0:T(8,128)} %get-tuple-element.80), channel_id=1, source_target_pairs={{0,2},{2,4},{4,6},{6,0},{1,3},{3,5},{5,7},{7,1},{8,10},{10,12},{12... | collective-permute-start | bytes 786440 | tf_op jit(solution)/shard_map/ppermute | solution.py:21
  153.0 12.8 %collective-permute-start.29 = (f32[2,2,256,128]{3,2,1,0:T(8,128)S(1)}, f32[2,2,256,128]{3,2,1,0:T(8,128)S(1)}, u32[]{:S(2)}, u32[]{:S(2)}) collective-permute-start(f32[2,2,256,128]{3,2,1,0:T(8,128)S(1)} %pad_maximum_fusion.5), channel_id=1, source_target_pairs={{0,6},{2,0},{4,2},{6,4},{1,7},{3,1},{5,3},{7,5},{8,14},{10,8},{12,... | collective-permute-start | bytes 1572872 | tf_op jit(solution)/shard_map/ppermute | solution.py:21
  153.1 12.7 %collective-permute-start.28 = (f32[2,2,256,128]{3,2,1,0:T(8,128)S(1)}, f32[2,2,256,128]{3,2,1,0:T(8,128)S(1)}, u32[]{:S(2)}, u32[]{:S(2)}) collective-permute-start(f32[2,2,256,128]{3,2,1,0:T(8,128)S(1)} %pad_maximum_fusion.4), channel_id=1, source_target_pairs={{0,2},{2,4},{4,6},{6,0},{1,3},{3,5},{5,7},{7,1},{8,10},{10,12},{12... | collective-permute-start | bytes 1572872 | tf_op jit(solution)/shard_map/ppermute | solution.py:21
  157.8 20.1 %collective-permute-start.26 = (f32[2,256,128]{2,1,0:T(8,128)S(1)}, f32[2,256,128]{2,1,0:T(8,128)S(1)}, u32[]{:S(2)}, u32[]{:S(2)}) collective-permute-start(f32[2,256,128]{2,1,0:T(8,128)S(1)} %slice_bitcast_fusion.4), channel_id=1, source_target_pairs={{8,64},{64,8},{9,65},{65,9},{10,66},{66,10},{11,67},{67,11},{12,68... | collective-permute-start | bytes 786440 | tf_op jit(solution)/shard_map/ppermute | solution.py:161
  161.0 16.9 %collective-permute-start.27 = (f32[2,256,128]{2,1,0:T(8,128)S(1)}, f32[2,256,128]{2,1,0:T(8,128)S(1)}, u32[]{:S(2)}, u32[]{:S(2)}) collective-permute-start(f32[2,256,128]{2,1,0:T(8,128)S(1)} %fusion.6), channel_id=1, source_target_pairs={{0,64},{8,0},{64,72},{72,8},{1,65},{9,1},{65,73},{73,9},{2,66},{10... | collective-permute-start | bytes 786440 | tf_op jit(solution)/shard_map/ppermute | solution.py:162
  165.9 16.0 %collective-permute-start.30 = (f32[2,256,128]{2,1,0:T(8,128)S(1)}, f32[2,256,128]{2,1,0:T(8,128)S(1)}, u32[]{:S(2)}, u32[]{:S(2)}) collective-permute-start(f32[2,256,128]{2,1,0:T(8,128)S(1)} %slice_bitcast_fusion.2), channel_id=1, source_target_pairs={{8,64},{64,8},{9,65},{65,9},{10,66},{66,10},{11,67},{67,11},{12,68... | collective-permute-start | bytes 786440 | tf_op jit(solution)/shard_map/ppermute | solution.py:161
  169.1 12.8 %collective-permute-start.31 = (f32[2,256,128]{2,1,0:T(8,128)S(1)}, f32[2,256,128]{2,1,0:T(8,128)S(1)}, u32[]{:S(2)}, u32[]{:S(2)}) collective-permute-start(f32[2,256,128]{2,1,0:T(8,128)S(1)} %fusion.7), channel_id=1, source_target_pairs={{0,64},{8,0},{64,72},{72,8},{1,65},{9,1},{65,73},{73,9},{2,66},{10... | collective-permute-start | bytes 786440 | tf_op jit(solution)/shard_map/ppermute | solution.py:162
  (16 other events, 233.1 us)
Sparse Core Ops, SparseCore 0:
  9.5 75.0 all-gather.2

commit v4 on v3

--- a/solution.py
+++ b/solution.py
@@ -61,27 +61,20 @@
     out_ref[0, 1] = dot3(split(re - im), l_sum, dims) - first + second
 
 
-def update_kernel(own, other, *refs):
+def blocks(m_hi, m_lo, a_refs, from_x, out_ref):
     x, y, zh = (lax.axis_index(name) for name in ("x", "y", "zh"))
-    a_refs, (out_ref, m_hi, m_lo) = refs[:-3], refs[-3:]
-    b, a = own.shape[2:]
+    b = m_hi.shape[2]
     wide = a_refs[0].shape[-1]
     dims = ((1,), (0,))
 
-    for level in range(2):
-        for part in range(2):
-            turned = other[level, part]
-            turned = jnp.concatenate([turned[:, a // 2 :], turned[:, : a // 2]], axis=1)
-            m_hi[level, part], m_lo[level, part] = split(own[level, part] + turned)
-
     def beside(p, q):
         return jnp.concatenate([p, q], axis=1)
 
-    for j in range(4):
+    for n, j in enumerate(from_x):
         sides = []
         for level in range(2):
             (rh, rl), (ih, il) = [
-                split(jnp.concatenate([ref[level, part] for ref in a_refs[2 * j : 2 * j + 2]], axis=0))
+                split(jnp.concatenate([ref[level, part] for ref in a_refs[2 * n : 2 * n + 2]], axis=0))
                 for part in range(2)
             ]
             sides.append(((beside(rh, ih), beside(rl, il)), (beside(-ih, rh), beside(-il, rl))))
@@ -99,6 +92,26 @@
             out_ref[at, to, 1] = total[:, wide:]
 
 
+def first_kernel(own, other, *refs):
+    a_refs, (out_ref, m_hi, m_lo) = refs[:-3], refs[-3:]
+    a = own.shape[-1]
+    for level in range(2):
+        for part in range(2):
+            turned = other[level, part]
+            turned = jnp.concatenate([turned[:, a // 2 :], turned[:, : a // 2]], axis=1)
+            m_hi[level, part], m_lo[level, part] = split(own[level, part] + turned)
+    blocks(m_hi, m_lo, a_refs, range(4), out_ref)
+
+
+def most_kernel(m_hi, m_lo, *refs):
+    blocks(m_hi, m_lo, refs[:-1], (0, 1, 3), refs[-1])
+
+
+def last_kernel(m_hi, m_lo, mine, theirs, so_far, out_ref):
+    del so_far
+    blocks(m_hi, m_lo, (mine, theirs), (2,), out_ref)
+
+
 def cost(flops, *values, scale=1):
     size = sum(v.dtype.itemsize * v.size for v in values)
     return pl.CostEstimate(flops=int(scale * flops), bytes_accessed=size, transcendentals=0)
@@ -125,19 +138,21 @@
     )(*envs, sites)
 
 
-def update_partial(shares, sites):
-    levels, _, b, a = shares[0].shape
+def update_partial(kernel, mixed, sites, so_far=None):
+    levels, _, b, a = mixed[0].shape
     c = sites[0].shape[-1]
-    out = jax.ShapeDtypeStruct((4, 2, 2, b // 2, c), F32)
-    operands = (*shares, *sites)
+    out = [jax.ShapeDtypeStruct((4, 2, 2, b // 2, c), F32)]
+    if kernel is first_kernel:
+        out += [jax.ShapeDtypeStruct(mixed[0].shape, BF16)] * 2
+    operands = (*mixed, *sites) if so_far is None else (*mixed, *sites, so_far)
     return pl.pallas_call(
-        update_kernel,
+        kernel,
         out_shape=out,
         in_specs=whole(len(operands)),
-        out_specs=pl.BlockSpec(memory_space=pltpu.VMEM),
-        scratch_shapes=[pltpu.VMEM((levels, 2, b, a), BF16)] * 2,
+        out_specs=whole(len(out)),
+        input_output_aliases={} if so_far is None else {len(operands) - 1: 0},
         compiler_params=pltpu.CompilerParams(vmem_limit_bytes=VMEM),
-        cost_estimate=cost(2 * 3 * 4 * levels * b * a * 4 * c, out, *operands, scale=COST),
+        cost_estimate=cost(3 * levels * b * a * len(sites) * 4 * c, *out, *operands, scale=COST),
     )(*operands)
 
 
@@ -161,6 +176,13 @@
     near = lax.ppermute(far, axes, [(1, 2), (2, 1)])
     got = lax.ppermute(jnp.where(same, far, mine), axes, [(0, 2), (1, 0), (2, 3), (3, 1)])
     return jnp.where(same, mine, near) + got
+
+
+def round_ring(mine, far, same):
+    axes = ("zh", "zl")
+    across = lax.ppermute(far, axes, [(0, 3), (3, 0), (1, 2), (2, 1)])
+    got = lax.ppermute(jnp.where(same, across, mine), axes, [(0, 1), (3, 2), (1, 0), (2, 3)])
+    return jnp.where(same, mine, across) + got
 
 
 def local(environment, initial_site, compressed_site):
@@ -200,22 +222,20 @@
     other = move(share, "core", 1)
     q_other = [move(q_0[1], "x", -1), move(q_0[1], "x", 1)]
 
-    parts_0 = update_partial([share, other], [*p_0, *p_1, *p_2, *p_3])
+    parts_0, *mixed = update_partial(first_kernel, [share, other], [*p_0, *p_1, *p_2, *p_3])
     came_0 = first_step(parts_0)
     *q_own, q_other[0], q_other[1], parts_0 = tie((*q_own, *q_other, parts_0))
     q_1, q_3 = zip(q_own, q_other)
     q_2 = [move(q_own[0], "x", -1), move(q_other[1], "x", 1)]
+    [parts_1] = update_partial(most_kernel, mixed, [*q_0, *q_1, *q_3])
+    parts_1, *came_0 = tie((parts_1, *came_0))
     came_0 = second_step(parts_0, came_0)
-    parts_1 = update_partial([share, other], [*q_0, *q_1, *q_2, *q_3])
+    [parts_1] = update_partial(last_kernel, mixed, q_2, parts_1)
     came_1 = first_step(parts_1)
-    parts_1, *came = tie((parts_1, *came_0, *came_1))
-    came_0, came_1 = came[:2], came[2:]
+    parts_1, *came_0 = tie((parts_1, *came_0))
+    result_0 = round_ring(*(parts_0[0] + came_0[0] + came_0[1]), zl == zh)
     came_1 = second_step(parts_1, came_1)
-
-    results = []
-    for parts, came in ((parts_0, came_0), (parts_1, came_1)):
-        mine, far = parts[0] + came[0] + came[1]
-        results.append(to_place(mine, far, zl == zh))
+    results = [result_0, to_place(*(parts_1[0] + came_1[0] + came_1[1]), zl == zh)]
     return jnp.concatenate(results, axis=2)
 
 

time: 193 us -> 191 us (0.990); the launches traced: 190 us -> 191 us
  starting transfers between devices: 42.1 us -> 50.3 us
  waiting for transfers between devices: 87.3 us -> 80 us
    ppermute x2 -> x1, waiting for transfers between devices: 12.7 us -> 4.99 us  [to_place(): near = lax.ppermute(far, axes, [(1, 2), (2, 1)])]
    ppermute x28, waiting for transfers between devices: 73.6 us -> 67.1 us  [move(): return lax.ppermute(value, axis, [(i, (i + step) % n) for i in range(n)])]
    ppermute x28, starting transfers between devices: 35.6 us -> 40.8 us  [move(): return lax.ppermute(value, axis, [(i, (i + step) % n) for i in range(n)])]
    ppermute x0 -> x2, waiting for transfers between devices: none -> 4.77 us  [the longest x1 4.76 us: round_ring(): across = lax.ppermute(far, axes, [(0, 3), (3, 0), (1, 2), (2, 1)])]
    ppermute x0 -> x2, starting transfers between devices: none -> 4.02 us  [the longest x1 2.2 us: round_ring(): lax.ppermute(jnp.where(same, across, mine), axes, [(0, 1), (3, 2), (1, 0)...]
    ppermute x2 -> x1, waiting for transfers between devices: 0.01 us -> 2.44 us  [to_place(): lax.ppermute(jnp.where(same, far, mine), axes, [(0, 2), (1, 0), (2, 3), (...]
    ppermute x2 -> x1, starting transfers between devices: 6.33 us -> 5.33 us  [to_place(): near = lax.ppermute(far, axes, [(1, 2), (2, 1)])]
    pallas_call x2 -> x3, Pallas kernels: 16.4 us -> 16.6 us  [update_partial(): pl.pallas_call(kernel, out_shape=out, in_specs=whole(len(operands)), out_...]
  transfers between devices with their start and end apart: 33 -> 33, of which waited for: 18 -> 14; matrix products, arithmetic and copies ran while one was open for 5% -> 6% of each run, Pallas kernels for 16% -> 16%
where the time goes in v4:
time: 191 us
  waiting for transfers between devices  80 us (42%)
  starting transfers between devices  50.3 us (26%)
  Pallas kernels  30.4 us (16%)
  between operations  13.8 us (7%)
  local copies, waits for them, and re-layouts  11.7 us (6%)
  other arithmetic  4.45 us (2%)
    ppermute x28, waiting for transfers between devices, move(): return lax.ppermute(value, axis, [(i, (i + step) % n) for i in range(n)])  67.1 us
    ppermute x28, starting transfers between devices, move(): return lax.ppermute(value, axis, [(i, (i + step) % n) for i in range(n)])  40.8 us
    pallas_call x3, Pallas kernels, update_partial(): pl.pallas_call(kernel, out_shape=out, in_specs=whole(len(operands)), out_...  16.6 us
    pallas_call x1, Pallas kernels, mixed_partial(): pl.pallas_call(mixed_kernel, grid=(levels, 2), out_shape=out, in_specs=wh...  13.8 us
    ppermute x1, starting transfers between devices, to_place(): near = lax.ppermute(far, axes, [(1, 2), (2, 1)])  5.33 us
    ppermute x1, waiting for transfers between devices, to_place(): near = lax.ppermute(far, axes, [(1, 2), (2, 1)])  4.99 us
    ppermute x1, waiting for transfers between devices, round_ring(): across = lax.ppermute(far, axes, [(0, 3), (3, 0), (1, 2), (2, 1)])  4.76 us
    unnamed x28, local copies, waits for them, and re-layouts  4.53 us
  transfers between devices with their start and end apart: 33, of which 14 were waited for; matrix products, arithmetic and copies ran while one was open for 6% of the time, Pallas kernels for 16%

profile of v4, /device:TPU:62, one launch (start us, length us, event | category | flops | bytes accessed | tf_op | source)
XLA Modules:
  0.0 190.6 jit_solution(16157627824998369574)
XLA Ops:
  12.7 2.4 %collective-permute-start.5 = (f32[2,2,256,128]{3,2,1,0:T(8,128)S(1)}, f32[2,2,256,128]{3,2,1,0:T(8,128)S(1)}, u32[]{:S(2)}, u32[]{:S(2)}) collective-permute-start(f32[2,2,256,128]{3,2,1,0:T(8,128)S(1)} %get-tuple-element.96.refs_0_), channel_id=1, source_target_pairs={{0,16},{16,32},{32,48},{48,0},{1,17},{17,33},{33,49},{49,1},{2,18}... | collective-permute-start | bytes 1572872 | tf_op jit(solution)/shard_map/ppermute | solution.py:21
  16.2 3.1 %collective-permute-start.1 = (f32[2,128,512]{2,1,0:T(8,128)S(1)}, f32[2,128,512]{2,1,0:T(8,128)S(1)}, u32[]{:S(2)}, u32[]{:S(2)}) collective-permute-start(f32[2,128,512]{2,1,0:T(8,128)S(1)} %pad_maximum_fusion.1), channel_id=1, source_target_pairs={{0,64},{64,0},{1,65},{65,1},{2,66},{66,2},{3,67},{67,3},{4,68},{68... | collective-permute-start | bytes 1572872 | tf_op jit(solution)/shard_map/ppermute | solution.py:21
  19.2 2.1 %fusion.8 = (f32[2,2,256,128]{3,2,1,0:T(8,128)}, f32[2,2,256,128]{3,2,1,0:T(8,128)S(1)}) fusion(f32[2,2,256,256]{3,2,1,0:T(8,128)} %collective-permute-done.3), kind=kLoop, calls=%fused_computation.42 | loop fusion | bytes 2097152 | tf_op jit(solution)/shard_map/slice | solution.py:200
  21.4 3.2 %collective-permute-start.6 = (f32[2,2,256,128]{3,2,1,0:T(8,128)S(1)}, f32[2,2,256,128]{3,2,1,0:T(8,128)}, u32[]{:S(2)}, u32[]{:S(2)}) collective-permute-start(f32[2,2,256,128]{3,2,1,0:T(8,128)S(1)} %get-tuple-element.98.refs_1_), channel_id=1, source_target_pairs={{0,16},{16,32},{32,48},{48,0},{1,17},{17,33},{33,49},{49,1},{2,18}... | collective-permute-start | bytes 1572872 | tf_op jit(solution)/shard_map/ppermute | solution.py:21
  24.6 3.4 %collective-permute-done.2.refs_2_ = f32[2,2,256,128]{3,2,1,0:T(8,128)} collective-permute-done((f32[2,2,256,128]{3,2,1,0:T(8,128)S(1)}, f32[2,2,256,128]{3,2,1,0:T(8,128)}, u32[]{:S(2)}, u32[]{:S(2)}) %collective-permute-start.2) | collective-permute-done | bytes 524320 | tf_op jit(solution)/shard_map/ppermute | solution.py:21
  28.0 10.4 %collective-permute-done.1 = f32[2,128,512]{2,1,0:T(8,128)S(1)} collective-permute-done((f32[2,128,512]{2,1,0:T(8,128)S(1)}, f32[2,128,512]{2,1,0:T(8,128)S(1)}, u32[]{:S(2)}, u32[]{:S(2)}) %collective-permute-start.1) | collective-permute-done | bytes 524320 | tf_op jit(solution)/shard_map/ppermute | solution.py:21
  39.4 3.2 %collective-permute-start.8 = (f32[2,2,128,512]{3,2,1,0:T(8,128)S(1)}, f32[2,2,128,512]{3,2,1,0:T(8,128)S(1)}, u32[]{:S(2)}, u32[]{:S(2)}) collective-permute-start(f32[2,2,128,512]{3,2,1,0:T(8,128)S(1)} %pad_maximum_fusion.e_0), channel_id=1, source_target_pairs={{0,16},{16,32},{32,48},{48,0},{1,17},{17,33},{33,49},{49,1},{2,18}... | collective-permute-start | bytes 3145736 | tf_op jit(solution)/shard_map/ppermute | solution.py:21
  42.7 22.1 %collective-permute-done.7.e_1 = f32[2,2,128,512]{3,2,1,0:T(8,128)S(1)} collective-permute-done((f32[2,2,128,512]{3,2,1,0:T(8,128)S(1)}, f32[2,2,128,512]{3,2,1,0:T(8,128)S(1)}, u32[]{:S(2)}, u32[]{:S(2)}) %collective-permute-start.7) | collective-permute-done | bytes 1048608 | tf_op jit(solution)/shard_map/ppermute | solution.py:21
  64.8 3.0 %collective-permute-start.10 = (f32[2,128,512]{2,1,0:T(8,128)S(1)}, f32[2,128,512]{2,1,0:T(8,128)S(1)}, u32[]{:S(2)}, u32[]{:S(2)}) collective-permute-start(f32[2,128,512]{2,1,0:T(8,128)S(1)} %slice_bitcast_fusion), channel_id=1, source_target_pairs={{0,16},{16,32},{32,48},{48,0},{1,17},{17,33},{33,49},{49,1},{2,18}... | collective-permute-start | bytes 1572872 | tf_op jit(solution)/shard_map/ppermute | solution.py:21
  68.0 3.2 %collective-permute-start.12 = (f32[2,2,256,128]{3,2,1,0:T(8,128)}, f32[2,2,256,128]{3,2,1,0:T(8,128)}, u32[]{:S(2)}, u32[]{:S(2)}) collective-permute-start(f32[2,2,256,128]{3,2,1,0:T(8,128)} %collective-permute-done.6.refs_7_), channel_id=1, source_target_pairs={{0,16},{16,32},{32,48},{48,0},{1,17},{17,33},{33,49},{49,1},{2,18}... | collective-permute-start | bytes 1572872 | tf_op jit(solution)/shard_map/ppermute | solution.py:21
  71.3 8.9 %collective-permute-done.10.e_2high = f32[2,128,512]{2,1,0:T(8,128)S(1)} collective-permute-done((f32[2,128,512]{2,1,0:T(8,128)S(1)}, f32[2,128,512]{2,1,0:T(8,128)S(1)}, u32[]{:S(2)}, u32[]{:S(2)}) %collective-permute-start.10) | collective-permute-done | bytes 524320 | tf_op jit(solution)/shard_map/ppermute | solution.py:21
  81.0 3.0 %collective-permute-done.9.e_2low = f32[2,128,512]{2,1,0:T(8,128)S(1)} collective-permute-done((f32[2,128,512]{2,1,0:T(8,128)S(1)}, f32[2,128,512]{2,1,0:T(8,128)S(1)}, u32[]{:S(2)}, u32[]{:S(2)}) %collective-permute-start.9) | collective-permute-done | bytes 524320 | tf_op jit(solution)/shard_map/ppermute | solution.py:21
  84.8 3.2 %collective-permute-start.14 = (f32[2,2,256,128]{3,2,1,0:T(8,128)}, f32[2,2,256,128]{3,2,1,0:T(8,128)}, u32[]{:S(2)}, u32[]{:S(2)}) collective-permute-start(f32[2,2,256,128]{3,2,1,0:T(8,128)} %get-tuple-element.74.refs_0_), channel_id=1, source_target_pairs={{0,16},{16,32},{32,48},{48,0},{1,17},{17,33},{33,49},{49,1},{2,18}... | collective-permute-start | bytes 1572872 | tf_op jit(solution)/shard_map/ppermute | solution.py:21
  90.2 13.8 %shard_map.37.own = f32[2,2,512,512]{3,2,1,0:T(8,128)S(1)} custom-call(f32[2,2,128,512]{3,2,1,0:T(8,128)S(1)} %pad_maximum_fusion.e_0, f32[2,2,128,512]{3,2,1,0:T(8,128)S(1)} %collective-permute-done.7.e_1, f32[2,2,128,512]{3,2,1,0:T(8,128)S(1)} %collective-permute-done.8.e_3, f32[2,128,512]{2,1,0:T(8,128)S(1)} %copy-done.12, f32[2,128,512]{2,1,0:T(8,128)S(1)} %copy-done.10, ...), custom_call_target="tpu_custom_call" | custom-call | flops 193273536 | bytes 12582912 | tf_op jit(solution)/shard_map/pallas_call | solution.py:128
  104.2 3.2 %collective-permute-start.16 = (f32[2,2,256,128]{3,2,1,0:T(8,128)S(1)}, f32[2,2,256,128]{3,2,1,0:T(8,128)S(1)}, u32[]{:S(2)}, u32[]{:S(2)}) collective-permute-start(f32[2,2,256,128]{3,2,1,0:T(8,128)S(1)} %copy-done), channel_id=1, source_target_pairs={{0,16},{16,32},{32,48},{48,0},{1,17},{17,33},{33,49},{49,1},{2,18}... | collective-permute-start | bytes 1572872 | tf_op jit(solution)/shard_map/ppermute | solution.py:21
  107.4 3.8 %collective-permute-done.17.other = f32[2,2,512,512]{3,2,1,0:T(8,128)S(1)} collective-permute-done((f32[2,2,512,512]{3,2,1,0:T(8,128)S(1)}, f32[2,2,512,512]{3,2,1,0:T(8,128)S(1)}, u32[]{:S(2)}, u32[]{:S(2)}) %collective-permute-start.17) | collective-permute-done | bytes 4194336 | tf_op jit(solution)/shard_map/ppermute | solution.py:21
  111.2 8.4 %shard_map.38 = (f32[4,2,2,256,128]{4,3,2,1,0:T(8,128)S(1)}, bf16[2,2,512,512]{3,2,1,0:T(8,128)(2,1)S(1)}, bf16[2,2,512,512]{3,2,1,0:T(8,128)(2,1)S(1)}) custom-call(f32[2,2,512,512]{3,2,1,0:T(8,128)S(1)} %shard_map.37.own, f32[2,2,512,512]{3,2,1,0:T(8,128)S(1)} %collective-permute-done.17.other, f32[2,2,256,128]{3,2,1,0:T(8,128)S(1)} %copy-done.2, ...), custom_call_target="tpu_custom_call" | custom-call | flops 128849016 | bytes 18874368 | tf_op jit(solution)/shard_map/pallas_call | solution.py:148
  120.0 1.8 collective-permute-start.21
  121.8 3.2 %collective-permute-start.19 = (f32[2,2,256,128]{3,2,1,0:T(8,128)S(1)}, f32[2,2,256,128]{3,2,1,0:T(8,128)S(1)}, u32[]{:S(2)}, u32[]{:S(2)}) collective-permute-start(f32[2,2,256,128]{3,2,1,0:T(8,128)S(1)} %collective-permute-done.16.refs_5_), channel_id=1, source_target_pairs={{0,16},{16,32},{32,48},{48,0},{1,17},{17,33},{33,49},{49,1},{2,18}... | collective-permute-start | bytes 1572872 | tf_op jit(solution)/shard_map/ppermute | solution.py:21
  125.1 6.4 %shard_map.39.so_far = f32[4,2,2,256,128]{4,3,2,1,0:T(8,128)S(1)} custom-call(bf16[2,2,512,512]{3,2,1,0:T(8,128)(2,1)S(1)} %get-tuple-element.70.m_hi, bf16[2,2,512,512]{3,2,1,0:T(8,128)(2,1)S(1)} %get-tuple-element.71.m_lo, f32[2,2,256,128]{3,2,1,0:T(8,128)} %get-tuple-element.74.refs_0_, f32[2,2,256,128]{3,2,1,0:T(8,128)S(1)} %copy-done, ...), custom_call_target="tpu_custom_call" | custom-call | flops 96636768 | bytes 9437184 | tf_op jit(solution)/shard_map/pallas_call | solution.py:148
  132.4 2.9 %collective-permute-start.22 = (f32[2,2,256,128]{3,2,1,0:T(8,128)S(1)}, f32[2,2,256,128]{3,2,1,0:T(8,128)S(1)}, u32[]{:S(2)}, u32[]{:S(2)}) collective-permute-start(f32[2,2,256,128]{3,2,1,0:T(8,128)S(1)} %pad_maximum_fusion.2), channel_id=1, source_target_pairs={{0,2},{2,4},{4,6},{6,0},{1,3},{3,5},{5,7},{7,1},{8,10},{10,12},{12... | collective-permute-start | bytes 1572872 | tf_op jit(solution)/shard_map/ppermute | solution.py:21
  136.6 1.8 shard_map.40
  140.6 7.2 %collective-permute-done.23 = f32[2,2,256,128]{3,2,1,0:T(8,128)S(1)} collective-permute-done((f32[2,2,256,128]{3,2,1,0:T(8,128)S(1)}, f32[2,2,256,128]{3,2,1,0:T(8,128)S(1)}, u32[]{:S(2)}, u32[]{:S(2)}) %collective-permute-start.23) | collective-permute-done | bytes 524320 | tf_op jit(solution)/shard_map/ppermute | solution.py:21
  147.8 3.1 %collective-permute-done.26 = f32[2,256,128]{2,1,0:T(8,128)S(1)} collective-permute-done((f32[2,256,128]{2,1,0:T(8,128)S(1)}, f32[2,256,128]{2,1,0:T(8,128)S(1)}, u32[]{:S(2)}, u32[]{:S(2)}) %collective-permute-start.26) | collective-permute-done | bytes 262176 | tf_op jit(solution)/shard_map/ppermute | solution.py:21
  151.5 3.4 %collective-permute-start.27 = (f32[2,2,256,128]{3,2,1,0:T(8,128)S(1)}, f32[2,2,256,128]{3,2,1,0:T(8,128)}, u32[]{:S(2)}, u32[]{:S(2)}) collective-permute-start(f32[2,2,256,128]{3,2,1,0:T(8,128)S(1)} %pad_maximum_fusion.4), channel_id=1, source_target_pairs={{0,2},{2,4},{4,6},{6,0},{1,3},{3,5},{5,7},{7,1},{8,10},{10,12},{12... | collective-permute-start | bytes 1572872 | tf_op jit(solution)/shard_map/ppermute | solution.py:21
  156.5 1.8 collective-permute-start.24
  158.3 4.8 %collective-permute-done.24 = f32[2,256,128]{2,1,0:T(8,128)S(1)} collective-permute-done((f32[2,256,128]{2,1,0:T(8,128)}, f32[2,256,128]{2,1,0:T(8,128)S(1)}, u32[]{:S(2)}, u32[]{:S(2)}) %collective-permute-start.24) | collective-permute-done | bytes 262176 | tf_op jit(solution)/shard_map/ppermute | solution.py:183
  163.1 2.2 %collective-permute-start.25 = (f32[2,256,128]{2,1,0:T(8,128)S(1)}, f32[2,256,128]{2,1,0:T(8,128)S(1)}, u32[]{:S(2)}, u32[]{:S(2)}) collective-permute-start(f32[2,256,128]{2,1,0:T(8,128)S(1)} %fusion.6), channel_id=1, source_target_pairs={{0,8},{72,64},{8,0},{64,72},{1,9},{73,65},{9,1},{65,73},{2,10},{74... | collective-permute-start | bytes 786440 | tf_op jit(solution)/shard_map/ppermute | solution.py:184
  165.3 3.2 %collective-permute-done.29 = f32[2,2,256,128]{3,2,1,0:T(8,128)} collective-permute-done((f32[2,2,256,128]{3,2,1,0:T(8,128)}, f32[2,2,256,128]{3,2,1,0:T(8,128)}, u32[]{:S(2)}, u32[]{:S(2)}) %collective-permute-start.29) | collective-permute-done | bytes 524320 | tf_op jit(solution)/shard_map/ppermute | solution.py:21
  170.1 5.3 %collective-permute-start.30 = (f32[2,256,128]{2,1,0:T(8,128)S(1)}, f32[2,256,128]{2,1,0:T(8,128)S(1)}, u32[]{:S(2)}, u32[]{:S(2)}) collective-permute-start(f32[2,256,128]{2,1,0:T(8,128)S(1)} %slice_bitcast_fusion.2), channel_id=1, source_target_pairs={{8,64},{64,8},{9,65},{65,9},{10,66},{66,10},{11,67},{67,11},{12,68... | collective-permute-start | bytes 786440 | tf_op jit(solution)/shard_map/ppermute | solution.py:176
  175.5 2.4 %collective-permute-done.31 = f32[2,256,128]{2,1,0:T(8,128)S(1)} collective-permute-done((f32[2,256,128]{2,1,0:T(8,128)S(1)}, f32[2,256,128]{2,1,0:T(8,128)S(1)}, u32[]{:S(2)}, u32[]{:S(2)}) %collective-permute-start.31) | collective-permute-done | bytes 262176 | tf_op jit(solution)/shard_map/ppermute | solution.py:177
  177.9 5.0 %collective-permute-done.30 = f32[2,256,128]{2,1,0:T(8,128)S(1)} collective-permute-done((f32[2,256,128]{2,1,0:T(8,128)S(1)}, f32[2,256,128]{2,1,0:T(8,128)S(1)}, u32[]{:S(2)}, u32[]{:S(2)}) %collective-permute-start.30) | collective-permute-done | bytes 262176 | tf_op jit(solution)/shard_map/ppermute | solution.py:176
  (94 shorter events, 21.6 us)
Async XLA Ops:
  6.5 81.5 %all-gather.3.cloned.1.call-start = ((), (), s32[]{:S(2)}) async-start(), calls=%async_computation | async-start | bytes 8912896 | tf_op jit(solution)/shard_map/all_gather | solution.py:192
  8.6 10.6 %collective-permute-start.3 = (f32[2,2,256,256]{3,2,1,0:T(8,128)S(1)}, f32[2,2,256,256]{3,2,1,0:T(8,128)}, u32[]{:S(2)}, u32[]{:S(2)}) collective-permute-start(f32[2,2,256,256]{3,2,1,0:T(8,128)S(1)} %constant_dynamic-slice_fusion.1), channel_id=1, source_target_pairs={{0,1},{1,0},{2,3},{3,2},{4,5},{5,4},{6,7},{7,6},{8,9},{9,8},{10,11... | collective-permute-start | bytes 3145736 | tf_op jit(solution)/shard_map/ppermute | solution.py:21
  11.9 16.1 %collective-permute-start.2 = (f32[2,2,256,128]{3,2,1,0:T(8,128)S(1)}, f32[2,2,256,128]{3,2,1,0:T(8,128)}, u32[]{:S(2)}, u32[]{:S(2)}) collective-permute-start(f32[2,2,256,128]{3,2,1,0:T(8,128)S(1)} %get-tuple-element.96.refs_0_), channel_id=1, source_target_pairs={{0,48},{16,0},{32,16},{48,32},{1,49},{17,1},{33,17},{49,33},{2,50}... | collective-permute-start | bytes 1572872 | tf_op jit(solution)/shard_map/ppermute | solution.py:21
  12.7 15.3 %collective-permute-start.5 = (f32[2,2,256,128]{3,2,1,0:T(8,128)S(1)}, f32[2,2,256,128]{3,2,1,0:T(8,128)S(1)}, u32[]{:S(2)}, u32[]{:S(2)}) collective-permute-start(f32[2,2,256,128]{3,2,1,0:T(8,128)S(1)} %get-tuple-element.96.refs_0_), channel_id=1, source_target_pairs={{0,16},{16,32},{32,48},{48,0},{1,17},{17,33},{33,49},{49,1},{2,18}... | collective-permute-start | bytes 1572872 | tf_op jit(solution)/shard_map/ppermute | solution.py:21
  16.2 22.3 %collective-permute-start.1 = (f32[2,128,512]{2,1,0:T(8,128)S(1)}, f32[2,128,512]{2,1,0:T(8,128)S(1)}, u32[]{:S(2)}, u32[]{:S(2)}) collective-permute-start(f32[2,128,512]{2,1,0:T(8,128)S(1)} %pad_maximum_fusion.1), channel_id=1, source_target_pairs={{0,64},{64,0},{1,65},{65,1},{2,66},{66,2},{3,67},{67,3},{4,68},{68... | collective-permute-start | bytes 1572872 | tf_op jit(solution)/shard_map/ppermute | solution.py:21
  21.4 17.1 %collective-permute-start.4 = (f32[2,2,256,128]{3,2,1,0:T(8,128)S(1)}, f32[2,2,256,128]{3,2,1,0:T(8,128)S(1)}, u32[]{:S(2)}, u32[]{:S(2)}) collective-permute-start(f32[2,2,256,128]{3,2,1,0:T(8,128)S(1)} %get-tuple-element.98.refs_1_), channel_id=1, source_target_pairs={{0,48},{16,0},{32,16},{48,32},{1,49},{17,1},{33,17},{49,33},{2,50}... | collective-permute-start | bytes 1572872 | tf_op jit(solution)/shard_map/ppermute | solution.py:21
  21.4 17.9 %collective-permute-start.6 = (f32[2,2,256,128]{3,2,1,0:T(8,128)S(1)}, f32[2,2,256,128]{3,2,1,0:T(8,128)}, u32[]{:S(2)}, u32[]{:S(2)}) collective-permute-start(f32[2,2,256,128]{3,2,1,0:T(8,128)S(1)} %get-tuple-element.98.refs_1_), channel_id=1, source_target_pairs={{0,16},{16,32},{32,48},{48,0},{1,17},{17,33},{33,49},{49,1},{2,18}... | collective-permute-start | bytes 1572872 | tf_op jit(solution)/shard_map/ppermute | solution.py:21
  39.4 25.4 %collective-permute-start.7 = (f32[2,2,128,512]{3,2,1,0:T(8,128)S(1)}, f32[2,2,128,512]{3,2,1,0:T(8,128)S(1)}, u32[]{:S(2)}, u32[]{:S(2)}) collective-permute-start(f32[2,2,128,512]{3,2,1,0:T(8,128)S(1)} %pad_maximum_fusion.e_0), channel_id=1, source_target_pairs={{0,48},{16,0},{32,16},{48,32},{1,49},{17,1},{33,17},{49,33},{2,50}... | collective-permute-start | bytes 3145736 | tf_op jit(solution)/shard_map/ppermute | solution.py:21
  39.4 25.3 %collective-permute-start.8 = (f32[2,2,128,512]{3,2,1,0:T(8,128)S(1)}, f32[2,2,128,512]{3,2,1,0:T(8,128)S(1)}, u32[]{:S(2)}, u32[]{:S(2)}) collective-permute-start(f32[2,2,128,512]{3,2,1,0:T(8,128)S(1)} %pad_maximum_fusion.e_0), channel_id=1, source_target_pairs={{0,16},{16,32},{32,48},{48,0},{1,17},{17,33},{33,49},{49,1},{2,18}... | collective-permute-start | bytes 3145736 | tf_op jit(solution)/shard_map/ppermute | solution.py:21
  64.8 15.4 %collective-permute-start.10 = (f32[2,128,512]{2,1,0:T(8,128)S(1)}, f32[2,128,512]{2,1,0:T(8,128)S(1)}, u32[]{:S(2)}, u32[]{:S(2)}) collective-permute-start(f32[2,128,512]{2,1,0:T(8,128)S(1)} %slice_bitcast_fusion), channel_id=1, source_target_pairs={{0,16},{16,32},{32,48},{48,0},{1,17},{17,33},{33,49},{49,1},{2,18}... | collective-permute-start | bytes 1572872 | tf_op jit(solution)/shard_map/ppermute | solution.py:21
  67.9 16.1 %collective-permute-start.9 = (f32[2,128,512]{2,1,0:T(8,128)S(1)}, f32[2,128,512]{2,1,0:T(8,128)S(1)}, u32[]{:S(2)}, u32[]{:S(2)}) collective-permute-start(f32[2,128,512]{2,1,0:T(8,128)S(1)} %slice_bitcast_fusion.1), channel_id=1, source_target_pairs={{0,48},{16,0},{32,16},{48,32},{1,49},{17,1},{33,17},{49,33},{2,50}... | collective-permute-start | bytes 1572872 | tf_op jit(solution)/shard_map/ppermute | solution.py:21
  68.0 36.0 %collective-permute-start.11 = (f32[2,2,256,128]{3,2,1,0:T(8,128)}, f32[2,2,256,128]{3,2,1,0:T(8,128)}, u32[]{:S(2)}, u32[]{:S(2)}) collective-permute-start(f32[2,2,256,128]{3,2,1,0:T(8,128)} %collective-permute-done.2.refs_2_), channel_id=1, source_target_pairs={{0,48},{16,0},{32,16},{48,32},{1,49},{17,1},{33,17},{49,33},{2,50}... | collective-permute-start | bytes 1572872 | tf_op jit(solution)/shard_map/ppermute | solution.py:21
  68.0 35.9 %collective-permute-start.12 = (f32[2,2,256,128]{3,2,1,0:T(8,128)}, f32[2,2,256,128]{3,2,1,0:T(8,128)}, u32[]{:S(2)}, u32[]{:S(2)}) collective-permute-start(f32[2,2,256,128]{3,2,1,0:T(8,128)} %collective-permute-done.6.refs_7_), channel_id=1, source_target_pairs={{0,16},{16,32},{32,48},{48,0},{1,17},{17,33},{33,49},{49,1},{2,18}... | collective-permute-start | bytes 1572872 | tf_op jit(solution)/shard_map/ppermute | solution.py:21
  84.8 19.1 %collective-permute-start.13 = (f32[2,2,256,128]{3,2,1,0:T(8,128)}, f32[2,2,256,128]{3,2,1,0:T(8,128)}, u32[]{:S(2)}, u32[]{:S(2)}) collective-permute-start(f32[2,2,256,128]{3,2,1,0:T(8,128)} %get-tuple-element.74.refs_0_), channel_id=1, source_target_pairs={{0,48},{16,0},{32,16},{48,32},{1,49},{17,1},{33,17},{49,33},{2,50}... | collective-permute-start | bytes 1572872 | tf_op jit(solution)/shard_map/ppermute | solution.py:21
  84.8 19.2 %collective-permute-start.14 = (f32[2,2,256,128]{3,2,1,0:T(8,128)}, f32[2,2,256,128]{3,2,1,0:T(8,128)}, u32[]{:S(2)}, u32[]{:S(2)}) collective-permute-start(f32[2,2,256,128]{3,2,1,0:T(8,128)} %get-tuple-element.74.refs_0_), channel_id=1, source_target_pairs={{0,16},{16,32},{32,48},{48,0},{1,17},{17,33},{33,49},{49,1},{2,18}... | collective-permute-start | bytes 1572872 | tf_op jit(solution)/shard_map/ppermute | solution.py:21
  104.0 7.2 %collective-permute-start.17 = (f32[2,2,512,512]{3,2,1,0:T(8,128)S(1)}, f32[2,2,512,512]{3,2,1,0:T(8,128)S(1)}, u32[]{:S(2)}, u32[]{:S(2)}) collective-permute-start(f32[2,2,512,512]{3,2,1,0:T(8,128)S(1)} %shard_map.37.own), channel_id=1, source_target_pairs={{0,1},{1,0},{2,3},{3,2},{4,5},{5,4},{6,7},{7,6},{8,9},{9,8},{10,11... | collective-permute-start | bytes 12582920 | tf_op jit(solution)/shard_map/ppermute | solution.py:21
  104.1 17.7 %collective-permute-start.15 = (f32[2,2,256,128]{3,2,1,0:T(8,128)S(1)}, f32[2,2,256,128]{3,2,1,0:T(8,128)S(1)}, u32[]{:S(2)}, u32[]{:S(2)}) collective-permute-start(f32[2,2,256,128]{3,2,1,0:T(8,128)S(1)} %copy-done), channel_id=1, source_target_pairs={{0,48},{16,0},{32,16},{48,32},{1,49},{17,1},{33,17},{49,33},{2,50}... | collective-permute-start | bytes 1572872 | tf_op jit(solution)/shard_map/ppermute | solution.py:21
  104.2 17.7 %collective-permute-start.16 = (f32[2,2,256,128]{3,2,1,0:T(8,128)S(1)}, f32[2,2,256,128]{3,2,1,0:T(8,128)S(1)}, u32[]{:S(2)}, u32[]{:S(2)}) collective-permute-start(f32[2,2,256,128]{3,2,1,0:T(8,128)S(1)} %copy-done), channel_id=1, source_target_pairs={{0,16},{16,32},{32,48},{48,0},{1,17},{17,33},{33,49},{49,1},{2,18}... | collective-permute-start | bytes 1572872 | tf_op jit(solution)/shard_map/ppermute | solution.py:21
  119.7 11.8 %collective-permute-start.20 = (f32[2,256,128]{2,1,0:T(8,128)S(1)}, f32[2,256,128]{2,1,0:T(8,128)S(1)}, u32[]{:S(2)}, u32[]{:S(2)}) collective-permute-start(f32[2,256,128]{2,1,0:T(8,128)S(1)} %get-tuple-element.94), channel_id=1, source_target_pairs={{0,2},{2,4},{4,6},{6,0},{1,3},{3,5},{5,7},{7,1},{8,10},{10,12},{12... | collective-permute-start | bytes 786440 | tf_op jit(solution)/shard_map/ppermute | solution.py:21
  120.0 11.5 %collective-permute-start.21 = (f32[2,256,128]{2,1,0:T(8,128)S(1)}, f32[2,256,128]{2,1,0:T(8,128)S(1)}, u32[]{:S(2)}, u32[]{:S(2)}) collective-permute-start(f32[2,256,128]{2,1,0:T(8,128)S(1)} %get-tuple-element.93), channel_id=1, source_target_pairs={{0,6},{2,0},{4,2},{6,4},{1,7},{3,1},{5,3},{7,5},{8,14},{10,8},{12,... | collective-permute-start | bytes 786440 | tf_op jit(solution)/shard_map/ppermute | solution.py:21
  121.8 14.8 %collective-permute-start.18 = (f32[2,2,256,128]{3,2,1,0:T(8,128)}, f32[2,2,256,128]{3,2,1,0:T(8,128)S(1)}, u32[]{:S(2)}, u32[]{:S(2)}) collective-permute-start(f32[2,2,256,128]{3,2,1,0:T(8,128)} %collective-permute-done.13.refs_2_), channel_id=1, source_target_pairs={{0,48},{16,0},{32,16},{48,32},{1,49},{17,1},{33,17},{49,33},{2,50}... | collective-permute-start | bytes 1572872 | tf_op jit(solution)/shard_map/ppermute | solution.py:21
  121.8 14.8 %collective-permute-start.19 = (f32[2,2,256,128]{3,2,1,0:T(8,128)S(1)}, f32[2,2,256,128]{3,2,1,0:T(8,128)S(1)}, u32[]{:S(2)}, u32[]{:S(2)}) collective-permute-start(f32[2,2,256,128]{3,2,1,0:T(8,128)S(1)} %collective-permute-done.16.refs_5_), channel_id=1, source_target_pairs={{0,16},{16,32},{32,48},{48,0},{1,17},{17,33},{33,49},{49,1},{2,18}... | collective-permute-start | bytes 1572872 | tf_op jit(solution)/shard_map/ppermute | solution.py:21
  131.7 16.1 %collective-permute-start.23 = (f32[2,2,256,128]{3,2,1,0:T(8,128)S(1)}, f32[2,2,256,128]{3,2,1,0:T(8,128)S(1)}, u32[]{:S(2)}, u32[]{:S(2)}) collective-permute-start(f32[2,2,256,128]{3,2,1,0:T(8,128)S(1)} %pad_maximum_fusion.3), channel_id=1, source_target_pairs={{0,6},{2,0},{4,2},{6,4},{1,7},{3,1},{5,3},{7,5},{8,14},{10,8},{12,... | collective-permute-start | bytes 1572872 | tf_op jit(solution)/shard_map/ppermute | solution.py:21
  132.4 15.4 %collective-permute-start.22 = (f32[2,2,256,128]{3,2,1,0:T(8,128)S(1)}, f32[2,2,256,128]{3,2,1,0:T(8,128)S(1)}, u32[]{:S(2)}, u32[]{:S(2)}) collective-permute-start(f32[2,2,256,128]{3,2,1,0:T(8,128)S(1)} %pad_maximum_fusion.2), channel_id=1, source_target_pairs={{0,2},{2,4},{4,6},{6,0},{1,3},{3,5},{5,7},{7,1},{8,10},{10,12},{12... | collective-permute-start | bytes 1572872 | tf_op jit(solution)/shard_map/ppermute | solution.py:21
  138.5 12.5 %collective-permute-start.26 = (f32[2,256,128]{2,1,0:T(8,128)S(1)}, f32[2,256,128]{2,1,0:T(8,128)S(1)}, u32[]{:S(2)}, u32[]{:S(2)}) collective-permute-start(f32[2,256,128]{2,1,0:T(8,128)S(1)} %get-tuple-element.85), channel_id=1, source_target_pairs={{0,2},{2,4},{4,6},{6,0},{1,3},{3,5},{5,7},{7,1},{8,10},{10,12},{12... | collective-permute-start | bytes 786440 | tf_op jit(solution)/shard_map/ppermute | solution.py:21
  140.1 11.2 %collective-permute-start.28 = (f32[2,256,128]{2,1,0:T(8,128)S(1)}, f32[2,256,128]{2,1,0:T(8,128)S(1)}, u32[]{:S(2)}, u32[]{:S(2)}) collective-permute-start(f32[2,256,128]{2,1,0:T(8,128)S(1)} %get-tuple-element.86), channel_id=1, source_target_pairs={{0,6},{2,0},{4,2},{6,4},{1,7},{3,1},{5,3},{7,5},{8,14},{10,8},{12,... | collective-permute-start | bytes 786440 | tf_op jit(solution)/shard_map/ppermute | solution.py:21
  151.5 13.8 %collective-permute-start.27 = (f32[2,2,256,128]{3,2,1,0:T(8,128)S(1)}, f32[2,2,256,128]{3,2,1,0:T(8,128)}, u32[]{:S(2)}, u32[]{:S(2)}) collective-permute-start(f32[2,2,256,128]{3,2,1,0:T(8,128)S(1)} %pad_maximum_fusion.4), channel_id=1, source_target_pairs={{0,2},{2,4},{4,6},{6,0},{1,3},{3,5},{5,7},{7,1},{8,10},{10,12},{12... | collective-permute-start | bytes 1572872 | tf_op jit(solution)/shard_map/ppermute | solution.py:21
  155.7 12.9 %collective-permute-start.29 = (f32[2,2,256,128]{3,2,1,0:T(8,128)}, f32[2,2,256,128]{3,2,1,0:T(8,128)}, u32[]{:S(2)}, u32[]{:S(2)}) collective-permute-start(f32[2,2,256,128]{3,2,1,0:T(8,128)} %pad_maximum_fusion.5), channel_id=1, source_target_pairs={{0,6},{2,0},{4,2},{6,4},{1,7},{3,1},{5,3},{7,5},{8,14},{10,8},{12,... | collective-permute-start | bytes 1572872 | tf_op jit(solution)/shard_map/ppermute | solution.py:21
  156.5 6.6 %collective-permute-start.24 = (f32[2,256,128]{2,1,0:T(8,128)}, f32[2,256,128]{2,1,0:T(8,128)S(1)}, u32[]{:S(2)}, u32[]{:S(2)}) collective-permute-start(f32[2,256,128]{2,1,0:T(8,128)} %slice_bitcast_fusion.6), channel_id=1, source_target_pairs={{0,72},{72,0},{8,64},{64,8},{1,73},{73,1},{9,65},{65,9},{2,74},{74... | collective-permute-start | bytes 786440 | tf_op jit(solution)/shard_map/ppermute | solution.py:183
  163.1 12.3 %collective-permute-start.25 = (f32[2,256,128]{2,1,0:T(8,128)S(1)}, f32[2,256,128]{2,1,0:T(8,128)S(1)}, u32[]{:S(2)}, u32[]{:S(2)}) collective-permute-start(f32[2,256,128]{2,1,0:T(8,128)S(1)} %fusion.6), channel_id=1, source_target_pairs={{0,8},{72,64},{8,0},{64,72},{1,9},{73,65},{9,1},{65,73},{2,10},{74... | collective-permute-start | bytes 786440 | tf_op jit(solution)/shard_map/ppermute | solution.py:184
  169.9 8.0 %collective-permute-start.31 = (f32[2,256,128]{2,1,0:T(8,128)S(1)}, f32[2,256,128]{2,1,0:T(8,128)S(1)}, u32[]{:S(2)}, u32[]{:S(2)}) collective-permute-start(f32[2,256,128]{2,1,0:T(8,128)S(1)} %fusion.7), channel_id=1, source_target_pairs={{0,64},{8,0},{64,72},{72,8},{1,65},{9,1},{65,73},{73,9},{2,66},{10... | collective-permute-start | bytes 786440 | tf_op jit(solution)/shard_map/ppermute | solution.py:177
  170.1 12.8 %collective-permute-start.30 = (f32[2,256,128]{2,1,0:T(8,128)S(1)}, f32[2,256,128]{2,1,0:T(8,128)S(1)}, u32[]{:S(2)}, u32[]{:S(2)}) collective-permute-start(f32[2,256,128]{2,1,0:T(8,128)S(1)} %slice_bitcast_fusion.2), channel_id=1, source_target_pairs={{8,64},{64,8},{9,65},{65,9},{10,66},{66,10},{11,67},{67,11},{12,68... | collective-permute-start | bytes 786440 | tf_op jit(solution)/shard_map/ppermute | solution.py:176
  (15 other events, 225.6 us)
Sparse Core Ops, SparseCore 0:
  9.5 75.7 all-gather.2

commit v5 on v4

--- a/solution.py
+++ b/solution.py
@@ -227,9 +227,9 @@
     *q_own, q_other[0], q_other[1], parts_0 = tie((*q_own, *q_other, parts_0))
     q_1, q_3 = zip(q_own, q_other)
     q_2 = [move(q_own[0], "x", -1), move(q_other[1], "x", 1)]
+    came_0 = second_step(parts_0, came_0)
     [parts_1] = update_partial(most_kernel, mixed, [*q_0, *q_1, *q_3])
-    parts_1, *came_0 = tie((parts_1, *came_0))
-    came_0 = second_step(parts_0, came_0)
+    parts_1, *q_2 = tie((parts_1, *q_2))
     [parts_1] = update_partial(last_kernel, mixed, q_2, parts_1)
     came_1 = first_step(parts_1)
     parts_1, *came_0 = tie((parts_1, *came_0))

time: 191 us -> 189 us (0.990)
  transfers between devices with their start and end apart: 33 -> 33, of which waited for: 14 -> 16; matrix products, arithmetic and copies ran while one was open for 6% -> 6% of each run, Pallas kernels for 16% -> 16%
where the time goes in v5:
time: 189 us
  waiting for transfers between devices  78.3 us (41%)
  starting transfers between devices  50.1 us (27%)
  Pallas kernels  30.4 us (16%)
  between operations  13.8 us (7%)
  local copies, waits for them, and re-layouts  11.7 us (6%)
  other arithmetic  4.45 us (2%)
    ppermute x28, waiting for transfers between devices, move(): return lax.ppermute(value, axis, [(i, (i + step) % n) for i in range(n)])  65.5 us
    ppermute x28, starting transfers between devices, move(): return lax.ppermute(value, axis, [(i, (i + step) % n) for i in range(n)])  40.6 us
    pallas_call x3, Pallas kernels, update_partial(): pl.pallas_call(kernel, out_shape=out, in_specs=whole(len(operands)), out_...  16.6 us
    pallas_call x1, Pallas kernels, mixed_partial(): pl.pallas_call(mixed_kernel, grid=(levels, 2), out_shape=out, in_specs=wh...  13.8 us
    ppermute x1, starting transfers between devices, to_place(): near = lax.ppermute(far, axes, [(1, 2), (2, 1)])  5.3 us
    ppermute x1, waiting for transfers between devices, to_place(): near = lax.ppermute(far, axes, [(1, 2), (2, 1)])  4.87 us
    ppermute x1, waiting for transfers between devices, round_ring(): across = lax.ppermute(far, axes, [(0, 3), (3, 0), (1, 2), (2, 1)])  4.77 us
    unnamed x28, local copies, waits for them, and re-layouts  4.53 us
  transfers between devices with their start and end apart: 33, of which 16 were waited for; matrix products, arithmetic and copies ran while one was open for 6% of the time, Pallas kernels for 16%

profile of v5, /device:TPU:62, one launch (start us, length us, event | category | flops | bytes accessed | tf_op | source)
XLA Modules:
  0.0 188.7 jit_solution(17415079166233572935)
XLA Ops:
  12.7 2.4 %collective-permute-start.5 = (f32[2,2,256,128]{3,2,1,0:T(8,128)S(1)}, f32[2,2,256,128]{3,2,1,0:T(8,128)S(1)}, u32[]{:S(2)}, u32[]{:S(2)}) collective-permute-start(f32[2,2,256,128]{3,2,1,0:T(8,128)S(1)} %get-tuple-element.96.refs_0_), channel_id=1, source_target_pairs={{0,16},{16,32},{32,48},{48,0},{1,17},{17,33},{33,49},{49,1},{2,18}... | collective-permute-start | bytes 1572872 | tf_op jit(solution)/shard_map/ppermute | solution.py:21
  16.2 3.1 %collective-permute-start.1 = (f32[2,128,512]{2,1,0:T(8,128)S(1)}, f32[2,128,512]{2,1,0:T(8,128)S(1)}, u32[]{:S(2)}, u32[]{:S(2)}) collective-permute-start(f32[2,128,512]{2,1,0:T(8,128)S(1)} %pad_maximum_fusion.1), channel_id=1, source_target_pairs={{0,64},{64,0},{1,65},{65,1},{2,66},{66,2},{3,67},{67,3},{4,68},{68... | collective-permute-start | bytes 1572872 | tf_op jit(solution)/shard_map/ppermute | solution.py:21
  19.2 2.1 %fusion.8 = (f32[2,2,256,128]{3,2,1,0:T(8,128)}, f32[2,2,256,128]{3,2,1,0:T(8,128)S(1)}) fusion(f32[2,2,256,256]{3,2,1,0:T(8,128)} %collective-permute-done.3), kind=kLoop, calls=%fused_computation.42 | loop fusion | bytes 2097152 | tf_op jit(solution)/shard_map/slice | solution.py:200
  21.4 3.2 %collective-permute-start.6 = (f32[2,2,256,128]{3,2,1,0:T(8,128)S(1)}, f32[2,2,256,128]{3,2,1,0:T(8,128)}, u32[]{:S(2)}, u32[]{:S(2)}) collective-permute-start(f32[2,2,256,128]{3,2,1,0:T(8,128)S(1)} %get-tuple-element.98.refs_1_), channel_id=1, source_target_pairs={{0,16},{16,32},{32,48},{48,0},{1,17},{17,33},{33,49},{49,1},{2,18}... | collective-permute-start | bytes 1572872 | tf_op jit(solution)/shard_map/ppermute | solution.py:21
  24.6 3.4 %collective-permute-done.2.refs_2_ = f32[2,2,256,128]{3,2,1,0:T(8,128)} collective-permute-done((f32[2,2,256,128]{3,2,1,0:T(8,128)S(1)}, f32[2,2,256,128]{3,2,1,0:T(8,128)}, u32[]{:S(2)}, u32[]{:S(2)}) %collective-permute-start.2) | collective-permute-done | bytes 524320 | tf_op jit(solution)/shard_map/ppermute | solution.py:21
  28.0 10.4 %collective-permute-done.1 = f32[2,128,512]{2,1,0:T(8,128)S(1)} collective-permute-done((f32[2,128,512]{2,1,0:T(8,128)S(1)}, f32[2,128,512]{2,1,0:T(8,128)S(1)}, u32[]{:S(2)}, u32[]{:S(2)}) %collective-permute-start.1) | collective-permute-done | bytes 524320 | tf_op jit(solution)/shard_map/ppermute | solution.py:21
  39.4 3.2 %collective-permute-start.8 = (f32[2,2,128,512]{3,2,1,0:T(8,128)S(1)}, f32[2,2,128,512]{3,2,1,0:T(8,128)S(1)}, u32[]{:S(2)}, u32[]{:S(2)}) collective-permute-start(f32[2,2,128,512]{3,2,1,0:T(8,128)S(1)} %pad_maximum_fusion.e_0), channel_id=1, source_target_pairs={{0,16},{16,32},{32,48},{48,0},{1,17},{17,33},{33,49},{49,1},{2,18}... | collective-permute-start | bytes 3145736 | tf_op jit(solution)/shard_map/ppermute | solution.py:21
  42.7 22.1 %collective-permute-done.7.e_1 = f32[2,2,128,512]{3,2,1,0:T(8,128)S(1)} collective-permute-done((f32[2,2,128,512]{3,2,1,0:T(8,128)S(1)}, f32[2,2,128,512]{3,2,1,0:T(8,128)S(1)}, u32[]{:S(2)}, u32[]{:S(2)}) %collective-permute-start.7) | collective-permute-done | bytes 1048608 | tf_op jit(solution)/shard_map/ppermute | solution.py:21
  64.8 3.0 %collective-permute-start.10 = (f32[2,128,512]{2,1,0:T(8,128)S(1)}, f32[2,128,512]{2,1,0:T(8,128)S(1)}, u32[]{:S(2)}, u32[]{:S(2)}) collective-permute-start(f32[2,128,512]{2,1,0:T(8,128)S(1)} %slice_bitcast_fusion), channel_id=1, source_target_pairs={{0,16},{16,32},{32,48},{48,0},{1,17},{17,33},{33,49},{49,1},{2,18}... | collective-permute-start | bytes 1572872 | tf_op jit(solution)/shard_map/ppermute | solution.py:21
  68.0 3.2 %collective-permute-start.12 = (f32[2,2,256,128]{3,2,1,0:T(8,128)}, f32[2,2,256,128]{3,2,1,0:T(8,128)}, u32[]{:S(2)}, u32[]{:S(2)}) collective-permute-start(f32[2,2,256,128]{3,2,1,0:T(8,128)} %collective-permute-done.6.refs_7_), channel_id=1, source_target_pairs={{0,16},{16,32},{32,48},{48,0},{1,17},{17,33},{33,49},{49,1},{2,18}... | collective-permute-start | bytes 1572872 | tf_op jit(solution)/shard_map/ppermute | solution.py:21
  71.3 8.9 %collective-permute-done.10.e_2high = f32[2,128,512]{2,1,0:T(8,128)S(1)} collective-permute-done((f32[2,128,512]{2,1,0:T(8,128)S(1)}, f32[2,128,512]{2,1,0:T(8,128)S(1)}, u32[]{:S(2)}, u32[]{:S(2)}) %collective-permute-start.10) | collective-permute-done | bytes 524320 | tf_op jit(solution)/shard_map/ppermute | solution.py:21
  81.0 3.0 %collective-permute-done.9.e_2low = f32[2,128,512]{2,1,0:T(8,128)S(1)} collective-permute-done((f32[2,128,512]{2,1,0:T(8,128)S(1)}, f32[2,128,512]{2,1,0:T(8,128)S(1)}, u32[]{:S(2)}, u32[]{:S(2)}) %collective-permute-start.9) | collective-permute-done | bytes 524320 | tf_op jit(solution)/shard_map/ppermute | solution.py:21
  84.8 3.2 %collective-permute-start.14 = (f32[2,2,256,128]{3,2,1,0:T(8,128)}, f32[2,2,256,128]{3,2,1,0:T(8,128)}, u32[]{:S(2)}, u32[]{:S(2)}) collective-permute-start(f32[2,2,256,128]{3,2,1,0:T(8,128)} %get-tuple-element.72.refs_0_), channel_id=1, source_target_pairs={{0,16},{16,32},{32,48},{48,0},{1,17},{17,33},{33,49},{49,1},{2,18}... | collective-permute-start | bytes 1572872 | tf_op jit(solution)/shard_map/ppermute | solution.py:21
  90.2 13.8 %shard_map.37.own = f32[2,2,512,512]{3,2,1,0:T(8,128)S(1)} custom-call(f32[2,2,128,512]{3,2,1,0:T(8,128)S(1)} %pad_maximum_fusion.e_0, f32[2,2,128,512]{3,2,1,0:T(8,128)S(1)} %collective-permute-done.7.e_1, f32[2,2,128,512]{3,2,1,0:T(8,128)S(1)} %collective-permute-done.8.e_3, f32[2,128,512]{2,1,0:T(8,128)S(1)} %copy-done.12, f32[2,128,512]{2,1,0:T(8,128)S(1)} %copy-done.10, ...), custom_call_target="tpu_custom_call" | custom-call | flops 193273536 | bytes 12582912 | tf_op jit(solution)/shard_map/pallas_call | solution.py:128
  104.2 3.2 %collective-permute-start.16 = (f32[2,2,256,128]{3,2,1,0:T(8,128)S(1)}, f32[2,2,256,128]{3,2,1,0:T(8,128)S(1)}, u32[]{:S(2)}, u32[]{:S(2)}) collective-permute-start(f32[2,2,256,128]{3,2,1,0:T(8,128)S(1)} %copy-done), channel_id=1, source_target_pairs={{0,16},{16,32},{32,48},{48,0},{1,17},{17,33},{33,49},{49,1},{2,18}... | collective-permute-start | bytes 1572872 | tf_op jit(solution)/shard_map/ppermute | solution.py:21
  107.4 3.8 %collective-permute-done.17.other = f32[2,2,512,512]{3,2,1,0:T(8,128)S(1)} collective-permute-done((f32[2,2,512,512]{3,2,1,0:T(8,128)S(1)}, f32[2,2,512,512]{3,2,1,0:T(8,128)S(1)}, u32[]{:S(2)}, u32[]{:S(2)}) %collective-permute-start.17) | collective-permute-done | bytes 4194336 | tf_op jit(solution)/shard_map/ppermute | solution.py:21
  111.2 8.4 %shard_map.38 = (f32[4,2,2,256,128]{4,3,2,1,0:T(8,128)S(1)}, bf16[2,2,512,512]{3,2,1,0:T(8,128)(2,1)S(1)}, bf16[2,2,512,512]{3,2,1,0:T(8,128)(2,1)S(1)}) custom-call(f32[2,2,512,512]{3,2,1,0:T(8,128)S(1)} %shard_map.37.own, f32[2,2,512,512]{3,2,1,0:T(8,128)S(1)} %collective-permute-done.17.other, f32[2,2,256,128]{3,2,1,0:T(8,128)S(1)} %copy-done.2, ...), custom_call_target="tpu_custom_call" | custom-call | flops 128849016 | bytes 18874368 | tf_op jit(solution)/shard_map/pallas_call | solution.py:148
  120.0 1.8 collective-permute-start.22
  121.8 3.2 %collective-permute-start.19 = (f32[2,2,256,128]{3,2,1,0:T(8,128)S(1)}, f32[2,2,256,128]{3,2,1,0:T(8,128)S(1)}, u32[]{:S(2)}, u32[]{:S(2)}) collective-permute-start(f32[2,2,256,128]{3,2,1,0:T(8,128)S(1)} %collective-permute-done.16.refs_5_), channel_id=1, source_target_pairs={{0,16},{16,32},{32,48},{48,0},{1,17},{17,33},{33,49},{49,1},{2,18}... | collective-permute-start | bytes 1572872 | tf_op jit(solution)/shard_map/ppermute | solution.py:21
  125.1 3.0 %collective-permute-done.20 = f32[2,256,128]{2,1,0:T(8,128)S(1)} collective-permute-done((f32[2,256,128]{2,1,0:T(8,128)S(1)}, f32[2,256,128]{2,1,0:T(8,128)S(1)}, u32[]{:S(2)}, u32[]{:S(2)}) %collective-permute-start.20) | collective-permute-done | bytes 262176 | tf_op jit(solution)/shard_map/ppermute | solution.py:21
  130.1 3.1 %collective-permute-start.21 = (f32[2,2,256,128]{3,2,1,0:T(8,128)S(1)}, f32[2,2,256,128]{3,2,1,0:T(8,128)S(1)}, u32[]{:S(2)}, u32[]{:S(2)}) collective-permute-start(f32[2,2,256,128]{3,2,1,0:T(8,128)S(1)} %pad_maximum_fusion.2), channel_id=1, source_target_pairs={{0,2},{2,4},{4,6},{6,0},{1,3},{3,5},{5,7},{7,1},{8,10},{10,12},{12... | collective-permute-start | bytes 1572872 | tf_op jit(solution)/shard_map/ppermute | solution.py:21
  133.2 6.4 %shard_map.39.so_far = f32[4,2,2,256,128]{4,3,2,1,0:T(8,128)S(1)} custom-call(bf16[2,2,512,512]{3,2,1,0:T(8,128)(2,1)S(1)} %get-tuple-element.70.m_hi, bf16[2,2,512,512]{3,2,1,0:T(8,128)(2,1)S(1)} %get-tuple-element.71.m_lo, f32[2,2,256,128]{3,2,1,0:T(8,128)} %get-tuple-element.72.refs_0_, f32[2,2,256,128]{3,2,1,0:T(8,128)S(1)} %copy-done, ...), custom_call_target="tpu_custom_call" | custom-call | flops 96636768 | bytes 9437184 | tf_op jit(solution)/shard_map/pallas_call | solution.py:148
  141.5 2.0 %collective-permute-start.28 = (f32[2,256,128]{2,1,0:T(8,128)S(1)}, f32[2,256,128]{2,1,0:T(8,128)S(1)}, u32[]{:S(2)}, u32[]{:S(2)}) collective-permute-start(f32[2,256,128]{2,1,0:T(8,128)S(1)} %get-tuple-element.86), channel_id=1, source_target_pairs={{0,6},{2,0},{4,2},{6,4},{1,7},{3,1},{5,3},{7,5},{8,14},{10,8},{12,... | collective-permute-start | bytes 786440 | tf_op jit(solution)/shard_map/ppermute | solution.py:21
  145.6 3.4 %collective-permute-done.26 = f32[2,256,128]{2,1,0:T(8,128)S(1)} collective-permute-done((f32[2,256,128]{2,1,0:T(8,128)S(1)}, f32[2,256,128]{2,1,0:T(8,128)S(1)}, u32[]{:S(2)}, u32[]{:S(2)}) %collective-permute-start.26) | collective-permute-done | bytes 262176 | tf_op jit(solution)/shard_map/ppermute | solution.py:21
  149.7 3.1 %collective-permute-start.27 = (f32[2,2,256,128]{3,2,1,0:T(8,128)S(1)}, f32[2,2,256,128]{3,2,1,0:T(8,128)}, u32[]{:S(2)}, u32[]{:S(2)}) collective-permute-start(f32[2,2,256,128]{3,2,1,0:T(8,128)S(1)} %pad_maximum_fusion.4), channel_id=1, source_target_pairs={{0,2},{2,4},{4,6},{6,0},{1,3},{3,5},{5,7},{7,1},{8,10},{10,12},{12... | collective-permute-start | bytes 1572872 | tf_op jit(solution)/shard_map/ppermute | solution.py:21
  154.5 1.8 collective-permute-start.24
  156.3 4.8 %collective-permute-done.24 = f32[2,256,128]{2,1,0:T(8,128)S(1)} collective-permute-done((f32[2,256,128]{2,1,0:T(8,128)}, f32[2,256,128]{2,1,0:T(8,128)S(1)}, u32[]{:S(2)}, u32[]{:S(2)}) %collective-permute-start.24) | collective-permute-done | bytes 262176 | tf_op jit(solution)/shard_map/ppermute | solution.py:183
  161.1 2.2 %collective-permute-start.25 = (f32[2,256,128]{2,1,0:T(8,128)S(1)}, f32[2,256,128]{2,1,0:T(8,128)S(1)}, u32[]{:S(2)}, u32[]{:S(2)}) collective-permute-start(f32[2,256,128]{2,1,0:T(8,128)S(1)} %fusion.6), channel_id=1, source_target_pairs={{0,8},{72,64},{8,0},{64,72},{1,9},{73,65},{9,1},{65,73},{2,10},{74... | collective-permute-start | bytes 786440 | tf_op jit(solution)/shard_map/ppermute | solution.py:184
  163.3 3.4 %collective-permute-done.29 = f32[2,2,256,128]{3,2,1,0:T(8,128)} collective-permute-done((f32[2,2,256,128]{3,2,1,0:T(8,128)}, f32[2,2,256,128]{3,2,1,0:T(8,128)}, u32[]{:S(2)}, u32[]{:S(2)}) %collective-permute-start.29) | collective-permute-done | bytes 524320 | tf_op jit(solution)/shard_map/ppermute | solution.py:21
  168.2 5.3 %collective-permute-start.30 = (f32[2,256,128]{2,1,0:T(8,128)S(1)}, f32[2,256,128]{2,1,0:T(8,128)S(1)}, u32[]{:S(2)}, u32[]{:S(2)}) collective-permute-start(f32[2,256,128]{2,1,0:T(8,128)S(1)} %slice_bitcast_fusion.2), channel_id=1, source_target_pairs={{8,64},{64,8},{9,65},{65,9},{10,66},{66,10},{11,67},{67,11},{12,68... | collective-permute-start | bytes 786440 | tf_op jit(solution)/shard_map/ppermute | solution.py:176
  173.6 2.5 %collective-permute-done.31 = f32[2,256,128]{2,1,0:T(8,128)S(1)} collective-permute-done((f32[2,256,128]{2,1,0:T(8,128)S(1)}, f32[2,256,128]{2,1,0:T(8,128)S(1)}, u32[]{:S(2)}, u32[]{:S(2)}) %collective-permute-start.31) | collective-permute-done | bytes 262176 | tf_op jit(solution)/shard_map/ppermute | solution.py:177
  176.1 4.9 %collective-permute-done.30 = f32[2,256,128]{2,1,0:T(8,128)S(1)} collective-permute-done((f32[2,256,128]{2,1,0:T(8,128)S(1)}, f32[2,256,128]{2,1,0:T(8,128)S(1)}, u32[]{:S(2)}, u32[]{:S(2)}) %collective-permute-start.30) | collective-permute-done | bytes 262176 | tf_op jit(solution)/shard_map/ppermute | solution.py:176
  (94 shorter events, 23.3 us)
Async XLA Ops:
  6.5 81.5 %all-gather.3.cloned.1.call-start = ((), (), s32[]{:S(2)}) async-start(), calls=%async_computation | async-start | bytes 8912896 | tf_op jit(solution)/shard_map/all_gather | solution.py:192
  8.6 10.6 %collective-permute-start.3 = (f32[2,2,256,256]{3,2,1,0:T(8,128)S(1)}, f32[2,2,256,256]{3,2,1,0:T(8,128)}, u32[]{:S(2)}, u32[]{:S(2)}) collective-permute-start(f32[2,2,256,256]{3,2,1,0:T(8,128)S(1)} %constant_dynamic-slice_fusion.1), channel_id=1, source_target_pairs={{0,1},{1,0},{2,3},{3,2},{4,5},{5,4},{6,7},{7,6},{8,9},{9,8},{10,11... | collective-permute-start | bytes 3145736 | tf_op jit(solution)/shard_map/ppermute | solution.py:21
  11.9 16.1 %collective-permute-start.2 = (f32[2,2,256,128]{3,2,1,0:T(8,128)S(1)}, f32[2,2,256,128]{3,2,1,0:T(8,128)}, u32[]{:S(2)}, u32[]{:S(2)}) collective-permute-start(f32[2,2,256,128]{3,2,1,0:T(8,128)S(1)} %get-tuple-element.96.refs_0_), channel_id=1, source_target_pairs={{0,48},{16,0},{32,16},{48,32},{1,49},{17,1},{33,17},{49,33},{2,50}... | collective-permute-start | bytes 1572872 | tf_op jit(solution)/shard_map/ppermute | solution.py:21
  12.7 15.3 %collective-permute-start.5 = (f32[2,2,256,128]{3,2,1,0:T(8,128)S(1)}, f32[2,2,256,128]{3,2,1,0:T(8,128)S(1)}, u32[]{:S(2)}, u32[]{:S(2)}) collective-permute-start(f32[2,2,256,128]{3,2,1,0:T(8,128)S(1)} %get-tuple-element.96.refs_0_), channel_id=1, source_target_pairs={{0,16},{16,32},{32,48},{48,0},{1,17},{17,33},{33,49},{49,1},{2,18}... | collective-permute-start | bytes 1572872 | tf_op jit(solution)/shard_map/ppermute | solution.py:21
  16.2 22.3 %collective-permute-start.1 = (f32[2,128,512]{2,1,0:T(8,128)S(1)}, f32[2,128,512]{2,1,0:T(8,128)S(1)}, u32[]{:S(2)}, u32[]{:S(2)}) collective-permute-start(f32[2,128,512]{2,1,0:T(8,128)S(1)} %pad_maximum_fusion.1), channel_id=1, source_target_pairs={{0,64},{64,0},{1,65},{65,1},{2,66},{66,2},{3,67},{67,3},{4,68},{68... | collective-permute-start | bytes 1572872 | tf_op jit(solution)/shard_map/ppermute | solution.py:21
  21.4 17.1 %collective-permute-start.4 = (f32[2,2,256,128]{3,2,1,0:T(8,128)S(1)}, f32[2,2,256,128]{3,2,1,0:T(8,128)S(1)}, u32[]{:S(2)}, u32[]{:S(2)}) collective-permute-start(f32[2,2,256,128]{3,2,1,0:T(8,128)S(1)} %get-tuple-element.98.refs_1_), channel_id=1, source_target_pairs={{0,48},{16,0},{32,16},{48,32},{1,49},{17,1},{33,17},{49,33},{2,50}... | collective-permute-start | bytes 1572872 | tf_op jit(solution)/shard_map/ppermute | solution.py:21
  21.4 17.9 %collective-permute-start.6 = (f32[2,2,256,128]{3,2,1,0:T(8,128)S(1)}, f32[2,2,256,128]{3,2,1,0:T(8,128)}, u32[]{:S(2)}, u32[]{:S(2)}) collective-permute-start(f32[2,2,256,128]{3,2,1,0:T(8,128)S(1)} %get-tuple-element.98.refs_1_), channel_id=1, source_target_pairs={{0,16},{16,32},{32,48},{48,0},{1,17},{17,33},{33,49},{49,1},{2,18}... | collective-permute-start | bytes 1572872 | tf_op jit(solution)/shard_map/ppermute | solution.py:21
  39.4 25.4 %collective-permute-start.7 = (f32[2,2,128,512]{3,2,1,0:T(8,128)S(1)}, f32[2,2,128,512]{3,2,1,0:T(8,128)S(1)}, u32[]{:S(2)}, u32[]{:S(2)}) collective-permute-start(f32[2,2,128,512]{3,2,1,0:T(8,128)S(1)} %pad_maximum_fusion.e_0), channel_id=1, source_target_pairs={{0,48},{16,0},{32,16},{48,32},{1,49},{17,1},{33,17},{49,33},{2,50}... | collective-permute-start | bytes 3145736 | tf_op jit(solution)/shard_map/ppermute | solution.py:21
  39.4 25.3 %collective-permute-start.8 = (f32[2,2,128,512]{3,2,1,0:T(8,128)S(1)}, f32[2,2,128,512]{3,2,1,0:T(8,128)S(1)}, u32[]{:S(2)}, u32[]{:S(2)}) collective-permute-start(f32[2,2,128,512]{3,2,1,0:T(8,128)S(1)} %pad_maximum_fusion.e_0), channel_id=1, source_target_pairs={{0,16},{16,32},{32,48},{48,0},{1,17},{17,33},{33,49},{49,1},{2,18}... | collective-permute-start | bytes 3145736 | tf_op jit(solution)/shard_map/ppermute | solution.py:21
  64.8 15.4 %collective-permute-start.10 = (f32[2,128,512]{2,1,0:T(8,128)S(1)}, f32[2,128,512]{2,1,0:T(8,128)S(1)}, u32[]{:S(2)}, u32[]{:S(2)}) collective-permute-start(f32[2,128,512]{2,1,0:T(8,128)S(1)} %slice_bitcast_fusion), channel_id=1, source_target_pairs={{0,16},{16,32},{32,48},{48,0},{1,17},{17,33},{33,49},{49,1},{2,18}... | collective-permute-start | bytes 1572872 | tf_op jit(solution)/shard_map/ppermute | solution.py:21
  67.9 16.1 %collective-permute-start.9 = (f32[2,128,512]{2,1,0:T(8,128)S(1)}, f32[2,128,512]{2,1,0:T(8,128)S(1)}, u32[]{:S(2)}, u32[]{:S(2)}) collective-permute-start(f32[2,128,512]{2,1,0:T(8,128)S(1)} %slice_bitcast_fusion.1), channel_id=1, source_target_pairs={{0,48},{16,0},{32,16},{48,32},{1,49},{17,1},{33,17},{49,33},{2,50}... | collective-permute-start | bytes 1572872 | tf_op jit(solution)/shard_map/ppermute | solution.py:21
  68.0 36.0 %collective-permute-start.11 = (f32[2,2,256,128]{3,2,1,0:T(8,128)}, f32[2,2,256,128]{3,2,1,0:T(8,128)}, u32[]{:S(2)}, u32[]{:S(2)}) collective-permute-start(f32[2,2,256,128]{3,2,1,0:T(8,128)} %collective-permute-done.2.refs_2_), channel_id=1, source_target_pairs={{0,48},{16,0},{32,16},{48,32},{1,49},{17,1},{33,17},{49,33},{2,50}... | collective-permute-start | bytes 1572872 | tf_op jit(solution)/shard_map/ppermute | solution.py:21
  68.0 35.9 %collective-permute-start.12 = (f32[2,2,256,128]{3,2,1,0:T(8,128)}, f32[2,2,256,128]{3,2,1,0:T(8,128)}, u32[]{:S(2)}, u32[]{:S(2)}) collective-permute-start(f32[2,2,256,128]{3,2,1,0:T(8,128)} %collective-permute-done.6.refs_7_), channel_id=1, source_target_pairs={{0,16},{16,32},{32,48},{48,0},{1,17},{17,33},{33,49},{49,1},{2,18}... | collective-permute-start | bytes 1572872 | tf_op jit(solution)/shard_map/ppermute | solution.py:21
  84.8 19.1 %collective-permute-start.13 = (f32[2,2,256,128]{3,2,1,0:T(8,128)}, f32[2,2,256,128]{3,2,1,0:T(8,128)}, u32[]{:S(2)}, u32[]{:S(2)}) collective-permute-start(f32[2,2,256,128]{3,2,1,0:T(8,128)} %get-tuple-element.72.refs_0_), channel_id=1, source_target_pairs={{0,48},{16,0},{32,16},{48,32},{1,49},{17,1},{33,17},{49,33},{2,50}... | collective-permute-start | bytes 1572872 | tf_op jit(solution)/shard_map/ppermute | solution.py:21
  84.8 19.2 %collective-permute-start.14 = (f32[2,2,256,128]{3,2,1,0:T(8,128)}, f32[2,2,256,128]{3,2,1,0:T(8,128)}, u32[]{:S(2)}, u32[]{:S(2)}) collective-permute-start(f32[2,2,256,128]{3,2,1,0:T(8,128)} %get-tuple-element.72.refs_0_), channel_id=1, source_target_pairs={{0,16},{16,32},{32,48},{48,0},{1,17},{17,33},{33,49},{49,1},{2,18}... | collective-permute-start | bytes 1572872 | tf_op jit(solution)/shard_map/ppermute | solution.py:21
  104.0 7.2 %collective-permute-start.17 = (f32[2,2,512,512]{3,2,1,0:T(8,128)S(1)}, f32[2,2,512,512]{3,2,1,0:T(8,128)S(1)}, u32[]{:S(2)}, u32[]{:S(2)}) collective-permute-start(f32[2,2,512,512]{3,2,1,0:T(8,128)S(1)} %shard_map.37.own), channel_id=1, source_target_pairs={{0,1},{1,0},{2,3},{3,2},{4,5},{5,4},{6,7},{7,6},{8,9},{9,8},{10,11... | collective-permute-start | bytes 12582920 | tf_op jit(solution)/shard_map/ppermute | solution.py:21
  104.1 17.7 %collective-permute-start.15 = (f32[2,2,256,128]{3,2,1,0:T(8,128)S(1)}, f32[2,2,256,128]{3,2,1,0:T(8,128)S(1)}, u32[]{:S(2)}, u32[]{:S(2)}) collective-permute-start(f32[2,2,256,128]{3,2,1,0:T(8,128)S(1)} %copy-done), channel_id=1, source_target_pairs={{0,48},{16,0},{32,16},{48,32},{1,49},{17,1},{33,17},{49,33},{2,50}... | collective-permute-start | bytes 1572872 | tf_op jit(solution)/shard_map/ppermute | solution.py:21
  104.2 17.7 %collective-permute-start.16 = (f32[2,2,256,128]{3,2,1,0:T(8,128)S(1)}, f32[2,2,256,128]{3,2,1,0:T(8,128)S(1)}, u32[]{:S(2)}, u32[]{:S(2)}) collective-permute-start(f32[2,2,256,128]{3,2,1,0:T(8,128)S(1)} %copy-done), channel_id=1, source_target_pairs={{0,16},{16,32},{32,48},{48,0},{1,17},{17,33},{33,49},{49,1},{2,18}... | collective-permute-start | bytes 1572872 | tf_op jit(solution)/shard_map/ppermute | solution.py:21
  119.7 8.4 %collective-permute-start.20 = (f32[2,256,128]{2,1,0:T(8,128)S(1)}, f32[2,256,128]{2,1,0:T(8,128)S(1)}, u32[]{:S(2)}, u32[]{:S(2)}) collective-permute-start(f32[2,256,128]{2,1,0:T(8,128)S(1)} %get-tuple-element.94), channel_id=1, source_target_pairs={{0,2},{2,4},{4,6},{6,0},{1,3},{3,5},{5,7},{7,1},{8,10},{10,12},{12... | collective-permute-start | bytes 786440 | tf_op jit(solution)/shard_map/ppermute | solution.py:21
  120.0 9.4 %collective-permute-start.22 = (f32[2,256,128]{2,1,0:T(8,128)S(1)}, f32[2,256,128]{2,1,0:T(8,128)S(1)}, u32[]{:S(2)}, u32[]{:S(2)}) collective-permute-start(f32[2,256,128]{2,1,0:T(8,128)S(1)} %get-tuple-element.93), channel_id=1, source_target_pairs={{0,6},{2,0},{4,2},{6,4},{1,7},{3,1},{5,3},{7,5},{8,14},{10,8},{12,... | collective-permute-start | bytes 786440 | tf_op jit(solution)/shard_map/ppermute | solution.py:21
  121.8 17.8 %collective-permute-start.18 = (f32[2,2,256,128]{3,2,1,0:T(8,128)}, f32[2,2,256,128]{3,2,1,0:T(8,128)S(1)}, u32[]{:S(2)}, u32[]{:S(2)}) collective-permute-start(f32[2,2,256,128]{3,2,1,0:T(8,128)} %collective-permute-done.13.refs_2_), channel_id=1, source_target_pairs={{0,48},{16,0},{32,16},{48,32},{1,49},{17,1},{33,17},{49,33},{2,50}... | collective-permute-start | bytes 1572872 | tf_op jit(solution)/shard_map/ppermute | solution.py:21
  121.8 17.8 %collective-permute-start.19 = (f32[2,2,256,128]{3,2,1,0:T(8,128)S(1)}, f32[2,2,256,128]{3,2,1,0:T(8,128)S(1)}, u32[]{:S(2)}, u32[]{:S(2)}) collective-permute-start(f32[2,2,256,128]{3,2,1,0:T(8,128)S(1)} %collective-permute-done.16.refs_5_), channel_id=1, source_target_pairs={{0,16},{16,32},{32,48},{48,0},{1,17},{17,33},{33,49},{49,1},{2,18}... | collective-permute-start | bytes 1572872 | tf_op jit(solution)/shard_map/ppermute | solution.py:21
  129.5 14.2 %collective-permute-start.23 = (f32[2,2,256,128]{3,2,1,0:T(8,128)S(1)}, f32[2,2,256,128]{3,2,1,0:T(8,128)S(1)}, u32[]{:S(2)}, u32[]{:S(2)}) collective-permute-start(f32[2,2,256,128]{3,2,1,0:T(8,128)S(1)} %pad_maximum_fusion.3), channel_id=1, source_target_pairs={{0,6},{2,0},{4,2},{6,4},{1,7},{3,1},{5,3},{7,5},{8,14},{10,8},{12,... | collective-permute-start | bytes 1572872 | tf_op jit(solution)/shard_map/ppermute | solution.py:21
  130.1 15.5 %collective-permute-start.21 = (f32[2,2,256,128]{3,2,1,0:T(8,128)S(1)}, f32[2,2,256,128]{3,2,1,0:T(8,128)S(1)}, u32[]{:S(2)}, u32[]{:S(2)}) collective-permute-start(f32[2,2,256,128]{3,2,1,0:T(8,128)S(1)} %pad_maximum_fusion.2), channel_id=1, source_target_pairs={{0,2},{2,4},{4,6},{6,0},{1,3},{3,5},{5,7},{7,1},{8,10},{10,12},{12... | collective-permute-start | bytes 1572872 | tf_op jit(solution)/shard_map/ppermute | solution.py:21
  141.4 7.5 %collective-permute-start.26 = (f32[2,256,128]{2,1,0:T(8,128)S(1)}, f32[2,256,128]{2,1,0:T(8,128)S(1)}, u32[]{:S(2)}, u32[]{:S(2)}) collective-permute-start(f32[2,256,128]{2,1,0:T(8,128)S(1)} %get-tuple-element.85), channel_id=1, source_target_pairs={{0,2},{2,4},{4,6},{6,0},{1,3},{3,5},{5,7},{7,1},{8,10},{10,12},{12... | collective-permute-start | bytes 786440 | tf_op jit(solution)/shard_map/ppermute | solution.py:21
  141.5 8.1 %collective-permute-start.28 = (f32[2,256,128]{2,1,0:T(8,128)S(1)}, f32[2,256,128]{2,1,0:T(8,128)S(1)}, u32[]{:S(2)}, u32[]{:S(2)}) collective-permute-start(f32[2,256,128]{2,1,0:T(8,128)S(1)} %get-tuple-element.86), channel_id=1, source_target_pairs={{0,6},{2,0},{4,2},{6,4},{1,7},{3,1},{5,3},{7,5},{8,14},{10,8},{12,... | collective-permute-start | bytes 786440 | tf_op jit(solution)/shard_map/ppermute | solution.py:21
  149.7 13.6 %collective-permute-start.27 = (f32[2,2,256,128]{3,2,1,0:T(8,128)S(1)}, f32[2,2,256,128]{3,2,1,0:T(8,128)}, u32[]{:S(2)}, u32[]{:S(2)}) collective-permute-start(f32[2,2,256,128]{3,2,1,0:T(8,128)S(1)} %pad_maximum_fusion.4), channel_id=1, source_target_pairs={{0,2},{2,4},{4,6},{6,0},{1,3},{3,5},{5,7},{7,1},{8,10},{10,12},{12... | collective-permute-start | bytes 1572872 | tf_op jit(solution)/shard_map/ppermute | solution.py:21
  153.7 13.0 %collective-permute-start.29 = (f32[2,2,256,128]{3,2,1,0:T(8,128)}, f32[2,2,256,128]{3,2,1,0:T(8,128)}, u32[]{:S(2)}, u32[]{:S(2)}) collective-permute-start(f32[2,2,256,128]{3,2,1,0:T(8,128)} %pad_maximum_fusion.5), channel_id=1, source_target_pairs={{0,6},{2,0},{4,2},{6,4},{1,7},{3,1},{5,3},{7,5},{8,14},{10,8},{12,... | collective-permute-start | bytes 1572872 | tf_op jit(solution)/shard_map/ppermute | solution.py:21
  154.5 6.6 %collective-permute-start.24 = (f32[2,256,128]{2,1,0:T(8,128)}, f32[2,256,128]{2,1,0:T(8,128)S(1)}, u32[]{:S(2)}, u32[]{:S(2)}) collective-permute-start(f32[2,256,128]{2,1,0:T(8,128)} %slice_bitcast_fusion.6), channel_id=1, source_target_pairs={{0,72},{72,0},{8,64},{64,8},{1,73},{73,1},{9,65},{65,9},{2,74},{74... | collective-permute-start | bytes 786440 | tf_op jit(solution)/shard_map/ppermute | solution.py:183
  161.1 12.4 %collective-permute-start.25 = (f32[2,256,128]{2,1,0:T(8,128)S(1)}, f32[2,256,128]{2,1,0:T(8,128)S(1)}, u32[]{:S(2)}, u32[]{:S(2)}) collective-permute-start(f32[2,256,128]{2,1,0:T(8,128)S(1)} %fusion.6), channel_id=1, source_target_pairs={{0,8},{72,64},{8,0},{64,72},{1,9},{73,65},{9,1},{65,73},{2,10},{74... | collective-permute-start | bytes 786440 | tf_op jit(solution)/shard_map/ppermute | solution.py:184
  168.0 8.1 %collective-permute-start.31 = (f32[2,256,128]{2,1,0:T(8,128)S(1)}, f32[2,256,128]{2,1,0:T(8,128)S(1)}, u32[]{:S(2)}, u32[]{:S(2)}) collective-permute-start(f32[2,256,128]{2,1,0:T(8,128)S(1)} %fusion.7), channel_id=1, source_target_pairs={{0,64},{8,0},{64,72},{72,8},{1,65},{9,1},{65,73},{73,9},{2,66},{10... | collective-permute-start | bytes 786440 | tf_op jit(solution)/shard_map/ppermute | solution.py:177
  168.2 12.7 %collective-permute-start.30 = (f32[2,256,128]{2,1,0:T(8,128)S(1)}, f32[2,256,128]{2,1,0:T(8,128)S(1)}, u32[]{:S(2)}, u32[]{:S(2)}) collective-permute-start(f32[2,256,128]{2,1,0:T(8,128)S(1)} %slice_bitcast_fusion.2), channel_id=1, source_target_pairs={{8,64},{64,8},{9,65},{65,9},{10,66},{66,10},{11,67},{67,11},{12,68... | collective-permute-start | bytes 786440 | tf_op jit(solution)/shard_map/ppermute | solution.py:176
  (15 other events, 225.6 us)
Sparse Core Ops, SparseCore 0:
  9.5 75.7 all-gather.2

commit v6 on v5

--- a/solution.py
+++ b/solution.py
@@ -171,13 +171,6 @@
     return [up, down]
 
 
-def to_place(mine, far, same):
-    axes = ("zh", "zl")
-    near = lax.ppermute(far, axes, [(1, 2), (2, 1)])
-    got = lax.ppermute(jnp.where(same, far, mine), axes, [(0, 2), (1, 0), (2, 3), (3, 1)])
-    return jnp.where(same, mine, near) + got
-
-
 def round_ring(mine, far, same):
     axes = ("zh", "zl")
     across = lax.ppermute(far, axes, [(0, 3), (3, 0), (1, 2), (2, 1)])
@@ -235,7 +228,7 @@
     parts_1, *came_0 = tie((parts_1, *came_0))
     result_0 = round_ring(*(parts_0[0] + came_0[0] + came_0[1]), zl == zh)
     came_1 = second_step(parts_1, came_1)
-    results = [result_0, to_place(*(parts_1[0] + came_1[0] + came_1[1]), zl == zh)]
+    results = [result_0, round_ring(*(parts_1[0] + came_1[0] + came_1[1]), zl == zh)]
     return jnp.concatenate(results, axis=2)
 
 

time: 189 us -> 190 us (level); the launches traced: 189 us -> 187 us
  waiting for transfers between devices: 78.3 us -> 80.7 us
  other arithmetic: 4.45 us -> 2.46 us
    ppermute x2 -> x0, waiting for transfers between devices: 7.38 us -> none  [the longest x1 4.87 us: to_place(): near = lax.ppermute(far, axes, [(1, 2), (2, 1)])]
    ppermute x28, waiting for transfers between devices: 65.5 us -> 72.8 us  [move(): return lax.ppermute(value, axis, [(i, (i + step) % n) for i in range(n)])]
    ppermute x2 -> x0, starting transfers between devices: 5.48 us -> none  [the longest x1 5.3 us: to_place(): near = lax.ppermute(far, axes, [(1, 2), (2, 1)])]
    ppermute x1 -> x2, waiting for transfers between devices: 0.01 us -> 5.09 us  [round_ring(): lax.ppermute(jnp.where(same, across, mine), axes, [(0, 1), (3, 2), (1, 0)...]
    ppermute x1 -> x2, waiting for transfers between devices: 4.77 us -> 2.14 us  [round_ring(): across = lax.ppermute(far, axes, [(0, 3), (3, 0), (1, 2), (2, 1)])]
    ppermute x1 -> x2, starting transfers between devices: 2.19 us -> 4.57 us  [round_ring(): lax.ppermute(jnp.where(same, across, mine), axes, [(0, 1), (3, 2), (1, 0)...]
    ppermute x1 -> x2, starting transfers between devices: 1.81 us -> 3.78 us  [round_ring(): across = lax.ppermute(far, axes, [(0, 3), (3, 0), (1, 2), (2, 1)])]
  transfers between devices with their start and end apart: 33 -> 33, of which waited for: 16 -> 17; matrix products, arithmetic and copies ran while one was open for 6% -> 4% of each run, Pallas kernels for 16% -> 16%
where the time goes in v6:
time: 190 us; the launch traced here: 187 us
  waiting for transfers between devices  80.7 us (42%)
  starting transfers between devices  49 us (26%)
  Pallas kernels  30.4 us (16%)
  between operations  13.8 us (7%)
  local copies, waits for them, and re-layouts  11 us (6%)
  other arithmetic  2.46 us (1%)
    ppermute x28, waiting for transfers between devices, move(): return lax.ppermute(value, axis, [(i, (i + step) % n) for i in range(n)])  72.8 us
    ppermute x28, starting transfers between devices, move(): return lax.ppermute(value, axis, [(i, (i + step) % n) for i in range(n)])  40.6 us
    pallas_call x3, Pallas kernels, update_partial(): pl.pallas_call(kernel, out_shape=out, in_specs=whole(len(operands)), out_...  16.6 us
    pallas_call x1, Pallas kernels, mixed_partial(): pl.pallas_call(mixed_kernel, grid=(levels, 2), out_shape=out, in_specs=wh...  13.8 us
    ppermute x2, waiting for transfers between devices, round_ring(): lax.ppermute(jnp.where(same, across, mine), axes, [(0, 1), (3, 2), (1, 0)...  5.09 us
    ppermute x2, starting transfers between devices, round_ring(): lax.ppermute(jnp.where(same, across, mine), axes, [(0, 1), (3, 2), (1, 0)...  4.57 us
    unnamed x28, local copies, waits for them, and re-layouts  4.53 us
  transfers between devices with their start and end apart: 33, of which 17 were waited for; matrix products, arithmetic and copies ran while one was open for 4% of the time, Pallas kernels for 16%

profile of v6, /device:TPU:62, one launch (start us, length us, event | category | flops | bytes accessed | tf_op | source)
XLA Modules:
  0.0 187.3 jit_solution(8704033281872048627)
XLA Ops:
  12.7 2.4 %collective-permute-start.5 = (f32[2,2,256,128]{3,2,1,0:T(8,128)S(1)}, f32[2,2,256,128]{3,2,1,0:T(8,128)S(1)}, u32[]{:S(2)}, u32[]{:S(2)}) collective-permute-start(f32[2,2,256,128]{3,2,1,0:T(8,128)S(1)} %get-tuple-element.96.refs_0_), channel_id=1, source_target_pairs={{0,16},{16,32},{32,48},{48,0},{1,17},{17,33},{33,49},{49,1},{2,18}... | collective-permute-start | bytes 1572872 | tf_op jit(solution)/shard_map/ppermute | solution.py:21
  16.2 3.1 %collective-permute-start.1 = (f32[2,128,512]{2,1,0:T(8,128)S(1)}, f32[2,128,512]{2,1,0:T(8,128)S(1)}, u32[]{:S(2)}, u32[]{:S(2)}) collective-permute-start(f32[2,128,512]{2,1,0:T(8,128)S(1)} %pad_maximum_fusion.1), channel_id=1, source_target_pairs={{0,64},{64,0},{1,65},{65,1},{2,66},{66,2},{3,67},{67,3},{4,68},{68... | collective-permute-start | bytes 1572872 | tf_op jit(solution)/shard_map/ppermute | solution.py:21
  19.2 2.1 %fusion.8 = (f32[2,2,256,128]{3,2,1,0:T(8,128)}, f32[2,2,256,128]{3,2,1,0:T(8,128)S(1)}) fusion(f32[2,2,256,256]{3,2,1,0:T(8,128)} %collective-permute-done.3), kind=kLoop, calls=%fused_computation.42 | loop fusion | bytes 2097152 | tf_op jit(solution)/shard_map/slice | solution.py:193
  21.4 3.2 %collective-permute-start.6 = (f32[2,2,256,128]{3,2,1,0:T(8,128)S(1)}, f32[2,2,256,128]{3,2,1,0:T(8,128)}, u32[]{:S(2)}, u32[]{:S(2)}) collective-permute-start(f32[2,2,256,128]{3,2,1,0:T(8,128)S(1)} %get-tuple-element.98.refs_1_), channel_id=1, source_target_pairs={{0,16},{16,32},{32,48},{48,0},{1,17},{17,33},{33,49},{49,1},{2,18}... | collective-permute-start | bytes 1572872 | tf_op jit(solution)/shard_map/ppermute | solution.py:21
  24.6 3.4 %collective-permute-done.2.refs_2_ = f32[2,2,256,128]{3,2,1,0:T(8,128)} collective-permute-done((f32[2,2,256,128]{3,2,1,0:T(8,128)S(1)}, f32[2,2,256,128]{3,2,1,0:T(8,128)}, u32[]{:S(2)}, u32[]{:S(2)}) %collective-permute-start.2) | collective-permute-done | bytes 524320 | tf_op jit(solution)/shard_map/ppermute | solution.py:21
  28.0 10.4 %collective-permute-done.1 = f32[2,128,512]{2,1,0:T(8,128)S(1)} collective-permute-done((f32[2,128,512]{2,1,0:T(8,128)S(1)}, f32[2,128,512]{2,1,0:T(8,128)S(1)}, u32[]{:S(2)}, u32[]{:S(2)}) %collective-permute-start.1) | collective-permute-done | bytes 524320 | tf_op jit(solution)/shard_map/ppermute | solution.py:21
  39.4 3.2 %collective-permute-start.8 = (f32[2,2,128,512]{3,2,1,0:T(8,128)S(1)}, f32[2,2,128,512]{3,2,1,0:T(8,128)S(1)}, u32[]{:S(2)}, u32[]{:S(2)}) collective-permute-start(f32[2,2,128,512]{3,2,1,0:T(8,128)S(1)} %pad_maximum_fusion.e_0), channel_id=1, source_target_pairs={{0,16},{16,32},{32,48},{48,0},{1,17},{17,33},{33,49},{49,1},{2,18}... | collective-permute-start | bytes 3145736 | tf_op jit(solution)/shard_map/ppermute | solution.py:21
  42.7 22.1 %collective-permute-done.7.e_1 = f32[2,2,128,512]{3,2,1,0:T(8,128)S(1)} collective-permute-done((f32[2,2,128,512]{3,2,1,0:T(8,128)S(1)}, f32[2,2,128,512]{3,2,1,0:T(8,128)S(1)}, u32[]{:S(2)}, u32[]{:S(2)}) %collective-permute-start.7) | collective-permute-done | bytes 1048608 | tf_op jit(solution)/shard_map/ppermute | solution.py:21
  64.8 3.0 %collective-permute-start.10 = (f32[2,128,512]{2,1,0:T(8,128)S(1)}, f32[2,128,512]{2,1,0:T(8,128)S(1)}, u32[]{:S(2)}, u32[]{:S(2)}) collective-permute-start(f32[2,128,512]{2,1,0:T(8,128)S(1)} %slice_bitcast_fusion), channel_id=1, source_target_pairs={{0,16},{16,32},{32,48},{48,0},{1,17},{17,33},{33,49},{49,1},{2,18}... | collective-permute-start | bytes 1572872 | tf_op jit(solution)/shard_map/ppermute | solution.py:21
  68.0 3.2 %collective-permute-start.12 = (f32[2,2,256,128]{3,2,1,0:T(8,128)}, f32[2,2,256,128]{3,2,1,0:T(8,128)}, u32[]{:S(2)}, u32[]{:S(2)}) collective-permute-start(f32[2,2,256,128]{3,2,1,0:T(8,128)} %collective-permute-done.6.refs_7_), channel_id=1, source_target_pairs={{0,16},{16,32},{32,48},{48,0},{1,17},{17,33},{33,49},{49,1},{2,18}... | collective-permute-start | bytes 1572872 | tf_op jit(solution)/shard_map/ppermute | solution.py:21
  71.3 8.9 %collective-permute-done.10.e_2high = f32[2,128,512]{2,1,0:T(8,128)S(1)} collective-permute-done((f32[2,128,512]{2,1,0:T(8,128)S(1)}, f32[2,128,512]{2,1,0:T(8,128)S(1)}, u32[]{:S(2)}, u32[]{:S(2)}) %collective-permute-start.10) | collective-permute-done | bytes 524320 | tf_op jit(solution)/shard_map/ppermute | solution.py:21
  81.0 3.0 %collective-permute-done.9.e_2low = f32[2,128,512]{2,1,0:T(8,128)S(1)} collective-permute-done((f32[2,128,512]{2,1,0:T(8,128)S(1)}, f32[2,128,512]{2,1,0:T(8,128)S(1)}, u32[]{:S(2)}, u32[]{:S(2)}) %collective-permute-start.9) | collective-permute-done | bytes 524320 | tf_op jit(solution)/shard_map/ppermute | solution.py:21
  84.8 3.2 %collective-permute-start.14 = (f32[2,2,256,128]{3,2,1,0:T(8,128)}, f32[2,2,256,128]{3,2,1,0:T(8,128)}, u32[]{:S(2)}, u32[]{:S(2)}) collective-permute-start(f32[2,2,256,128]{3,2,1,0:T(8,128)} %get-tuple-element.72.refs_0_), channel_id=1, source_target_pairs={{0,16},{16,32},{32,48},{48,0},{1,17},{17,33},{33,49},{49,1},{2,18}... | collective-permute-start | bytes 1572872 | tf_op jit(solution)/shard_map/ppermute | solution.py:21
  90.2 13.8 %shard_map.37.own = f32[2,2,512,512]{3,2,1,0:T(8,128)S(1)} custom-call(f32[2,2,128,512]{3,2,1,0:T(8,128)S(1)} %pad_maximum_fusion.e_0, f32[2,2,128,512]{3,2,1,0:T(8,128)S(1)} %collective-permute-done.7.e_1, f32[2,2,128,512]{3,2,1,0:T(8,128)S(1)} %collective-permute-done.8.e_3, f32[2,128,512]{2,1,0:T(8,128)S(1)} %copy-done.12, f32[2,128,512]{2,1,0:T(8,128)S(1)} %copy-done.10, ...), custom_call_target="tpu_custom_call" | custom-call | flops 193273536 | bytes 12582912 | tf_op jit(solution)/shard_map/pallas_call | solution.py:128
  104.2 3.2 %collective-permute-start.16 = (f32[2,2,256,128]{3,2,1,0:T(8,128)S(1)}, f32[2,2,256,128]{3,2,1,0:T(8,128)S(1)}, u32[]{:S(2)}, u32[]{:S(2)}) collective-permute-start(f32[2,2,256,128]{3,2,1,0:T(8,128)S(1)} %copy-done), channel_id=1, source_target_pairs={{0,16},{16,32},{32,48},{48,0},{1,17},{17,33},{33,49},{49,1},{2,18}... | collective-permute-start | bytes 1572872 | tf_op jit(solution)/shard_map/ppermute | solution.py:21
  107.4 3.8 %collective-permute-done.17.other = f32[2,2,512,512]{3,2,1,0:T(8,128)S(1)} collective-permute-done((f32[2,2,512,512]{3,2,1,0:T(8,128)S(1)}, f32[2,2,512,512]{3,2,1,0:T(8,128)S(1)}, u32[]{:S(2)}, u32[]{:S(2)}) %collective-permute-start.17) | collective-permute-done | bytes 4194336 | tf_op jit(solution)/shard_map/ppermute | solution.py:21
  111.2 8.4 %shard_map.38 = (f32[4,2,2,256,128]{4,3,2,1,0:T(8,128)S(1)}, bf16[2,2,512,512]{3,2,1,0:T(8,128)(2,1)S(1)}, bf16[2,2,512,512]{3,2,1,0:T(8,128)(2,1)S(1)}) custom-call(f32[2,2,512,512]{3,2,1,0:T(8,128)S(1)} %shard_map.37.own, f32[2,2,512,512]{3,2,1,0:T(8,128)S(1)} %collective-permute-done.17.other, f32[2,2,256,128]{3,2,1,0:T(8,128)S(1)} %copy-done.2, ...), custom_call_target="tpu_custom_call" | custom-call | flops 128849016 | bytes 18874368 | tf_op jit(solution)/shard_map/pallas_call | solution.py:148
  121.8 3.2 %collective-permute-start.19 = (f32[2,2,256,128]{3,2,1,0:T(8,128)S(1)}, f32[2,2,256,128]{3,2,1,0:T(8,128)S(1)}, u32[]{:S(2)}, u32[]{:S(2)}) collective-permute-start(f32[2,2,256,128]{3,2,1,0:T(8,128)S(1)} %collective-permute-done.16.refs_5_), channel_id=1, source_target_pairs={{0,16},{16,32},{32,48},{48,0},{1,17},{17,33},{33,49},{49,1},{2,18}... | collective-permute-start | bytes 1572872 | tf_op jit(solution)/shard_map/ppermute | solution.py:21
  125.1 3.0 %collective-permute-done.20 = f32[2,256,128]{2,1,0:T(8,128)S(1)} collective-permute-done((f32[2,256,128]{2,1,0:T(8,128)S(1)}, f32[2,256,128]{2,1,0:T(8,128)S(1)}, u32[]{:S(2)}, u32[]{:S(2)}) %collective-permute-start.20) | collective-permute-done | bytes 262176 | tf_op jit(solution)/shard_map/ppermute | solution.py:21
  130.1 3.1 %collective-permute-start.21 = (f32[2,2,256,128]{3,2,1,0:T(8,128)S(1)}, f32[2,2,256,128]{3,2,1,0:T(8,128)S(1)}, u32[]{:S(2)}, u32[]{:S(2)}) collective-permute-start(f32[2,2,256,128]{3,2,1,0:T(8,128)S(1)} %pad_maximum_fusion.2), channel_id=1, source_target_pairs={{0,2},{2,4},{4,6},{6,0},{1,3},{3,5},{5,7},{7,1},{8,10},{10,12},{12... | collective-permute-start | bytes 1572872 | tf_op jit(solution)/shard_map/ppermute | solution.py:21
  133.2 6.4 %shard_map.39.so_far = f32[4,2,2,256,128]{4,3,2,1,0:T(8,128)S(1)} custom-call(bf16[2,2,512,512]{3,2,1,0:T(8,128)(2,1)S(1)} %get-tuple-element.70.m_hi, bf16[2,2,512,512]{3,2,1,0:T(8,128)(2,1)S(1)} %get-tuple-element.71.m_lo, f32[2,2,256,128]{3,2,1,0:T(8,128)} %get-tuple-element.72.refs_0_, f32[2,2,256,128]{3,2,1,0:T(8,128)S(1)} %copy-done, ...), custom_call_target="tpu_custom_call" | custom-call | flops 96636768 | bytes 9437184 | tf_op jit(solution)/shard_map/pallas_call | solution.py:148
  141.5 2.0 %collective-permute-start.28 = (f32[2,256,128]{2,1,0:T(8,128)S(1)}, f32[2,256,128]{2,1,0:T(8,128)S(1)}, u32[]{:S(2)}, u32[]{:S(2)}) collective-permute-start(f32[2,256,128]{2,1,0:T(8,128)S(1)} %get-tuple-element.86), channel_id=1, source_target_pairs={{0,6},{2,0},{4,2},{6,4},{1,7},{3,1},{5,3},{7,5},{8,14},{10,8},{12,... | collective-permute-start | bytes 786440 | tf_op jit(solution)/shard_map/ppermute | solution.py:21
  145.6 3.4 %collective-permute-done.26 = f32[2,256,128]{2,1,0:T(8,128)S(1)} collective-permute-done((f32[2,256,128]{2,1,0:T(8,128)S(1)}, f32[2,256,128]{2,1,0:T(8,128)S(1)}, u32[]{:S(2)}, u32[]{:S(2)}) %collective-permute-start.26) | collective-permute-done | bytes 262176 | tf_op jit(solution)/shard_map/ppermute | solution.py:21
  149.7 3.1 %collective-permute-start.27 = (f32[2,2,256,128]{3,2,1,0:T(8,128)S(1)}, f32[2,2,256,128]{3,2,1,0:T(8,128)S(1)}, u32[]{:S(2)}, u32[]{:S(2)}) collective-permute-start(f32[2,2,256,128]{3,2,1,0:T(8,128)S(1)} %pad_maximum_fusion.4), channel_id=1, source_target_pairs={{0,2},{2,4},{4,6},{6,0},{1,3},{3,5},{5,7},{7,1},{8,10},{10,12},{12... | collective-permute-start | bytes 1572872 | tf_op jit(solution)/shard_map/ppermute | solution.py:21
  153.1 1.9 %collective-permute-start.24 = (f32[2,256,128]{2,1,0:T(8,128)S(1)}, f32[2,256,128]{2,1,0:T(8,128)S(1)}, u32[]{:S(2)}, u32[]{:S(2)}) collective-permute-start(f32[2,256,128]{2,1,0:T(8,128)S(1)} %slice_bitcast_fusion.6), channel_id=1, source_target_pairs={{0,72},{72,0},{8,64},{64,8},{1,73},{73,1},{9,65},{65,9},{2,74},{74... | collective-permute-start | bytes 786440 | tf_op jit(solution)/shard_map/ppermute | solution.py:176
  155.0 7.2 %collective-permute-done.27 = f32[2,2,256,128]{3,2,1,0:T(8,128)S(1)} collective-permute-done((f32[2,2,256,128]{3,2,1,0:T(8,128)S(1)}, f32[2,2,256,128]{3,2,1,0:T(8,128)S(1)}, u32[]{:S(2)}, u32[]{:S(2)}) %collective-permute-start.27) | collective-permute-done | bytes 524320 | tf_op jit(solution)/shard_map/ppermute | solution.py:21
  162.1 3.5 %collective-permute-done.29 = f32[2,2,256,128]{3,2,1,0:T(8,128)S(1)} collective-permute-done((f32[2,2,256,128]{3,2,1,0:T(8,128)S(1)}, f32[2,2,256,128]{3,2,1,0:T(8,128)S(1)}, u32[]{:S(2)}, u32[]{:S(2)}) %collective-permute-start.29) | collective-permute-done | bytes 524320 | tf_op jit(solution)/shard_map/ppermute | solution.py:21
  167.7 2.4 %collective-permute-start.25 = (f32[2,256,128]{2,1,0:T(8,128)S(1)}, f32[2,256,128]{2,1,0:T(8,128)S(1)}, u32[]{:S(2)}, u32[]{:S(2)}) collective-permute-start(f32[2,256,128]{2,1,0:T(8,128)S(1)} %fusion.6), channel_id=1, source_target_pairs={{0,8},{72,64},{8,0},{64,72},{1,9},{73,65},{9,1},{65,73},{2,10},{74... | collective-permute-start | bytes 786440 | tf_op jit(solution)/shard_map/ppermute | solution.py:177
  170.1 2.1 %collective-permute-done.30 = f32[2,256,128]{2,1,0:T(8,128)S(1)} collective-permute-done((f32[2,256,128]{2,1,0:T(8,128)S(1)}, f32[2,256,128]{2,1,0:T(8,128)S(1)}, u32[]{:S(2)}, u32[]{:S(2)}) %collective-permute-start.30) | collective-permute-done | bytes 262176 | tf_op jit(solution)/shard_map/ppermute | solution.py:176
  172.2 2.2 %collective-permute-start.31 = (f32[2,256,128]{2,1,0:T(8,128)S(1)}, f32[2,256,128]{2,1,0:T(8,128)S(1)}, u32[]{:S(2)}, u32[]{:S(2)}) collective-permute-start(f32[2,256,128]{2,1,0:T(8,128)S(1)} %fusion.7), channel_id=1, source_target_pairs={{0,8},{72,64},{8,0},{64,72},{1,9},{73,65},{9,1},{65,73},{2,10},{74... | collective-permute-start | bytes 786440 | tf_op jit(solution)/shard_map/ppermute | solution.py:177
  174.4 2.3 %collective-permute-done.25 = f32[2,256,128]{2,1,0:T(8,128)S(1)} collective-permute-done((f32[2,256,128]{2,1,0:T(8,128)S(1)}, f32[2,256,128]{2,1,0:T(8,128)S(1)}, u32[]{:S(2)}, u32[]{:S(2)}) %collective-permute-start.25) | collective-permute-done | bytes 262176 | tf_op jit(solution)/shard_map/ppermute | solution.py:177
  176.8 2.8 %collective-permute-done.31 = f32[2,256,128]{2,1,0:T(8,128)S(1)} collective-permute-done((f32[2,256,128]{2,1,0:T(8,128)S(1)}, f32[2,256,128]{2,1,0:T(8,128)S(1)}, u32[]{:S(2)}, u32[]{:S(2)}) %collective-permute-start.31) | collective-permute-done | bytes 262176 | tf_op jit(solution)/shard_map/ppermute | solution.py:177
  (94 shorter events, 24.2 us)
Async XLA Ops:
  6.5 81.5 %all-gather.3.cloned.1.call-start = ((), (), s32[]{:S(2)}) async-start(), calls=%async_computation | async-start | bytes 8912896 | tf_op jit(solution)/shard_map/all_gather | solution.py:185
  8.6 10.6 %collective-permute-start.3 = (f32[2,2,256,256]{3,2,1,0:T(8,128)S(1)}, f32[2,2,256,256]{3,2,1,0:T(8,128)}, u32[]{:S(2)}, u32[]{:S(2)}) collective-permute-start(f32[2,2,256,256]{3,2,1,0:T(8,128)S(1)} %constant_dynamic-slice_fusion.1), channel_id=1, source_target_pairs={{0,1},{1,0},{2,3},{3,2},{4,5},{5,4},{6,7},{7,6},{8,9},{9,8},{10,11... | collective-permute-start | bytes 3145736 | tf_op jit(solution)/shard_map/ppermute | solution.py:21
  11.9 16.1 %collective-permute-start.2 = (f32[2,2,256,128]{3,2,1,0:T(8,128)S(1)}, f32[2,2,256,128]{3,2,1,0:T(8,128)}, u32[]{:S(2)}, u32[]{:S(2)}) collective-permute-start(f32[2,2,256,128]{3,2,1,0:T(8,128)S(1)} %get-tuple-element.96.refs_0_), channel_id=1, source_target_pairs={{0,48},{16,0},{32,16},{48,32},{1,49},{17,1},{33,17},{49,33},{2,50}... | collective-permute-start | bytes 1572872 | tf_op jit(solution)/shard_map/ppermute | solution.py:21
  12.7 15.3 %collective-permute-start.5 = (f32[2,2,256,128]{3,2,1,0:T(8,128)S(1)}, f32[2,2,256,128]{3,2,1,0:T(8,128)S(1)}, u32[]{:S(2)}, u32[]{:S(2)}) collective-permute-start(f32[2,2,256,128]{3,2,1,0:T(8,128)S(1)} %get-tuple-element.96.refs_0_), channel_id=1, source_target_pairs={{0,16},{16,32},{32,48},{48,0},{1,17},{17,33},{33,49},{49,1},{2,18}... | collective-permute-start | bytes 1572872 | tf_op jit(solution)/shard_map/ppermute | solution.py:21
  16.2 22.3 %collective-permute-start.1 = (f32[2,128,512]{2,1,0:T(8,128)S(1)}, f32[2,128,512]{2,1,0:T(8,128)S(1)}, u32[]{:S(2)}, u32[]{:S(2)}) collective-permute-start(f32[2,128,512]{2,1,0:T(8,128)S(1)} %pad_maximum_fusion.1), channel_id=1, source_target_pairs={{0,64},{64,0},{1,65},{65,1},{2,66},{66,2},{3,67},{67,3},{4,68},{68... | collective-permute-start | bytes 1572872 | tf_op jit(solution)/shard_map/ppermute | solution.py:21
  21.4 17.1 %collective-permute-start.4 = (f32[2,2,256,128]{3,2,1,0:T(8,128)S(1)}, f32[2,2,256,128]{3,2,1,0:T(8,128)S(1)}, u32[]{:S(2)}, u32[]{:S(2)}) collective-permute-start(f32[2,2,256,128]{3,2,1,0:T(8,128)S(1)} %get-tuple-element.98.refs_1_), channel_id=1, source_target_pairs={{0,48},{16,0},{32,16},{48,32},{1,49},{17,1},{33,17},{49,33},{2,50}... | collective-permute-start | bytes 1572872 | tf_op jit(solution)/shard_map/ppermute | solution.py:21
  21.4 17.9 %collective-permute-start.6 = (f32[2,2,256,128]{3,2,1,0:T(8,128)S(1)}, f32[2,2,256,128]{3,2,1,0:T(8,128)}, u32[]{:S(2)}, u32[]{:S(2)}) collective-permute-start(f32[2,2,256,128]{3,2,1,0:T(8,128)S(1)} %get-tuple-element.98.refs_1_), channel_id=1, source_target_pairs={{0,16},{16,32},{32,48},{48,0},{1,17},{17,33},{33,49},{49,1},{2,18}... | collective-permute-start | bytes 1572872 | tf_op jit(solution)/shard_map/ppermute | solution.py:21
  39.4 25.4 %collective-permute-start.7 = (f32[2,2,128,512]{3,2,1,0:T(8,128)S(1)}, f32[2,2,128,512]{3,2,1,0:T(8,128)S(1)}, u32[]{:S(2)}, u32[]{:S(2)}) collective-permute-start(f32[2,2,128,512]{3,2,1,0:T(8,128)S(1)} %pad_maximum_fusion.e_0), channel_id=1, source_target_pairs={{0,48},{16,0},{32,16},{48,32},{1,49},{17,1},{33,17},{49,33},{2,50}... | collective-permute-start | bytes 3145736 | tf_op jit(solution)/shard_map/ppermute | solution.py:21
  39.4 25.3 %collective-permute-start.8 = (f32[2,2,128,512]{3,2,1,0:T(8,128)S(1)}, f32[2,2,128,512]{3,2,1,0:T(8,128)S(1)}, u32[]{:S(2)}, u32[]{:S(2)}) collective-permute-start(f32[2,2,128,512]{3,2,1,0:T(8,128)S(1)} %pad_maximum_fusion.e_0), channel_id=1, source_target_pairs={{0,16},{16,32},{32,48},{48,0},{1,17},{17,33},{33,49},{49,1},{2,18}... | collective-permute-start | bytes 3145736 | tf_op jit(solution)/shard_map/ppermute | solution.py:21
  64.8 15.4 %collective-permute-start.10 = (f32[2,128,512]{2,1,0:T(8,128)S(1)}, f32[2,128,512]{2,1,0:T(8,128)S(1)}, u32[]{:S(2)}, u32[]{:S(2)}) collective-permute-start(f32[2,128,512]{2,1,0:T(8,128)S(1)} %slice_bitcast_fusion), channel_id=1, source_target_pairs={{0,16},{16,32},{32,48},{48,0},{1,17},{17,33},{33,49},{49,1},{2,18}... | collective-permute-start | bytes 1572872 | tf_op jit(solution)/shard_map/ppermute | solution.py:21
  67.9 16.1 %collective-permute-start.9 = (f32[2,128,512]{2,1,0:T(8,128)S(1)}, f32[2,128,512]{2,1,0:T(8,128)S(1)}, u32[]{:S(2)}, u32[]{:S(2)}) collective-permute-start(f32[2,128,512]{2,1,0:T(8,128)S(1)} %slice_bitcast_fusion.1), channel_id=1, source_target_pairs={{0,48},{16,0},{32,16},{48,32},{1,49},{17,1},{33,17},{49,33},{2,50}... | collective-permute-start | bytes 1572872 | tf_op jit(solution)/shard_map/ppermute | solution.py:21
  68.0 36.0 %collective-permute-start.11 = (f32[2,2,256,128]{3,2,1,0:T(8,128)}, f32[2,2,256,128]{3,2,1,0:T(8,128)}, u32[]{:S(2)}, u32[]{:S(2)}) collective-permute-start(f32[2,2,256,128]{3,2,1,0:T(8,128)} %collective-permute-done.2.refs_2_), channel_id=1, source_target_pairs={{0,48},{16,0},{32,16},{48,32},{1,49},{17,1},{33,17},{49,33},{2,50}... | collective-permute-start | bytes 1572872 | tf_op jit(solution)/shard_map/ppermute | solution.py:21
  68.0 35.9 %collective-permute-start.12 = (f32[2,2,256,128]{3,2,1,0:T(8,128)}, f32[2,2,256,128]{3,2,1,0:T(8,128)}, u32[]{:S(2)}, u32[]{:S(2)}) collective-permute-start(f32[2,2,256,128]{3,2,1,0:T(8,128)} %collective-permute-done.6.refs_7_), channel_id=1, source_target_pairs={{0,16},{16,32},{32,48},{48,0},{1,17},{17,33},{33,49},{49,1},{2,18}... | collective-permute-start | bytes 1572872 | tf_op jit(solution)/shard_map/ppermute | solution.py:21
  84.8 19.1 %collective-permute-start.13 = (f32[2,2,256,128]{3,2,1,0:T(8,128)}, f32[2,2,256,128]{3,2,1,0:T(8,128)}, u32[]{:S(2)}, u32[]{:S(2)}) collective-permute-start(f32[2,2,256,128]{3,2,1,0:T(8,128)} %get-tuple-element.72.refs_0_), channel_id=1, source_target_pairs={{0,48},{16,0},{32,16},{48,32},{1,49},{17,1},{33,17},{49,33},{2,50}... | collective-permute-start | bytes 1572872 | tf_op jit(solution)/shard_map/ppermute | solution.py:21
  84.8 19.2 %collective-permute-start.14 = (f32[2,2,256,128]{3,2,1,0:T(8,128)}, f32[2,2,256,128]{3,2,1,0:T(8,128)}, u32[]{:S(2)}, u32[]{:S(2)}) collective-permute-start(f32[2,2,256,128]{3,2,1,0:T(8,128)} %get-tuple-element.72.refs_0_), channel_id=1, source_target_pairs={{0,16},{16,32},{32,48},{48,0},{1,17},{17,33},{33,49},{49,1},{2,18}... | collective-permute-start | bytes 1572872 | tf_op jit(solution)/shard_map/ppermute | solution.py:21
  104.0 7.2 %collective-permute-start.17 = (f32[2,2,512,512]{3,2,1,0:T(8,128)S(1)}, f32[2,2,512,512]{3,2,1,0:T(8,128)S(1)}, u32[]{:S(2)}, u32[]{:S(2)}) collective-permute-start(f32[2,2,512,512]{3,2,1,0:T(8,128)S(1)} %shard_map.37.own), channel_id=1, source_target_pairs={{0,1},{1,0},{2,3},{3,2},{4,5},{5,4},{6,7},{7,6},{8,9},{9,8},{10,11... | collective-permute-start | bytes 12582920 | tf_op jit(solution)/shard_map/ppermute | solution.py:21
  104.1 17.7 %collective-permute-start.15 = (f32[2,2,256,128]{3,2,1,0:T(8,128)S(1)}, f32[2,2,256,128]{3,2,1,0:T(8,128)S(1)}, u32[]{:S(2)}, u32[]{:S(2)}) collective-permute-start(f32[2,2,256,128]{3,2,1,0:T(8,128)S(1)} %copy-done), channel_id=1, source_target_pairs={{0,48},{16,0},{32,16},{48,32},{1,49},{17,1},{33,17},{49,33},{2,50}... | collective-permute-start | bytes 1572872 | tf_op jit(solution)/shard_map/ppermute | solution.py:21
  104.2 17.7 %collective-permute-start.16 = (f32[2,2,256,128]{3,2,1,0:T(8,128)S(1)}, f32[2,2,256,128]{3,2,1,0:T(8,128)S(1)}, u32[]{:S(2)}, u32[]{:S(2)}) collective-permute-start(f32[2,2,256,128]{3,2,1,0:T(8,128)S(1)} %copy-done), channel_id=1, source_target_pairs={{0,16},{16,32},{32,48},{48,0},{1,17},{17,33},{33,49},{49,1},{2,18}... | collective-permute-start | bytes 1572872 | tf_op jit(solution)/shard_map/ppermute | solution.py:21
  119.7 8.4 %collective-permute-start.20 = (f32[2,256,128]{2,1,0:T(8,128)S(1)}, f32[2,256,128]{2,1,0:T(8,128)S(1)}, u32[]{:S(2)}, u32[]{:S(2)}) collective-permute-start(f32[2,256,128]{2,1,0:T(8,128)S(1)} %get-tuple-element.94), channel_id=1, source_target_pairs={{0,2},{2,4},{4,6},{6,0},{1,3},{3,5},{5,7},{7,1},{8,10},{10,12},{12... | collective-permute-start | bytes 786440 | tf_op jit(solution)/shard_map/ppermute | solution.py:21
  120.0 9.4 %collective-permute-start.22 = (f32[2,256,128]{2,1,0:T(8,128)S(1)}, f32[2,256,128]{2,1,0:T(8,128)S(1)}, u32[]{:S(2)}, u32[]{:S(2)}) collective-permute-start(f32[2,256,128]{2,1,0:T(8,128)S(1)} %get-tuple-element.93), channel_id=1, source_target_pairs={{0,6},{2,0},{4,2},{6,4},{1,7},{3,1},{5,3},{7,5},{8,14},{10,8},{12,... | collective-permute-start | bytes 786440 | tf_op jit(solution)/shard_map/ppermute | solution.py:21
  121.8 17.8 %collective-permute-start.18 = (f32[2,2,256,128]{3,2,1,0:T(8,128)}, f32[2,2,256,128]{3,2,1,0:T(8,128)S(1)}, u32[]{:S(2)}, u32[]{:S(2)}) collective-permute-start(f32[2,2,256,128]{3,2,1,0:T(8,128)} %collective-permute-done.13.refs_2_), channel_id=1, source_target_pairs={{0,48},{16,0},{32,16},{48,32},{1,49},{17,1},{33,17},{49,33},{2,50}... | collective-permute-start | bytes 1572872 | tf_op jit(solution)/shard_map/ppermute | solution.py:21
  121.8 17.8 %collective-permute-start.19 = (f32[2,2,256,128]{3,2,1,0:T(8,128)S(1)}, f32[2,2,256,128]{3,2,1,0:T(8,128)S(1)}, u32[]{:S(2)}, u32[]{:S(2)}) collective-permute-start(f32[2,2,256,128]{3,2,1,0:T(8,128)S(1)} %collective-permute-done.16.refs_5_), channel_id=1, source_target_pairs={{0,16},{16,32},{32,48},{48,0},{1,17},{17,33},{33,49},{49,1},{2,18}... | collective-permute-start | bytes 1572872 | tf_op jit(solution)/shard_map/ppermute | solution.py:21
  129.5 14.2 %collective-permute-start.23 = (f32[2,2,256,128]{3,2,1,0:T(8,128)S(1)}, f32[2,2,256,128]{3,2,1,0:T(8,128)S(1)}, u32[]{:S(2)}, u32[]{:S(2)}) collective-permute-start(f32[2,2,256,128]{3,2,1,0:T(8,128)S(1)} %pad_maximum_fusion.3), channel_id=1, source_target_pairs={{0,6},{2,0},{4,2},{6,4},{1,7},{3,1},{5,3},{7,5},{8,14},{10,8},{12,... | collective-permute-start | bytes 1572872 | tf_op jit(solution)/shard_map/ppermute | solution.py:21
  130.1 15.5 %collective-permute-start.21 = (f32[2,2,256,128]{3,2,1,0:T(8,128)S(1)}, f32[2,2,256,128]{3,2,1,0:T(8,128)S(1)}, u32[]{:S(2)}, u32[]{:S(2)}) collective-permute-start(f32[2,2,256,128]{3,2,1,0:T(8,128)S(1)} %pad_maximum_fusion.2), channel_id=1, source_target_pairs={{0,2},{2,4},{4,6},{6,0},{1,3},{3,5},{5,7},{7,1},{8,10},{10,12},{12... | collective-permute-start | bytes 1572872 | tf_op jit(solution)/shard_map/ppermute | solution.py:21
  141.4 7.5 %collective-permute-start.26 = (f32[2,256,128]{2,1,0:T(8,128)S(1)}, f32[2,256,128]{2,1,0:T(8,128)S(1)}, u32[]{:S(2)}, u32[]{:S(2)}) collective-permute-start(f32[2,256,128]{2,1,0:T(8,128)S(1)} %get-tuple-element.85), channel_id=1, source_target_pairs={{0,2},{2,4},{4,6},{6,0},{1,3},{3,5},{5,7},{7,1},{8,10},{10,12},{12... | collective-permute-start | bytes 786440 | tf_op jit(solution)/shard_map/ppermute | solution.py:21
  141.5 8.1 %collective-permute-start.28 = (f32[2,256,128]{2,1,0:T(8,128)S(1)}, f32[2,256,128]{2,1,0:T(8,128)S(1)}, u32[]{:S(2)}, u32[]{:S(2)}) collective-permute-start(f32[2,256,128]{2,1,0:T(8,128)S(1)} %get-tuple-element.86), channel_id=1, source_target_pairs={{0,6},{2,0},{4,2},{6,4},{1,7},{3,1},{5,3},{7,5},{8,14},{10,8},{12,... | collective-permute-start | bytes 786440 | tf_op jit(solution)/shard_map/ppermute | solution.py:21
  149.7 12.4 %collective-permute-start.27 = (f32[2,2,256,128]{3,2,1,0:T(8,128)S(1)}, f32[2,2,256,128]{3,2,1,0:T(8,128)S(1)}, u32[]{:S(2)}, u32[]{:S(2)}) collective-permute-start(f32[2,2,256,128]{3,2,1,0:T(8,128)S(1)} %pad_maximum_fusion.4), channel_id=1, source_target_pairs={{0,2},{2,4},{4,6},{6,0},{1,3},{3,5},{5,7},{7,1},{8,10},{10,12},{12... | collective-permute-start | bytes 1572872 | tf_op jit(solution)/shard_map/ppermute | solution.py:21
  152.9 12.8 %collective-permute-start.29 = (f32[2,2,256,128]{3,2,1,0:T(8,128)S(1)}, f32[2,2,256,128]{3,2,1,0:T(8,128)S(1)}, u32[]{:S(2)}, u32[]{:S(2)}) collective-permute-start(f32[2,2,256,128]{3,2,1,0:T(8,128)S(1)} %pad_maximum_fusion.5), channel_id=1, source_target_pairs={{0,6},{2,0},{4,2},{6,4},{1,7},{3,1},{5,3},{7,5},{8,14},{10,8},{12,... | collective-permute-start | bytes 1572872 | tf_op jit(solution)/shard_map/ppermute | solution.py:21
  153.1 14.6 %collective-permute-start.24 = (f32[2,256,128]{2,1,0:T(8,128)S(1)}, f32[2,256,128]{2,1,0:T(8,128)S(1)}, u32[]{:S(2)}, u32[]{:S(2)}) collective-permute-start(f32[2,256,128]{2,1,0:T(8,128)S(1)} %slice_bitcast_fusion.6), channel_id=1, source_target_pairs={{0,72},{72,0},{8,64},{64,8},{1,73},{73,1},{9,65},{65,9},{2,74},{74... | collective-permute-start | bytes 786440 | tf_op jit(solution)/shard_map/ppermute | solution.py:176
  165.8 6.5 %collective-permute-start.30 = (f32[2,256,128]{2,1,0:T(8,128)S(1)}, f32[2,256,128]{2,1,0:T(8,128)S(1)}, u32[]{:S(2)}, u32[]{:S(2)}) collective-permute-start(f32[2,256,128]{2,1,0:T(8,128)S(1)} %slice_bitcast_fusion.2), channel_id=1, source_target_pairs={{0,72},{72,0},{8,64},{64,8},{1,73},{73,1},{9,65},{65,9},{2,74},{74... | collective-permute-start | bytes 786440 | tf_op jit(solution)/shard_map/ppermute | solution.py:176
  167.7 9.1 %collective-permute-start.25 = (f32[2,256,128]{2,1,0:T(8,128)S(1)}, f32[2,256,128]{2,1,0:T(8,128)S(1)}, u32[]{:S(2)}, u32[]{:S(2)}) collective-permute-start(f32[2,256,128]{2,1,0:T(8,128)S(1)} %fusion.6), channel_id=1, source_target_pairs={{0,8},{72,64},{8,0},{64,72},{1,9},{73,65},{9,1},{65,73},{2,10},{74... | collective-permute-start | bytes 786440 | tf_op jit(solution)/shard_map/ppermute | solution.py:177
  172.2 7.3 %collective-permute-start.31 = (f32[2,256,128]{2,1,0:T(8,128)S(1)}, f32[2,256,128]{2,1,0:T(8,128)S(1)}, u32[]{:S(2)}, u32[]{:S(2)}) collective-permute-start(f32[2,256,128]{2,1,0:T(8,128)S(1)} %fusion.7), channel_id=1, source_target_pairs={{0,8},{72,64},{8,0},{64,72},{1,9},{73,65},{9,1},{65,73},{2,10},{74... | collective-permute-start | bytes 786440 | tf_op jit(solution)/shard_map/ppermute | solution.py:177
  (15 other events, 225.6 us)
Sparse Core Ops, SparseCore 0:
  9.5 75.7 all-gather.2
